TPU v7x, 128 devices: a whole 4x4x4 slice. The times are simulated.
128 devices in a mesh: dp: 4 (over y), ctx: 32 (over z, x, core).
Axes of the slice: x: 4, y: 4, z: 4, core: 2. Of those that a mesh axis runs over, the one named last changes fastest.
Arguments:
- hidden_in: bfloat16 [4, 4096, 1024], P('dp', 'ctx'), may hold values from -6 to 6
- positions: int32 [4, 4096], P('dp', 'ctx'), may hold values from 0 to 8190, as said below
- block_of: int32 [64], replicated, may hold values from 0 to 63, as said below
- attn_gain: bfloat16 [1024], P('dp'), may hold values from 0.099609375 to 1.8984375
- query_weight: bfloat16 [1024, 1024], P('dp'), may hold values from -0.1875 to 0.1875
- key_weight: bfloat16 [1024, 512], P('dp'), may hold values from -0.1875 to 0.1875
- value_weight: bfloat16 [1024, 512], P('dp'), may hold values from -0.1875 to 0.1875
- out_weight: bfloat16 [1024, 1024], P('dp'), may hold values from -2 to 2
- query_gain: bfloat16 [64], P('dp'), may hold values from 0.099609375 to 1.8984375
- key_gain: bfloat16 [64], P('dp'), may hold values from 0.099609375 to 1.8984375
- ffn_gain: bfloat16 [1024], P('dp'), may hold values from 0.099609375 to 1.8984375
- gate_weight: bfloat16 [1024, 4608], P('dp'), may hold values from -0.1875 to 0.1875
- up_weight: bfloat16 [1024, 4608], P('dp'), may hold values from -0.1875 to 0.1875
- down_weight: bfloat16 [4608, 1024], P('dp'), may hold values from -0.09375 to 0.09375
- cotangent: bfloat16 [4, 4096, 1024], P('dp', 'ctx'), may hold values from -6 to 6
Outputs:
- layer_out: bfloat16 [4, 4096, 1024], P('dp', 'ctx')
- input_grad: bfloat16 [4, 4096, 1024], P('dp', 'ctx')
- attn_gain_grad: float32 [1024], P('dp')
- query_weight_grad: float32 [1024, 1024], P('dp')
- key_weight_grad: float32 [1024, 512], P('dp')
- value_weight_grad: float32 [1024, 512], P('dp')
- out_weight_grad: float32 [1024, 1024], P('dp')
- query_gain_grad: float32 [64], P('dp')
- key_gain_grad: float32 [64], P('dp')
- ffn_gain_grad: float32 [1024], P('dp')
- gate_weight_grad: float32 [1024, 4608], P('dp')
- up_weight_grad: float32 [1024, 4608], P('dp')
- down_weight_grad: float32 [4608, 1024], P('dp')
Inputs may be any that keep to these rules, and one draw needn't show every extreme that they name: `block_of`: entries 2c and 2c + 1 (the slots of ctx index c) are a block b of the sequence's first half and its mirror, the block that counts back by b from the last; every block once. Each sequence's positions are an offset of the sequence below 4096 plus the row's causal order.
All inputs are finite; a program needn't handle non-finite values.
Results may differ from a plain program's by a relative error of at most 0.025.
Values may be sent and summed in bfloat16 or wider, within the bound.
A program may use at most 192 MiB of HBM per device.

v0:
```python
from functools import partial

import jax
import jax.numpy as jnp
from jax import lax
from jax.sharding import PartitionSpec as P

HEADS = 16
KVH = 8
HD = 64
BLK = 64


NORM_EPS = 1e-05
ROPE_BASE = 1000000.0
MASKED_SCORE = -1e30


def matmul(left, right):
    return jnp.dot(left, right, preferred_element_type=jnp.float32)


def matmul_trans(left, right):
    return lax.dot_general(
        left, right, (((1,), (1,)), ((), ())), preferred_element_type=jnp.float32
    )


def rows_contract(left, right):
    return lax.dot_general(
        left, right, (((0,), (0,)), ((), ())), preferred_element_type=jnp.float32
    )


def rms_scale(values, gain):
    return values * lax.rsqrt(jnp.mean(values * values, axis=-1, keepdims=True) + NORM_EPS) * gain


def rope_tables(places):
    half_dim = HD // 2
    frequency = ROPE_BASE ** (-2.0 * jnp.arange(half_dim, dtype=jnp.float32) / HD)
    angles = places.astype(jnp.float32)[:, None] * frequency[None, :]
    return (jnp.cos(angles), jnp.sin(angles))


def rotate(values, cosine, sine_table):
    half_dim = HD // 2
    front_half = values[..., :half_dim]
    back_half = values[..., half_dim:]
    cos_rows = cosine[:, None, :]
    sin_rows = sine_table[:, None, :]
    return jnp.concatenate(
        [
            front_half * cos_rows - back_half * sin_rows,
            back_half * cos_rows + front_half * sin_rows,
        ],
        axis=-1,
    )


def qk_post(cosine, sine_table, query_flat, key_flat, gain_q, gain_k):
    row_count = query_flat.shape[0]
    query_heads = rotate(
        rms_scale(query_flat.reshape(row_count, HEADS, HD), gain_q), cosine, sine_table
    )
    key_heads = rotate(rms_scale(key_flat.reshape(row_count, KVH, HD), gain_k), cosine, sine_table)
    return (query_heads.reshape(row_count, HEADS * HD), key_heads.reshape(row_count, KVH * HD))


def swiglu(gate_proj, upward):
    return jax.nn.silu(gate_proj) * upward


def key_blocks(keys_all, values_all, key_order):
    seq_rows = keys_all.shape[0]
    block_rows = min(512, seq_rows)
    block_count = seq_rows // block_rows
    return (
        keys_all.reshape(block_count, block_rows, KVH, HD),
        values_all.reshape(block_count, block_rows, KVH, HD),
        key_order.reshape(block_count, block_rows),
    )


def score_block(query_heads, key_block, order_block, query_order):
    scores = jnp.einsum(
        "rkgd,ckd->rkgc", query_heads, key_block, preferred_element_type=jnp.float32
    ) * HD ** (-0.5)
    allowed = order_block[None, None, None, :] <= query_order[:, None, None, None]
    return (scores, allowed)


def attend_forward(queries, keys_all, values_all, query_order, key_order):
    row_count = queries.shape[0]
    group_size = HEADS // KVH
    query_heads = queries.reshape(row_count, KVH, group_size, HD)
    blocks = key_blocks(keys_all, values_all, key_order)

    def statistics(carried, block_set):
        running_max, running_sum = carried
        scores, allowed = score_block(query_heads, block_set[0], block_set[2], query_order)
        new_max = jnp.maximum(
            running_max, jnp.max(jnp.where(allowed, scores, MASKED_SCORE), axis=-1)
        )
        fresh_sum = jnp.sum(jnp.where(allowed, jnp.exp(scores - new_max[..., None]), 0.0), axis=-1)
        return ((new_max, running_sum * jnp.exp(running_max - new_max) + fresh_sum), None)

    start_max = jnp.full((row_count, KVH, group_size), MASKED_SCORE, jnp.float32)
    (final_max, final_sum), unused = lax.scan(
        statistics, (start_max, jnp.zeros_like(start_max)), blocks
    )
    log_total = final_max + jnp.log(final_sum)

    def mixing(carried, block_set):
        scores, allowed = score_block(query_heads, block_set[0], block_set[2], query_order)
        probs_low = jnp.where(allowed, jnp.exp(scores - log_total[..., None]), 0.0).astype(
            jnp.bfloat16
        )
        return (
            carried
            + jnp.einsum(
                "rkgc,ckd->rkgd", probs_low, block_set[1], preferred_element_type=jnp.float32
            ),
            None,
        )

    mixed_sum, unused = lax.scan(
        mixing, jnp.zeros((row_count, KVH, group_size, HD), jnp.float32), blocks
    )
    return (log_total, mixed_sum.reshape(row_count, HEADS * HD))


def attend_backward(queries, keys_all, values_all, mixed_grad, log_total, query_order, key_order):
    row_count = queries.shape[0]
    group_size = HEADS // KVH
    score_scale = HD ** (-0.5)
    query_heads = queries.reshape(row_count, KVH, group_size, HD)
    grad_heads = mixed_grad.reshape(row_count, KVH, group_size, HD)
    blocks = key_blocks(keys_all, values_all, key_order)

    def weighted(block_set):
        scores, allowed = score_block(query_heads, block_set[0], block_set[2], query_order)
        attn_probs = jnp.where(allowed, jnp.exp(scores - log_total[..., None]), 0.0)
        prob_grads = jnp.einsum(
            "rkgd,ckd->rkgc", grad_heads, block_set[1], preferred_element_type=jnp.float32
        )
        return (attn_probs, prob_grads)

    def gather_dot(carried, block_set):
        attn_probs, prob_grads = weighted(block_set)
        return (carried + jnp.sum(attn_probs * prob_grads, axis=-1), None)

    prob_dot, unused = lax.scan(
        gather_dot, jnp.zeros((row_count, KVH, group_size), jnp.float32), blocks
    )

    def key_step(carried, block_set):
        attn_probs, prob_grads = weighted(block_set)
        value_grad = jnp.einsum(
            "rkgc,rkgd->ckd",
            attn_probs.astype(jnp.bfloat16),
            grad_heads,
            preferred_element_type=jnp.float32,
        )
        score_grad = (attn_probs * (prob_grads - prob_dot[..., None])).astype(jnp.bfloat16)
        query_grad = (
            carried
            + jnp.einsum(
                "rkgc,ckd->rkgd", score_grad, block_set[0], preferred_element_type=jnp.float32
            )
            * score_scale
        )
        key_grad = (
            jnp.einsum(
                "rkgc,rkgd->ckd", score_grad, query_heads, preferred_element_type=jnp.float32
            )
            * score_scale
        )
        return (query_grad, (key_grad, value_grad))

    query_grad, (key_grads, value_grads) = lax.scan(
        key_step, jnp.zeros((row_count, KVH, group_size, HD), jnp.float32), blocks
    )
    seq_rows = keys_all.shape[0]
    return (
        query_grad.reshape(row_count, HEADS * HD),
        key_grads.reshape(seq_rows, KVH * HD),
        value_grads.reshape(seq_rows, KVH * HD),
    )


def on_device(
    hidden_in,
    positions,
    block_of,
    attn_gain,
    query_weight,
    key_weight,
    value_weight,
    out_weight,
    query_gain,
    key_gain,
    ffn_gain,
    gate_weight,
    up_weight,
    down_weight,
    cotangent,
):
    row_count = hidden_in.shape[1]
    ctx_place = lax.axis_index("ctx")
    in_block = jnp.arange(BLK, dtype=jnp.int32)
    own_blocks = lax.dynamic_slice_in_dim(block_of, 2 * ctx_place, 2)
    query_order = (own_blocks[:, None] * BLK + in_block[None, :]).reshape(row_count)
    key_order = (block_of[:, None] * BLK + in_block[None, :]).reshape(block_of.shape[0] * BLK)
    hidden = hidden_in[0].astype(jnp.float32)
    attn_set = (
        lax.all_gather(attn_gain, "dp", axis=0, tiled=True),
        lax.all_gather(query_weight, "dp", axis=0, tiled=True),
        lax.all_gather(key_weight, "dp", axis=0, tiled=True),
        lax.all_gather(value_weight, "dp", axis=0, tiled=True),
        lax.all_gather(out_weight, "dp", axis=0, tiled=True),
        lax.all_gather(query_gain, "dp", axis=0, tiled=True),
        lax.all_gather(key_gain, "dp", axis=0, tiled=True),
    )
    cosine, sine_table = rope_tables(positions[0])
    normed, norm_attn_back = jax.vjp(rms_scale, hidden, attn_set[0].astype(jnp.float32))
    attn_in = normed.astype(jnp.bfloat16)
    query_raw = matmul(attn_in, attn_set[1])
    key_raw = matmul(attn_in, attn_set[2])
    value_raw = matmul(attn_in, attn_set[3])
    (query_rot, key_rot), qk_back = jax.vjp(
        partial(qk_post, cosine, sine_table),
        query_raw,
        key_raw,
        attn_set[5].astype(jnp.float32),
        attn_set[6].astype(jnp.float32),
    )
    query_low = query_rot.astype(jnp.bfloat16)
    key_low = key_rot.astype(jnp.bfloat16)
    value_low = value_raw.astype(jnp.bfloat16)
    keys_all, values_all = (
        lax.all_gather(key_low, "ctx", axis=0, tiled=True),
        lax.all_gather(value_low, "ctx", axis=0, tiled=True),
    )
    log_total, mixed_out = attend_forward(query_low, keys_all, values_all, query_order, key_order)
    attn_low = mixed_out.astype(jnp.bfloat16)
    after_attn = hidden + matmul(attn_low, attn_set[4])
    ffn_set = (
        lax.all_gather(ffn_gain, "dp", axis=0, tiled=True),
        lax.all_gather(gate_weight, "dp", axis=0, tiled=True),
        lax.all_gather(up_weight, "dp", axis=0, tiled=True),
        lax.all_gather(down_weight, "dp", axis=0, tiled=True),
    )
    normed_ffn, norm_ffn_back = jax.vjp(rms_scale, after_attn, ffn_set[0].astype(jnp.float32))
    ffn_in = normed_ffn.astype(jnp.bfloat16)
    gate_proj = matmul(ffn_in, ffn_set[1])
    up_proj = matmul(ffn_in, ffn_set[2])
    activated, swiglu_back = jax.vjp(swiglu, gate_proj, up_proj)
    activated_low = activated.astype(jnp.bfloat16)
    layer_out = (after_attn + matmul(activated_low, ffn_set[3])).astype(jnp.bfloat16)
    attn_set = (
        lax.all_gather(attn_gain, "dp", axis=0, tiled=True),
        lax.all_gather(query_weight, "dp", axis=0, tiled=True),
        lax.all_gather(key_weight, "dp", axis=0, tiled=True),
        lax.all_gather(value_weight, "dp", axis=0, tiled=True),
        lax.all_gather(out_weight, "dp", axis=0, tiled=True),
        lax.all_gather(query_gain, "dp", axis=0, tiled=True),
        lax.all_gather(key_gain, "dp", axis=0, tiled=True),
    )
    ffn_set = (
        lax.all_gather(ffn_gain, "dp", axis=0, tiled=True),
        lax.all_gather(gate_weight, "dp", axis=0, tiled=True),
        lax.all_gather(up_weight, "dp", axis=0, tiled=True),
        lax.all_gather(down_weight, "dp", axis=0, tiled=True),
    )
    keys_all, values_all = (
        lax.all_gather(key_low, "ctx", axis=0, tiled=True),
        lax.all_gather(value_low, "ctx", axis=0, tiled=True),
    )
    residual_grad = cotangent[0].astype(jnp.float32)
    branch_low = residual_grad.astype(jnp.bfloat16)
    activated_grad = matmul_trans(branch_low, ffn_set[3])
    gate_grad, up_grad = swiglu_back(activated_grad)
    gate_grad_low = gate_grad.astype(jnp.bfloat16)
    up_grad_low = up_grad.astype(jnp.bfloat16)
    ffn_in_grad = matmul_trans(gate_grad_low, ffn_set[1]) + matmul_trans(up_grad_low, ffn_set[2])
    mid_part, ffn_gain_part = norm_ffn_back(ffn_in_grad)
    mid_grad = residual_grad + mid_part
    branch_attn = mid_grad.astype(jnp.bfloat16)
    mixed_grad = matmul_trans(branch_attn, attn_set[4]).astype(jnp.bfloat16)
    query_grad, key_grad_all, value_grad_all = attend_backward(
        query_low, keys_all, values_all, mixed_grad, log_total, query_order, key_order
    )
    key_grad, value_grad = (
        lax.psum_scatter(
            key_grad_all.astype(jnp.bfloat16), "ctx", scatter_dimension=0, tiled=True
        ).astype(jnp.float32),
        lax.psum_scatter(
            value_grad_all.astype(jnp.bfloat16), "ctx", scatter_dimension=0, tiled=True
        ).astype(jnp.float32),
    )
    query_pre, key_pre, query_gain_part, key_gain_part = qk_back((query_grad, key_grad))
    query_pre_low = query_pre.astype(jnp.bfloat16)
    key_pre_low = key_pre.astype(jnp.bfloat16)
    value_grad_low = value_grad.astype(jnp.bfloat16)
    attn_in_grad = (
        matmul_trans(query_pre_low, attn_set[1])
        + matmul_trans(key_pre_low, attn_set[2])
        + matmul_trans(value_grad_low, attn_set[3])
    )
    hidden_part, attn_gain_part = norm_attn_back(attn_in_grad)
    input_grad = (mid_grad + hidden_part).astype(jnp.bfloat16)
    gain_sums = lax.psum(
        (attn_gain_part, query_gain_part, key_gain_part, ffn_gain_part), ("dp", "ctx")
    )
    dp_place = lax.axis_index("dp")
    dp_count = lax.axis_size("dp")

    def own_slice(full_vector):
        piece_len = full_vector.shape[0] // dp_count
        return lax.dynamic_slice_in_dim(full_vector, dp_place * piece_len, piece_len)

    query_part = rows_contract(attn_in, query_pre_low)
    key_part = rows_contract(attn_in, key_pre_low)
    value_part = rows_contract(attn_in, value_grad_low)
    out_part = rows_contract(attn_low, branch_attn)
    gate_part = rows_contract(ffn_in, gate_grad_low)
    up_part = rows_contract(ffn_in, up_grad_low)
    down_part = rows_contract(activated_low, branch_low)
    rows_summed = (
        lax.psum_scatter(
            query_part.astype(jnp.bfloat16), "dp", scatter_dimension=0, tiled=True
        ).astype(jnp.float32),
        lax.psum_scatter(
            key_part.astype(jnp.bfloat16), "dp", scatter_dimension=0, tiled=True
        ).astype(jnp.float32),
        lax.psum_scatter(
            value_part.astype(jnp.bfloat16), "dp", scatter_dimension=0, tiled=True
        ).astype(jnp.float32),
        lax.psum_scatter(
            out_part.astype(jnp.bfloat16), "dp", scatter_dimension=0, tiled=True
        ).astype(jnp.float32),
        lax.psum_scatter(
            gate_part.astype(jnp.bfloat16), "dp", scatter_dimension=0, tiled=True
        ).astype(jnp.float32),
        lax.psum_scatter(
            up_part.astype(jnp.bfloat16), "dp", scatter_dimension=0, tiled=True
        ).astype(jnp.float32),
        lax.psum_scatter(
            down_part.astype(jnp.bfloat16), "dp", scatter_dimension=0, tiled=True
        ).astype(jnp.float32),
    )
    shards = (
        lax.psum_scatter(
            rows_summed[0].astype(jnp.bfloat16), "ctx", scatter_dimension=1, tiled=True
        ).astype(jnp.float32),
        lax.psum_scatter(
            rows_summed[1].astype(jnp.bfloat16), "ctx", scatter_dimension=1, tiled=True
        ).astype(jnp.float32),
        lax.psum_scatter(
            rows_summed[2].astype(jnp.bfloat16), "ctx", scatter_dimension=1, tiled=True
        ).astype(jnp.float32),
        lax.psum_scatter(
            rows_summed[3].astype(jnp.bfloat16), "ctx", scatter_dimension=1, tiled=True
        ).astype(jnp.float32),
        lax.psum_scatter(
            rows_summed[4].astype(jnp.bfloat16), "ctx", scatter_dimension=1, tiled=True
        ).astype(jnp.float32),
        lax.psum_scatter(
            rows_summed[5].astype(jnp.bfloat16), "ctx", scatter_dimension=1, tiled=True
        ).astype(jnp.float32),
        lax.psum_scatter(
            rows_summed[6].astype(jnp.bfloat16), "ctx", scatter_dimension=1, tiled=True
        ).astype(jnp.float32),
    )
    full_rows = (
        lax.all_gather(shards[0].astype(jnp.bfloat16), "ctx", axis=1, tiled=True).astype(
            jnp.float32
        ),
        lax.all_gather(shards[1].astype(jnp.bfloat16), "ctx", axis=1, tiled=True).astype(
            jnp.float32
        ),
        lax.all_gather(shards[2].astype(jnp.bfloat16), "ctx", axis=1, tiled=True).astype(
            jnp.float32
        ),
        lax.all_gather(shards[3].astype(jnp.bfloat16), "ctx", axis=1, tiled=True).astype(
            jnp.float32
        ),
        lax.all_gather(shards[4].astype(jnp.bfloat16), "ctx", axis=1, tiled=True).astype(
            jnp.float32
        ),
        lax.all_gather(shards[5].astype(jnp.bfloat16), "ctx", axis=1, tiled=True).astype(
            jnp.float32
        ),
        lax.all_gather(shards[6].astype(jnp.bfloat16), "ctx", axis=1, tiled=True).astype(
            jnp.float32
        ),
    )
    return (
        layer_out[None],
        input_grad[None],
        own_slice(gain_sums[0]),
        full_rows[0],
        full_rows[1],
        full_rows[2],
        full_rows[3],
        own_slice(gain_sums[1]),
        own_slice(gain_sums[2]),
        own_slice(gain_sums[3]),
        full_rows[4],
        full_rows[5],
        full_rows[6],
    )


def solution(mesh):
    in_specs = (
        P("dp", "ctx", None),
        P("dp", "ctx"),
        P(),
        P("dp"),
        P("dp", None),
        P("dp", None),
        P("dp", None),
        P("dp", None),
        P("dp"),
        P("dp"),
        P("dp"),
        P("dp", None),
        P("dp", None),
        P("dp", None),
        P("dp", "ctx", None),
    )
    out_specs = (
        P("dp", "ctx", None),
        P("dp", "ctx", None),
        P("dp"),
        P("dp", None),
        P("dp", None),
        P("dp", None),
        P("dp", None),
        P("dp"),
        P("dp"),
        P("dp"),
        P("dp", None),
        P("dp", None),
        P("dp", None),
    )
    return jax.shard_map(
        on_device, mesh=mesh, in_specs=in_specs, out_specs=out_specs, check_vma=False
    )
```

profile of v0, /device:TPU:1, one launch (start us, length us, event | category | flops | bytes accessed | tf_op | source)
XLA Modules:
  0.0 2009.1 jit_solution(2293354181877165440)
XLA Ops:
  10.1 8.8 all-gather
  22.5 6.8 all-reduce.7
  31.3 4.7 all-gather.19.cloned.1.call-done
  40.5 21.5 %all-gather.15.cloned.1.call-done = bf16[1024,512]{1,0:T(8,128)(2,1)} async-done(((bf16[256,512]{1,0:T(8,128)(2,1)}), bf16[1024,512]{1,0:T(8,128)(2,1)}) %all-gather.15.cloned.1.call-update) | async-done | bytes 1048592 | tf_op jit(solution)/shard_map/all_gather | solution.py:220
  67.7 6.9 all-gather.1
  74.6 21.2 %all-gather.23.cloned.1.call-done = bf16[1024,1024]{1,0:T(8,128)(2,1)} async-done(((bf16[256,1024]{1,0:T(8,128)(2,1)}), bf16[1024,1024]{1,0:T(8,128)(2,1)}) %all-gather.23.cloned.1.call-update) | async-done | bytes 2097168 | tf_op jit(solution)/shard_map/all_gather | solution.py:218
  100.3 47.9 %all-gather.21.cloned.1.call-done = bf16[4096,512]{0,1:T(8,128)(2,1)} async-done(((bf16[128,512]{0,1:T(8,128)(2,1)}), bf16[4096,512]{0,1:T(8,128)(2,1)}) %all-gather.21.cloned.1.call-update) | async-done | bytes 4194320 | tf_op jit(solution)/shard_map/all_gather | solution.py:242
  148.2 4.4 copy.125
  156.1 58.8 %while.50 = (s32[]{:T(128)}, f32[128,8,2]{0,2,1:T(2,128)S(1)}, f32[128,8,2]{0,2,1:T(2,128)S(1)}, s32[8,512]{1,0:T(8,128)S(1)}, bf16[8,512,8,64]{1,3,2,0:T(8,128)...) while((s32[]{:T(128)}, f32[128,8,2]{0,2,1:T(2,128)S(1)}, ...), condition=%wide.region_6.7_spmd.clone, body=%wide.region_3.6_spmd.clone.sunk | while | flops 141633664 | bytes 9486964 | solution.py:109
  214.9 11.2 reshape.460
  226.2 9.8 copy.65
  236.0 24.1 %while.51 = (s32[]{:T(128)}, f32[128,8,2,64]{0,3,2,1:T(8,128)S(1)}, bf16[8,512,8,64]{1,3,2,0:T(8,128)(2,1)}, s32[8,512]{1,0:T(8,128)S(1)}, bf16[8,512,8,64]{1,3,...) while((s32[]{:T(128)}, f32[128,8,2,64]{0,3,2,1:T(8,128)S(1)}, ...), condition=%wide.region_8.9_spmd.clone, body=%wide.region_7.8_spmd.clone.sunk | while | flops 272957568 | bytes 2507899 | solution.py:127
  262.5 59.2 %all-gather.27.cloned.1.call-done = bf16[1024,4608]{1,0:T(8,128)(2,1)} async-done(((bf16[256,4608]{1,0:T(8,128)(2,1)}), bf16[1024,4608]{1,0:T(8,128)(2,1)}) %all-gather.27.cloned.1.call-update) | async-done | bytes 9437200 | tf_op jit(solution)/shard_map/all_gather | solution.py:250
  321.7 6.5 fusion.123
  328.3 88.1 %all-gather.29.cloned.1.call-done = bf16[1024,4608]{1,0:T(8,128)(2,1)} async-done(((bf16[256,4608]{1,0:T(8,128)(2,1)}), bf16[1024,4608]{1,0:T(8,128)(2,1)}) %all-gather.29.cloned.1.call-update) | async-done | bytes 9437200 | tf_op jit(solution)/shard_map/all_gather | solution.py:251
  416.4 6.5 fusion.124
  422.9 88.2 %all-gather.31.cloned.1.call-done = bf16[4608,1024]{1,0:T(8,128)(2,1)} async-done(((bf16[1152,1024]{1,0:T(8,128)(2,1)}), bf16[4608,1024]{1,0:T(8,128)(2,1)}) %all-gather.31.cloned.1.call-update) | async-done | bytes 9437200 | tf_op jit(solution)/shard_map/all_gather | solution.py:252
  511.0 9.9 multiply_convert_fusion
  520.9 7.7 fusion.125
  533.8 63.8 %while.52 = (s32[]{:T(128)}, f32[128,8,2]{0,2,1:T(2,128)S(1)}, s32[8,512]{1,0:T(8,128)S(1)}, bf16[8,512,8,64]{1,3,2,0:T(8,128)(2,1)}, bf16[128,8,2,64]{0,3,2,1:T...) while((s32[]{:T(128)}, f32[128,8,2]{0,2,1:T(2,128)S(1)}, ...), condition=%wide.region_13.14_spmd.clone, body=%wide.region_11.13_spmd.clone.sunk | while | flops 273746048 | bytes 10142851 | solution.py:153
  597.6 112.0 %while.53 = (s32[]{:T(128)}, f32[128,8,2,64]{0,3,2,1:T(8,128)S(1)}, bf16[8,512,8,64]{1,3,2,0:T(8,128)(2,1)}, bf16[8,512,8,64]{1,3,2,0:T(8,128)(2,1)}, bf16[8,512...) while((s32[]{:T(128)}, f32[128,8,2,64]{0,3,2,1:T(8,128)S(1)}, ...), condition=%wide.region_15.16_spmd.clone, body=%wide.region_14.15_spmd.clone.sunk | while | flops 682295424 | bytes 41650872 | solution.py:181
  601.8 4.0 fusion.225
  615.8 4.0 fusion.225
  643.8 4.0 fusion.225
  657.8 4.0 fusion.225
  671.8 4.0 fusion.225
  699.8 4.0 fusion.225
  709.6 10.0 copy.121
  719.6 11.8 reshape.442
  731.5 10.0 copy.122
  741.5 11.9 reshape.444
  754.7 5.2 convolution_convert_fusion.2
  761.2 5.2 convolution_convert_fusion.1
  767.7 5.3 convolution_convert_fusion
  779.0 34.0 %reduce-scatter.49.cloned.1.call-done = bf16[128,512]{1,0:T(8,128)(2,1)} async-done(((bf16[4096,512]{1,0:T(8,128)(2,1)}), bf16[128,512]{1,0:T(8,128)(2,1)}) %reduce-scatter.49.cloned.1.call-update) | async-done | bytes 131088
  816.0 83.0 %reduce-scatter.51.cloned.1.call-done = bf16[128,512]{1,0:T(8,128)(2,1)} async-done(((bf16[4096,512]{1,0:T(8,128)(2,1)}), bf16[128,512]{1,0:T(8,128)(2,1)}) %reduce-scatter.51.cloned.1.call-update) | async-done | bytes 131088
  901.5 89.8 %reduce-scatter.43.cloned.1.call-done = bf16[256,4608]{1,0:T(8,128)(2,1)} async-done(((bf16[1024,4608]{1,0:T(8,128)(2,1)}), bf16[256,4608]{1,0:T(8,128)(2,1)}) %reduce-scatter.43.cloned.1.call-update) | async-done | bytes 2359312 | tf_op jit(solution)/shard_map/reduce_scatter | solution.py:343
  991.2 4.3 copy.113
  995.6 86.9 %reduce-scatter.45.cloned.1.call-done = bf16[256,4608]{1,0:T(8,128)(2,1)} async-done(((bf16[1024,4608]{1,0:T(8,128)(2,1)}), bf16[256,4608]{1,0:T(8,128)(2,1)}) %reduce-scatter.45.cloned.1.call-update) | async-done | bytes 2359312 | tf_op jit(solution)/shard_map/reduce_scatter | solution.py:346
  1082.5 4.3 copy.115
  1086.8 86.7 %reduce-scatter.47.cloned.1.call-done = bf16[1152,1024]{1,0:T(8,128)(2,1)} async-done(((bf16[4608,1024]{1,0:T(8,128)(2,1)}), bf16[1152,1024]{1,0:T(8,128)(2,1)}) %reduce-scatter.47.cloned.1.call-update) | async-done | bytes 2359312 | tf_op jit(solution)/shard_map/reduce_scatter | solution.py:349
  1173.6 4.3 copy.117
  1177.9 27.3 %reduce-scatter.41.cloned.1.call-done = bf16[256,1024]{1,0:T(8,128)(2,1)} async-done(((bf16[1024,1024]{1,0:T(8,128)(2,1)}), bf16[256,1024]{1,0:T(8,128)(2,1)}) %reduce-scatter.41.cloned.1.call-update) | async-done | bytes 524304 | tf_op jit(solution)/shard_map/reduce_scatter | solution.py:340
  1207.4 29.7 %reduce-scatter.35.cloned.1.call-done = bf16[256,1024]{1,0:T(8,128)(2,1)} async-done(((bf16[1024,1024]{1,0:T(8,128)(2,1)}), bf16[256,1024]{1,0:T(8,128)(2,1)}) %reduce-scatter.35.cloned.1.call-update) | async-done | bytes 524304 | tf_op jit(solution)/shard_map/reduce_scatter | solution.py:331
  1239.2 22.5 %reduce-scatter.37.cloned.1.call-done = bf16[256,512]{1,0:T(8,128)(2,1)} async-done(((bf16[1024,512]{1,0:T(8,128)(2,1)}), bf16[256,512]{1,0:T(8,128)(2,1)}) %reduce-scatter.37.cloned.1.call-update) | async-done | bytes 262160 | tf_op jit(solution)/shard_map/reduce_scatter | solution.py:334
  1263.6 24.4 %reduce-scatter.39.cloned.1.call-done = bf16[256,512]{1,0:T(8,128)(2,1)} async-done(((bf16[1024,512]{1,0:T(8,128)(2,1)}), bf16[256,512]{1,0:T(8,128)(2,1)}) %reduce-scatter.39.cloned.1.call-update) | async-done | bytes 262160 | tf_op jit(solution)/shard_map/reduce_scatter | solution.py:337
  1289.8 81.2 %reduce-scatter.61.cloned.1.call-done = bf16[144,256]{1,0:T(8,128)(2,1)} async-done(((bf16[4608,256]{1,0:T(8,128)(2,1)}), bf16[144,256]{1,0:T(8,128)(2,1)}) %reduce-scatter.61.cloned.1.call-update) | async-done | bytes 73744
  1371.1 83.0 %reduce-scatter.63.cloned.1.call-done = bf16[144,256]{1,0:T(8,128)(2,1)} async-done(((bf16[4608,256]{1,0:T(8,128)(2,1)}), bf16[144,256]{1,0:T(8,128)(2,1)}) %reduce-scatter.63.cloned.1.call-update) | async-done | bytes 73744
  1454.2 82.7 %reduce-scatter.65.cloned.1.call-done = bf16[32,1152]{1,0:T(8,128)(2,1)} async-done(((bf16[1024,1152]{1,0:T(8,128)(2,1)}), bf16[32,1152]{1,0:T(8,128)(2,1)}) %reduce-scatter.65.cloned.1.call-update) | async-done | bytes 73744
  1540.2 5.8 fusion.83
  1545.9 71.2 %reduce-scatter.59.cloned.1.call-done = bf16[32,256]{1,0:T(8,128)(2,1)} async-done(((bf16[1024,256]{1,0:T(8,128)(2,1)}), bf16[32,256]{1,0:T(8,128)(2,1)}) %reduce-scatter.59.cloned.1.call-update) | async-done | bytes 16400
  1617.2 26.2 %all_gather.85 = bf16[256,1024]{0,1:T(8,128)(2,1)S(1)} all-gather(bf16[256,32]{0,1:T(8,128)(2,1)} %bitcast.402), channel_id=1, replica_groups=mesh['dp'=4,'ctx'=32] {'ctx'}, dimensions={1}, use_global_device_ids=true | all-gather | bytes 540672 | tf_op jit(solution)/shard_map/all_gather | solution.py:386
  1644.5 52.8 %reduce-scatter.53.cloned.1.call-done = bf16[32,256]{1,0:T(8,128)(2,1)} async-done(((bf16[1024,256]{1,0:T(8,128)(2,1)}), bf16[32,256]{1,0:T(8,128)(2,1)}) %reduce-scatter.53.cloned.1.call-update) | async-done | bytes 16400
  1697.3 26.5 %all_gather.82 = bf16[256,1024]{0,1:T(8,128)(2,1)S(1)} all-gather(bf16[256,32]{0,1:T(8,128)(2,1)} %bitcast.403), channel_id=1, replica_groups=mesh['dp'=4,'ctx'=32] {'ctx'}, dimensions={1}, use_global_device_ids=true | all-gather | bytes 540672 | tf_op jit(solution)/shard_map/all_gather | solution.py:377
  1727.3 64.4 %all-reduce.6 = (f32[1024]{0:T(1024)S(1)}, f32[64]{0:T(128)S(1)}, f32[64]{0:T(128)S(1)}, f32[1024]{0:T(1024)S(1)}) all-reduce(f32[1024]{0:T(1024)S(1)} %get-tuple-element.461, f32[64]{0:T(128)S(1)} %get-tuple-element.459, f32[64]{0:T(128)S(1)} %get-tuple-element.463, ...), channel_id=1, replica_groups=mesh['dp'=4,'ctx'=32] {'dp','ctx'}, use_global_device_ids=true, to_apply=%region_22.23 | all-reduce | flops 2176 | bytes 17408 | tf_op jit(solution)/shard_map/psum | solution.py:313
  1795.0 23.1 %all_gather.83 = bf16[256,512]{0,1:T(8,128)(2,1)S(1)} all-gather(bf16[256,16]{0,1:T(8,128)(2,1)} %bitcast.405), channel_id=1, replica_groups=mesh['dp'=4,'ctx'=32] {'ctx'}, dimensions={1}, use_global_device_ids=true | all-gather | bytes 270336 | tf_op jit(solution)/shard_map/all_gather | solution.py:380
  1819.0 37.9 %reduce-scatter.57.cloned.1.call-done = bf16[16,256]{1,0:T(8,128)(2,1)} async-done(((bf16[512,256]{1,0:T(8,128)(2,1)}), bf16[16,256]{1,0:T(8,128)(2,1)}) %reduce-scatter.57.cloned.1.call-update) | async-done | bytes 8208
  1857.0 26.6 %all_gather.84 = bf16[256,512]{0,1:T(8,128)(2,1)S(1)} all-gather(bf16[256,16]{0,1:T(8,128)(2,1)} %bitcast.406), channel_id=1, replica_groups=mesh['dp'=4,'ctx'=32] {'ctx'}, dimensions={1}, use_global_device_ids=true | all-gather | bytes 270336 | tf_op jit(solution)/shard_map/all_gather | solution.py:383
  1884.5 20.8 %all-gather.33.cloned.1.call-done = bf16[256,4608]{0,1:T(8,128)(2,1)} async-done(((bf16[256,144]{0,1:T(8,128)(2,1)}), bf16[256,4608]{0,1:T(8,128)(2,1)}) %all-gather.33.cloned.1.call-update) | async-done | bytes 2359312 | tf_op jit(solution)/shard_map/all_gather | solution.py:389
  1905.3 4.5 copy.85
  1909.9 41.4 %all-gather.35.cloned.1.call-done = bf16[256,4608]{0,1:T(8,128)(2,1)} async-done(((bf16[256,144]{0,1:T(8,128)(2,1)}), bf16[256,4608]{0,1:T(8,128)(2,1)}) %all-gather.35.cloned.1.call-update) | async-done | bytes 2359312 | tf_op jit(solution)/shard_map/all_gather | solution.py:392
  1951.3 4.5 copy.86
  1955.9 41.6 %all-gather.37.cloned.1.call-done = bf16[1152,1024]{0,1:T(8,128)(2,1)} async-done(((bf16[1152,32]{0,1:T(8,128)(2,1)}), bf16[1152,1024]{0,1:T(8,128)(2,1)}) %all-gather.37.cloned.1.call-update) | async-done | bytes 2359312 | tf_op jit(solution)/shard_map/all_gather | solution.py:395
  1997.4 4.6 copy.87
  (491 shorter events, 302.1 us)
Async XLA Ops:
  7.2 54.9 %copy-start.2 = (bf16[1,128,1024]{2,1,0:T(8,128)(2,1)S(1)}, bf16[1,128,1024]{2,1,0:T(8,128)(2,1)}, u32[]{:S(2)}) copy-start(bf16[1,128,1024]{2,1,0:T(8,128)(2,1)} %param.23) | copy-start | bytes 786436
  7.2 28.9 %all-gather.19.cloned.1.call-start = ((), (), s32[]{:S(2)}) async-start(), calls=%async_computation.18 | async-start | bytes 1310720 | tf_op jit(solution)/shard_map/all_gather | solution.py:219
  7.9 54.1 %all-gather.15.cloned.1.call-start = ((), (), s32[]{:S(2)}) async-start(), calls=%async_computation.16 | async-start | bytes 1310720 | tf_op jit(solution)/shard_map/all_gather | solution.py:220
  8.7 87.1 %all-gather.23.cloned.1.call-start = ((), (), s32[]{:S(2)}) async-start(), calls=%async_computation.20 | async-start | bytes 2621440 | tf_op jit(solution)/shard_map/all_gather | solution.py:218
  9.4 138.8 %all-gather.21.cloned.1.call-start = ((), (), s32[]{:S(2)}) async-start(), calls=%async_computation.19 | async-start | bytes 4325376 | tf_op jit(solution)/shard_map/all_gather | solution.py:242
  18.9 79.8 %copy-start.29 = (f32[4,1,256]{2,1,0:T(1,128)}, f32[4,1,256]{2,1,0:T(1,128)S(1)}, u32[]{:S(2)}) copy-start(f32[4,1,256]{2,1,0:T(1,128)S(1)} %convert_element_type.248) | copy-start | bytes 12292
  29.4 36.3 %copy-start.43 = (f32[64]{0:T(128)}, f32[64]{0:T(128)S(1)}, u32[]{:S(2)}) copy-start(f32[64]{0:T(128)S(1)} %convert_element_type.207) | copy-start | bytes 772
  30.5 35.2 %copy-start.45 = (f32[128]{0:T(128)}, f32[128]{0:T(128)S(1)}, u32[]{:S(2)}) copy-start(f32[128]{0:T(128)S(1)} %fusion.92) | copy-start | bytes 1540
  30.5 68.2 %copy-start.39 = (f32[128]{0:T(128)}, f32[128]{0:T(128)S(1)}, u32[]{:S(2)}) copy-start(f32[128]{0:T(128)S(1)} %fusion.117) | copy-start | bytes 1540
  31.3 68.4 %copy-start.25 = (f32[128,32]{0,1:T(8,128)}, f32[128,32]{0,1:T(8,128)S(1)}, u32[]{:S(2)}) copy-start(f32[128,32]{0,1:T(8,128)S(1)} %get-tuple-element.556) | copy-start | bytes 49156
  31.3 68.4 %copy-start.27 = (f32[128,32]{0,1:T(8,128)}, f32[128,32]{0,1:T(8,128)S(1)}, u32[]{:S(2)}) copy-start(f32[128,32]{0,1:T(8,128)S(1)} %get-tuple-element.557) | copy-start | bytes 49156
  39.0 28.1 %copy-start.16 = (f32[128,8,64]{0,2,1:T(8,128)}, f32[128,8,64]{0,2,1:T(8,128)S(1)}, u32[]{:S(2)}) copy-start(f32[128,8,64]{0,2,1:T(8,128)S(1)} %get-tuple-element.559) | copy-start | bytes 786436
  40.5 174.5 %all-gather.17.cloned.1.call-start = ((), (), s32[]{:S(2)}) async-start(), calls=%async_computation.17 | async-start | bytes 4325376 | tf_op jit(solution)/shard_map/all_gather | solution.py:243
  64.3 195.8 %all-gather.25.cloned.1.call-start = ((), (), s32[]{:S(2)}) async-start(), calls=%async_computation.21 | async-start | bytes 2621440 | tf_op jit(solution)/shard_map/all_gather | solution.py:221
  64.9 256.9 %all-gather.27.cloned.1.call-start = ((), (), s32[]{:S(2)}) async-start(), calls=%async_computation.22 | async-start | bytes 11796480 | tf_op jit(solution)/shard_map/all_gather | solution.py:250
  65.6 350.7 %all-gather.29.cloned.1.call-start = ((), (), s32[]{:S(2)}) async-start(), calls=%async_computation.23 | async-start | bytes 11796480 | tf_op jit(solution)/shard_map/all_gather | solution.py:251
  66.4 444.6 %all-gather.31.cloned.1.call-start = ((), (), s32[]{:S(2)}) async-start(), calls=%async_computation.24 | async-start | bytes 11796480 | tf_op jit(solution)/shard_map/all_gather | solution.py:252
  67.1 745.9 %reduce-scatter.49.cloned.1.call-start = ((), (), s32[]{:S(2)}) async-start(), calls=%async_computation.35 | async-start | bytes 4325376
  67.3 32.5 %copy-start.41 = (f32[64]{0:T(128)}, f32[64]{0:T(128)S(1)}, u32[]{:S(2)}) copy-start(f32[64]{0:T(128)S(1)} %convert_element_type.211) | copy-start | bytes 772
  99.5 53.2 %copy-start.33 = (f32[128,16]{0,1:T(8,128)}, f32[128,16]{0,1:T(8,128)S(1)}, u32[]{:S(2)}) copy-start(f32[128,16]{0,1:T(8,128)S(1)} %get-tuple-element.560) | copy-start | bytes 24580
  99.5 53.1 %copy-start.31 = (f32[128,16]{0,1:T(8,128)}, f32[128,16]{0,1:T(8,128)S(1)}, u32[]{:S(2)}) copy-start(f32[128,16]{0,1:T(8,128)S(1)} %fusion.115) | copy-start | bytes 24580
  226.2 9.8 copy-start.23
  260.1 68.2 %copy-start.18 = (bf16[128,8,2,64]{0,3,2,1:T(8,128)(2,1)}, bf16[128,8,2,64]{0,3,2,1:T(8,128)(2,1)S(1)}, u32[]{:S(2)}) copy-start(bf16[128,8,2,64]{0,3,2,1:T(8,128)(2,1)S(1)} %convert_element_type.213) | copy-start | bytes 786436
  262.4 269.5 %copy-start.3 = (f32[128,1024]{1,0:T(8,128)}, f32[128,1024]{1,0:T(8,128)S(1)}, u32[]{:S(2)}) copy-start(f32[128,1024]{1,0:T(8,128)S(1)} %get-tuple-element.563) | copy-start | bytes 1572868
  328.3 182.8 %copy-start.21 = (bf16[1,128,1024]{2,1,0:T(8,128)(2,1)S(1)}, bf16[1,128,1024]{2,1,0:T(8,128)(2,1)}, u32[]{:S(2)}) copy-start(bf16[1,128,1024]{2,1,0:T(8,128)(2,1)} %param.37) | copy-start | bytes 786436
  520.9 7.7 copy-start.13
  520.9 7.7 copy-start.11
  520.9 7.7 copy-start.1
  601.8 5.6 copy-start
  615.8 5.6 copy-start
  629.8 5.6 copy-start
  643.8 5.6 copy-start
  657.8 5.6 copy-start
  671.8 5.6 copy-start
  685.8 5.6 copy-start
  699.8 5.6 copy-start
  731.4 167.6 %reduce-scatter.51.cloned.1.call-start = ((), (), s32[]{:S(2)}) async-start(), calls=%async_computation.36 | async-start | bytes 4325376
  753.4 237.9 %reduce-scatter.43.cloned.1.call-start = ((), (), s32[]{:S(2)}) async-start(), calls=%async_computation.29 | async-start | bytes 11796480 | tf_op jit(solution)/shard_map/reduce_scatter | solution.py:343
  759.9 322.5 %reduce-scatter.45.cloned.1.call-start = ((), (), s32[]{:S(2)}) async-start(), calls=%async_computation.31 | async-start | bytes 11796480 | tf_op jit(solution)/shard_map/reduce_scatter | solution.py:346
  766.4 407.1 %reduce-scatter.47.cloned.1.call-start = ((), (), s32[]{:S(2)}) async-start(), calls=%async_computation.33 | async-start | bytes 11796480 | tf_op jit(solution)/shard_map/reduce_scatter | solution.py:349
  773.2 3.7 copy-start.30
  773.2 432.1 %reduce-scatter.41.cloned.1.call-start = ((), (), s32[]{:S(2)}) async-start(), calls=%async_computation.28 | async-start | bytes 2621440 | tf_op jit(solution)/shard_map/reduce_scatter | solution.py:340
  776.2 460.9 %reduce-scatter.35.cloned.1.call-start = ((), (), s32[]{:S(2)}) async-start(), calls=%async_computation.25 | async-start | bytes 2621440 | tf_op jit(solution)/shard_map/reduce_scatter | solution.py:331
  776.4 37.7 %copy-start.17 = (f32[128,8,64]{0,2,1:T(8,128)S(1)}, f32[128,8,64]{0,2,1:T(8,128)}, u32[]{:S(2)}) copy-start(f32[128,8,64]{0,2,1:T(8,128)} %copy-done.16) | copy-start | bytes 786436
  776.4 37.7 %copy-start.36 = (f32[128,8]{0,1:T(8,128)S(1)}, f32[128,8]{0,1:T(8,128)}, u32[]{:S(2)}) copy-start(f32[128,8]{0,1:T(8,128)} %copy-done.35) | copy-start | bytes 12292
  776.4 37.7 %copy-start.44 = (f32[64]{0:T(128)S(1)}, f32[64]{0:T(128)}, u32[]{:S(2)}) copy-start(f32[64]{0:T(128)} %copy-done.43) | copy-start | bytes 772
  776.4 37.9 %copy-start.38 = (f32[128,8]{0,1:T(8,128)S(1)}, f32[128,8]{0,1:T(8,128)}, u32[]{:S(2)}) copy-start(f32[128,8]{0,1:T(8,128)} %copy-done.37) | copy-start | bytes 12292
  779.0 482.8 %reduce-scatter.37.cloned.1.call-start = ((), (), s32[]{:S(2)}) async-start(), calls=%async_computation.26 | async-start | bytes 1310720 | tf_op jit(solution)/shard_map/reduce_scatter | solution.py:334
  816.0 472.0 %reduce-scatter.39.cloned.1.call-start = ((), (), s32[]{:S(2)}) async-start(), calls=%async_computation.27 | async-start | bytes 1310720 | tf_op jit(solution)/shard_map/reduce_scatter | solution.py:337
  901.4 469.6 %reduce-scatter.61.cloned.1.call-start = ((), (), s32[]{:S(2)}) async-start(), calls=%async_computation.41 | async-start | bytes 2433024
  995.5 458.6 %reduce-scatter.63.cloned.1.call-start = ((), (), s32[]{:S(2)}) async-start(), calls=%async_computation.42 | async-start | bytes 2433024
  1086.8 450.1 %reduce-scatter.65.cloned.1.call-start = ((), (), s32[]{:S(2)}) async-start(), calls=%async_computation.43 | async-start | bytes 2433024
  1177.9 362.3 %copy-start.4 = (f32[128,1024]{1,0:T(8,128)S(1)}, f32[128,1024]{1,0:T(8,128)}, u32[]{:S(2)}) copy-start(f32[128,1024]{1,0:T(8,128)} %copy-done.3) | copy-start | bytes 1572868
  1177.9 439.3 %reduce-scatter.59.cloned.1.call-start = ((), (), s32[]{:S(2)}) async-start(), calls=%async_computation.40 | async-start | bytes 540672
  1207.3 490.0 %reduce-scatter.53.cloned.1.call-start = ((), (), s32[]{:S(2)}) async-start(), calls=%async_computation.37 | async-start | bytes 540672
  1239.1 555.9 %reduce-scatter.55.cloned.1.call-start = ((), (), s32[]{:S(2)}) async-start(), calls=%async_computation.38 | async-start | bytes 270336
  1263.5 593.4 %reduce-scatter.57.cloned.1.call-start = ((), (), s32[]{:S(2)}) async-start(), calls=%async_computation.39 | async-start | bytes 270336
  1289.8 615.6 %all-gather.33.cloned.1.call-start = ((), (), s32[]{:S(2)}) async-start(), calls=%async_computation.30 | async-start | bytes 2433024 | tf_op jit(solution)/shard_map/all_gather | solution.py:389
  1371.0 580.3 %all-gather.35.cloned.1.call-start = ((), (), s32[]{:S(2)}) async-start(), calls=%async_computation.32 | async-start | bytes 2433024 | tf_op jit(solution)/shard_map/all_gather | solution.py:392
  1454.2 543.3 %all-gather.37.cloned.1.call-start = ((), (), s32[]{:S(2)}) async-start(), calls=%async_computation.34 | async-start | bytes 2433024 | tf_op jit(solution)/shard_map/all_gather | solution.py:395
  1545.9 179.1 %copy-start.15 = (bf16[1024,512]{1,0:T(8,128)(2,1)S(1)}, bf16[1024,512]{1,0:T(8,128)(2,1)}, u32[]{:S(2)}) copy-start(bf16[1024,512]{1,0:T(8,128)(2,1)} %all-gather.19.cloned.1.call-done) | copy-start | bytes 3145732
  1545.9 179.1 %copy-start.20 = (f32[128,1024]{1,0:T(8,128)S(1)}, f32[128,1024]{1,0:T(8,128)}, u32[]{:S(2)}) copy-start(f32[128,1024]{1,0:T(8,128)} %fusion.126) | copy-start | bytes 1572868
  1545.9 179.5 %copy-start.24 = (bf16[128,512]{1,0:T(8,128)(2,1)S(1)}, bf16[128,512]{1,0:T(8,128)(2,1)}, u32[]{:S(2)}) copy-start(bf16[128,512]{1,0:T(8,128)(2,1)} %reduce-scatter.51.cloned.1.call-done) | copy-start | bytes 393220
  1643.4 150.8 %copy-start.46 = (f32[128]{0:T(128)S(1)}, f32[128]{0:T(128)}, u32[]{:S(2)}) copy-start(f32[128]{0:T(128)} %copy-done.45) | copy-start | bytes 1540
  (20 other events, 44.4 us)
Sparse Core Ops, SparseCore 0:
  9.7 26.3 all-gather.18
  37.7 24.2 all-gather.14
  63.7 32.0 all-gather.22
  98.4 49.7 all-gather.20
  150.9 45.8 all-gather.16
  198.3 29.6 all-gather.24
  229.7 91.9 all-gather.26
  323.4 92.9 all-gather.28
  418.1 92.9 all-gather.30
  731.5 81.4 reduce-scatter.48
  817.7 81.2 reduce-scatter.50
  901.3 89.9 reduce-scatter.42
  993.7 88.7 reduce-scatter.44
  1084.8 88.7 reduce-scatter.46
  1175.8 29.3 reduce-scatter.40
  1207.6 29.3 reduce-scatter.34
  1239.9 21.7 reduce-scatter.36
  1264.7 23.2 reduce-scatter.38
  1292.1 78.8 reduce-scatter.60
  1375.4 78.6 reduce-scatter.62
  1458.3 78.5 reduce-scatter.64
  1540.8 76.3 reduce-scatter.58
  1621.0 76.2 reduce-scatter.52
  1701.0 75.8 reduce-scatter.54
  1780.7 76.1 reduce-scatter.56
  1859.3 45.9 all-gather.32
  1907.7 43.5 all-gather.34
  1953.8 43.5 all-gather.36
where the time goes:
time: 2020 us; the launch traced here: 2010 us
  waiting for transfers between devices  1330 us (66%)
  matrix products  298 us (15%)
  blocking collectives  189 us (9%)
  local copies, waits for them, and re-layouts  132 us (7%)
  other arithmetic  36.8 us (2%)
    unnamed x37, waiting for transfers between devices  531 us
    unnamed x125, local copies, waits for them, and re-layouts  110 us
    dot_general x24, matrix products, score_block(): jnp.einsum('rkgd,ckd->rkgc', query_heads, key_block, preferred_element_ty...  93 us
    reduce_scatter x1, waiting for transfers between devices, on_device(): lax.psum_scatter(gate_part.astype(jnp.bfloat16), 'dp', scatter_dimension=...  89.8 us
    all_gather x1, waiting for transfers between devices, on_device(): lax.all_gather(down_weight, 'dp', axis=0, tiled=True)  88.2 us
    all_gather x1, waiting for transfers between devices, on_device(): lax.all_gather(up_weight, 'dp', axis=0, tiled=True)  88.1 us
    reduce_scatter x1, waiting for transfers between devices, on_device(): lax.psum_scatter(up_part.astype(jnp.bfloat16), 'dp', scatter_dimension=0,...  86.9 us
    reduce_scatter x1, waiting for transfers between devices, on_device(): lax.psum_scatter(down_part.astype(jnp.bfloat16), 'dp', scatter_dimension=...  86.7 us
  transfers between devices with their start and end apart: 28, of which 25 were waited for; matrix products, arithmetic and copies ran while one was open for 12% of the time, Pallas kernels for 0%

commit v1 on v0

v1 whole, which is shorter than its diff:
```python
import jax
import jax.numpy as jnp
import numpy as np
from jax import lax
from jax.experimental import pallas as pl
from jax.experimental.pallas import tpu as pltpu
from jax.sharding import Mesh, PartitionSpec as P

HEADS = 16
KVH = 8
HD = 64
BLK = 64
LINE = 8
QUARTERS = 4
HALF = 512
ROWS = 1024

NORM_EPS = 1e-05
ROPE_BASE = 1000000.0
EXP2_SCALE = float(HD ** -0.5 * np.log2(np.e))
SCORE_SCALE = HD ** -0.5

F32 = jnp.float32
BF16 = jnp.bfloat16


def dot(left, right, left_dim=1, right_dim=0):
    return lax.dot_general(
        left, right, (((left_dim,), (right_dim,)), ((), ())), preferred_element_type=F32
    )


def rms_scale(values, gain):
    return values * lax.rsqrt(jnp.mean(values * values, axis=-1, keepdims=True) + NORM_EPS) * gain


def head_norm_rope(raw, gain, cosine, sine):
    scaled = (
        raw
        * lax.rsqrt(jnp.mean(raw * raw, axis=1, keepdims=True) + NORM_EPS)
        * gain[None, :, None]
    )
    front = scaled[:, : HD // 2]
    back = scaled[:, HD // 2 :]
    return jnp.concatenate(
        [front * cosine - back * sine, back * cosine + front * sine], axis=1
    )


def scores_of(keys_t, queries_t):
    return dot(keys_t, queries_t, 0, 0)


def attend_kernel(q_ref, kv_ref, qo_ref, ko_ref, mixed_ref, low_ref, log_ref):
    for half in range(2):
        cols = slice(half * HALF, (half + 1) * HALF)
        q_order = qo_ref[:, cols]
        for head in range(2):
            q_t = q_ref[head * HD : (head + 1) * HD, cols]

            def quarter(z, carried):
                acc, total = carried
                for k_half in range(half + 1):
                    keys = slice(k_half * HALF, (k_half + 1) * HALF)
                    probs = jnp.exp2(scores_of(kv_ref[z, 0:HD, keys], q_t) * EXP2_SCALE)
                    if k_half == half:
                        allowed = ko_ref[z, keys, :] <= q_order
                        probs = jnp.where(allowed, probs, 0.0)
                    total = total + jnp.sum(probs, axis=0, keepdims=True)
                    acc = acc + dot(kv_ref[z, HD : 2 * HD, keys], probs.astype(BF16))
                return acc, total

            acc, total = lax.fori_loop(
                0,
                QUARTERS,
                quarter,
                (jnp.zeros((HD, HALF), F32), jnp.zeros((1, HALF), F32)),
            )
            mixed = acc / total
            mixed_ref[head * HD : (head + 1) * HD, cols] = mixed
            low_ref[head * HD : (head + 1) * HD, cols] = mixed.astype(BF16)
            log_ref[head : head + 1, cols] = jnp.log2(total)


def attend(q_t, kv_t, q_order, k_order):
    return pl.pallas_call(
        attend_kernel,
        out_shape=(
            jax.ShapeDtypeStruct((2 * HD, ROWS), F32),
            jax.ShapeDtypeStruct((2 * HD, ROWS), BF16),
            jax.ShapeDtypeStruct((2, ROWS), F32),
        ),
        in_specs=[pl.BlockSpec(memory_space=pltpu.VMEM)] * 4,
        out_specs=(pl.BlockSpec(memory_space=pltpu.VMEM),) * 3,
        compiler_params=pltpu.CompilerParams(vmem_limit_bytes=40 * 2**20),
        cost_estimate=pl.CostEstimate(flops=2 * 10**9, bytes_accessed=4 * 10**6, transcendentals=6 * 10**6),
    )(q_t, kv_t, q_order, k_order)


def attend_back_kernel(
    q_ref, kv_ref, qo_ref, ko_ref, mixed_ref, log_ref, grad_ref, dq_ref, dkv_ref, dkv_acc
):
    dkv_acc[...] = jnp.zeros_like(dkv_acc)
    for half in range(2):
        cols = slice(half * HALF, (half + 1) * HALF)
        q_order = qo_ref[:, cols]
        for head in range(2):
            rows = slice(head * HD, (head + 1) * HD)
            q_t = q_ref[rows, cols]
            grad_t = grad_ref[rows, cols]
            log_total = log_ref[head : head + 1, cols]
            prob_dot = jnp.sum(
                mixed_ref[rows, cols] * grad_t.astype(F32), axis=0, keepdims=True
            )

            def quarter(z, dq):
                for k_half in range(half + 1):
                    keys = slice(k_half * HALF, (k_half + 1) * HALF)
                    k_t = kv_ref[z, 0:HD, keys]
                    v_t = kv_ref[z, HD : 2 * HD, keys]
                    probs = jnp.exp2(scores_of(k_t, q_t) * EXP2_SCALE - log_total)
                    if k_half == half:
                        allowed = ko_ref[z, keys, :] <= q_order
                        probs = jnp.where(allowed, probs, 0.0)
                    dkv_acc[z, HD : 2 * HD, keys] += dot(grad_t, probs.astype(BF16), 1, 1)
                    score_grad = (probs * (scores_of(v_t, grad_t) - prob_dot)).astype(BF16)
                    dkv_acc[z, 0:HD, keys] += dot(q_t, score_grad, 1, 1)
                    dq = dq + dot(k_t, score_grad)
                return dq

            dq = lax.fori_loop(0, QUARTERS, quarter, jnp.zeros((HD, HALF), F32))
            dq_ref[rows, cols] = dq * SCORE_SCALE
    for z in range(QUARTERS):
        dkv_ref[z, 0:HD, :] = (dkv_acc[z, 0:HD, :] * SCORE_SCALE).astype(BF16)
        dkv_ref[z, HD : 2 * HD, :] = dkv_acc[z, HD : 2 * HD, :].astype(BF16)


def attend_back(q_t, kv_t, q_order, k_order, mixed, log_total, mixed_grad):
    return pl.pallas_call(
        attend_back_kernel,
        out_shape=(
            jax.ShapeDtypeStruct((2 * HD, ROWS), F32),
            jax.ShapeDtypeStruct((QUARTERS, 2 * HD, ROWS), BF16),
        ),
        in_specs=[pl.BlockSpec(memory_space=pltpu.VMEM)] * 7,
        out_specs=(pl.BlockSpec(memory_space=pltpu.VMEM),) * 2,
        scratch_shapes=[pltpu.VMEM((QUARTERS, 2 * HD, ROWS), F32)],
        compiler_params=pltpu.CompilerParams(vmem_limit_bytes=40 * 2**20),
        cost_estimate=pl.CostEstimate(flops=4 * 10**9, bytes_accessed=6 * 10**6, transcendentals=6 * 10**6),
    )(q_t, kv_t, q_order, k_order, mixed, log_total, mixed_grad)


LINE_AXES = ("x", "core")


def line_gather(rows):
    width = rows.shape[1]
    parts = lax.all_gather(rows.reshape(2, BLK, width), LINE_AXES, axis=1)
    return parts.reshape(ROWS, width)


def line_scatter(partial):
    width = partial.shape[1]
    parts = partial.reshape(2, LINE, BLK, width).transpose(1, 0, 2, 3)
    return lax.psum_scatter(
        parts.reshape(LINE * 2 * BLK, width), LINE_AXES, scatter_dimension=0, tiled=True
    )


SWAP = [(a * 4 + b, b * 4 + a) for a in range(4) for b in range(4)]


def on_device(
    hidden_in,
    positions,
    block_of,
    attn_gain,
    query_weight,
    key_weight,
    value_weight,
    out_weight,
    query_gain,
    key_gain,
    ffn_gain,
    gate_weight,
    up_weight,
    down_weight,
    cotangent,
):
    z_at = lax.axis_index("z")
    x_at = lax.axis_index("x")
    core_at = lax.axis_index("core")
    place = x_at * 2 + core_at
    dp_at = lax.axis_index("dp")

    hidden_rows = hidden_in[0]
    grad_rows = cotangent[0]

    in_block = jnp.arange(BLK, dtype=jnp.int32)
    blocks = block_of.reshape(QUARTERS, LINE, 2).transpose(0, 2, 1)
    order_all = (blocks[..., None] * BLK + in_block).reshape(QUARTERS, ROWS)
    own_order = lax.dynamic_index_in_dim(order_all, z_at, 0, keepdims=True)
    k_order = order_all.reshape(QUARTERS, ROWS, 1)
    first_block = lax.dynamic_index_in_dim(block_of, 2 * (z_at * LINE + place), 0, keepdims=False)
    offset = positions[0, 0] - first_block * BLK
    frequency = ROPE_BASE ** (-2.0 * jnp.arange(HD // 2, dtype=F32) / HD)
    angles = (own_order + offset).astype(F32) * frequency[:, None]
    cosine, sine = jnp.cos(angles), jnp.sin(angles)

    gains = lax.all_gather(
        jnp.concatenate([attn_gain, ffn_gain, query_gain, key_gain]), "dp", axis=0
    ).astype(F32)
    attn_gain_all = gains[:, 0:256].reshape(1024)
    ffn_gain_all = gains[:, 256:512].reshape(1024)
    query_gain_all = gains[:, 512:528].reshape(HD)
    key_gain_all = gains[:, 528:544].reshape(HD)
    qkv_own = jnp.concatenate(
        [
            lax.dynamic_slice_in_dim(query_weight, place * 128, 128, axis=1),
            lax.dynamic_slice_in_dim(key_weight, place * 64, 64, axis=1),
            lax.dynamic_slice_in_dim(value_weight, place * 64, 64, axis=1),
        ],
        axis=1,
    )
    qkv_weight = lax.all_gather(qkv_own, "dp", axis=0, tiled=True)
    out_own = lax.dynamic_slice_in_dim(out_weight, core_at * 128 + x_at * 32, 32, axis=0)
    out_slice = lax.all_gather(
        lax.ppermute(out_own, ("dp", "x"), SWAP), "dp", axis=0, tiled=True
    )

    def ff_columns(weight):
        parts = weight.reshape(256, 4, LINE, 144)
        return lax.dynamic_slice_in_dim(parts, place, 1, axis=2).reshape(256, 576)

    gate_up = lax.all_gather(
        jnp.concatenate([ff_columns(gate_weight), ff_columns(up_weight)], axis=1),
        "dp",
        axis=0,
        tiled=True,
    )
    down_slice = lax.all_gather(
        lax.dynamic_slice_in_dim(down_weight, place * 144, 144, axis=0), "dp", axis=0, tiled=True
    )

    hidden = hidden_rows.astype(F32)
    line_hidden = line_gather(hidden_rows)
    attn_in = rms_scale(line_hidden.astype(F32), attn_gain_all).astype(BF16)
    qkv_t = dot(qkv_weight, attn_in, 0, 1)
    q_rot, q_back = jax.vjp(
        lambda r, g: head_norm_rope(r, g, cosine, sine),
        qkv_t[0:128].reshape(2, HD, ROWS),
        query_gain_all,
    )
    k_rot, k_back = jax.vjp(
        lambda r, g: head_norm_rope(r, g, cosine, sine),
        qkv_t[128:192].reshape(1, HD, ROWS),
        key_gain_all,
    )
    q_low = q_rot.reshape(128, ROWS).astype(BF16)
    kv_low = jnp.concatenate([k_rot.reshape(HD, ROWS), qkv_t[192:256]], axis=0).astype(BF16)
    kv_all = lax.all_gather(kv_low, "z", axis=0)
    mixed, attn_low, log_total = attend(q_low, kv_all, own_order, k_order)
    after_attn = hidden + line_scatter(dot(attn_low, out_slice, 0, 0).astype(BF16)).astype(F32)
    normed_ffn, norm_ffn_back = jax.vjp(rms_scale, after_attn, ffn_gain_all)
    ffn_in = line_gather(normed_ffn.astype(BF16))
    gate_up_proj = dot(ffn_in, gate_up)
    gate_proj = gate_up_proj[:, :576]
    up_proj = gate_up_proj[:, 576:]
    activated, swiglu_back = jax.vjp(lambda g, u: jax.nn.silu(g) * u, gate_proj, up_proj)
    activated_low = activated.astype(BF16)
    layer_out = (
        after_attn + line_scatter(dot(activated_low, down_slice).astype(BF16)).astype(F32)
    ).astype(BF16)

    residual_grad = grad_rows.astype(F32)
    branch_low = line_gather(grad_rows)
    activated_grad = dot(branch_low, down_slice, 1, 1)
    gate_grad, up_grad = swiglu_back(activated_grad)
    gate_up_grad = jnp.concatenate([gate_grad, up_grad], axis=1).astype(BF16)
    ffn_in_grad = line_scatter(dot(gate_up_grad, gate_up, 1, 1).astype(BF16)).astype(F32)
    mid_part, ffn_gain_part = norm_ffn_back(ffn_in_grad)
    mid_grad = residual_grad + mid_part
    branch_attn = line_gather(mid_grad.astype(BF16))
    mixed_grad = dot(out_slice, branch_attn, 1, 1).astype(BF16)
    q_grad, kv_grad_all = attend_back(
        q_low, kv_all, own_order, k_order, mixed, log_total, mixed_grad
    )
    kv_grad = lax.psum_scatter(kv_grad_all, "z", scatter_dimension=0, tiled=False).astype(F32)
    q_pre, q_gain_part = q_back(q_grad.reshape(2, HD, ROWS))
    k_pre, k_gain_part = k_back(kv_grad[0:HD].reshape(1, HD, ROWS))
    qkv_pre = jnp.concatenate(
        [q_pre.reshape(128, ROWS), k_pre.reshape(HD, ROWS), kv_grad[HD:]], axis=0
    ).astype(BF16)
    attn_in_grad = line_scatter(dot(qkv_pre, qkv_weight, 0, 1).astype(BF16)).astype(F32)
    unused, norm_attn_back = jax.vjp(rms_scale, hidden, attn_gain_all)
    hidden_part, attn_gain_part = norm_attn_back(attn_in_grad)
    input_grad = (mid_grad + hidden_part).astype(BF16)

    gain_sums = lax.psum(
        jnp.concatenate([attn_gain_part, ffn_gain_part, q_gain_part, k_gain_part]),
        ("dp", "z", "x", "core"),
    )

    def own_slice(begin, size):
        return lax.dynamic_slice_in_dim(gain_sums[begin : begin + size], dp_at * (size // 4), size // 4)

    def reduce_rows(part):
        rows = lax.psum_scatter(part.astype(BF16), "dp", scatter_dimension=0, tiled=True)
        return lax.psum_scatter(rows, "z", scatter_dimension=0, tiled=True)

    gate_up_rows = reduce_rows(dot(ffn_in, gate_up_grad, 0, 0))
    down_rows = reduce_rows(dot(activated_low, branch_low, 0, 0))
    out_rows = lax.ppermute(reduce_rows(dot(attn_low, branch_attn)), ("dp", "x"), SWAP)
    qkv_rows = reduce_rows(dot(attn_in, qkv_pre, 0, 1))
    ctx = ("z", "x", "core")
    gate_up_all = lax.all_gather(gate_up_rows, ctx, axis=0).reshape(4, LINE, 64, 2, 4, 144)
    gate_up_all = gate_up_all.transpose(3, 0, 2, 4, 1, 5).reshape(2, 256, 4608).astype(F32)
    down_all = lax.all_gather(down_rows, ctx, axis=0).reshape(4, LINE, 36, 1024)
    down_all = down_all.transpose(1, 0, 2, 3).reshape(1152, 1024).astype(F32)
    out_all = lax.all_gather(out_rows, ctx, axis=0).reshape(4, 4, 2, 8, 1024)
    out_all = out_all.transpose(2, 1, 0, 3, 4).reshape(256, 1024).astype(F32)
    qkv_all = lax.all_gather(qkv_rows, ctx, axis=0).reshape(4, LINE, 64, 256)
    qkv_all = qkv_all.transpose(0, 2, 1, 3).reshape(256, LINE, 256).astype(F32)
    return (
        layer_out[None],
        input_grad[None],
        own_slice(0, 1024),
        qkv_all[:, :, 0:128].reshape(256, 1024),
        qkv_all[:, :, 128:192].reshape(256, 512),
        qkv_all[:, :, 192:256].reshape(256, 512),
        out_all,
        own_slice(2048, 64),
        own_slice(2112, 64),
        own_slice(1024, 1024),
        gate_up_all[0],
        gate_up_all[1],
        down_all,
    )


def solution(mesh):
    fine = Mesh(mesh.devices.reshape(4, 4, 4, 2), ("dp", "z", "x", "core"))
    ctx = ("z", "x", "core")
    rows = P("dp", ctx, None)
    in_specs = (
        rows,
        P("dp", ctx),
        P(),
        P("dp"),
        P("dp", None),
        P("dp", None),
        P("dp", None),
        P("dp", None),
        P("dp"),
        P("dp"),
        P("dp"),
        P("dp", None),
        P("dp", None),
        P("dp", None),
        rows,
    )
    out_specs = (
        rows,
        rows,
        P("dp"),
        P("dp", None),
        P("dp", None),
        P("dp", None),
        P("dp", None),
        P("dp"),
        P("dp"),
        P("dp"),
        P("dp", None),
        P("dp", None),
        P("dp", None),
    )
    return jax.shard_map(
        on_device, mesh=fine, in_specs=in_specs, out_specs=out_specs, check_vma=False
    )
```

time: 2020 us -> 744 us (0.37)
  waiting for transfers between devices: 1330 us -> 338 us
  matrix products: 298 us -> 41.1 us
  blocking collectives: 189 us -> 140 us
  Pallas kernels: 0 us -> 31.9 us
    unnamed x37 -> x23, waiting for transfers between devices: 531 us -> 1.7 us
    all_gather x12 -> x10, waiting for transfers between devices: 435 us -> 126 us  [the longest x4 87.5 us: line_gather(): parts = lax.all_gather(rows.reshape(2, BLK, width), LINE_AXES, axis=1)]
    dot_general x93 -> x12, matrix products: 298 us -> 41.1 us  [dot(): lax.dot_general(left, right, (((left_dim,), (right_dim,)), ((), ())), pre...]
    reduce_scatter x7 -> x12, waiting for transfers between devices: 367 us -> 211 us  [the longest x4 78.2 us: reduce_rows(): lax.psum_scatter(part.astype(BF16), 'dp', scatter_dimension=0, tiled=True)]
    unnamed x125 -> x135, local copies, waits for them, and re-layouts: 110 us -> 21.7 us
    all_gather x6 -> x3, blocking collectives: 118 us -> 50.1 us  [the longest x1 30.2 us: on_device(): out_all = lax.all_gather(out_rows, ctx, axis=0).reshape(4, 4, 2, 8, 1024)]
    convert_element_type x1 -> x5, local copies, waits for them, and re-layouts: 0.84 us -> 35 us  [the longest x1 26.8 us: on_device(): gate_up_all.transpose(3, 0, 2, 4, 1, 5).reshape(2, 256, 4608).astype(F32)]
    slice x0 -> x13, local copies, waits for them, and re-layouts: none -> 33.2 us  [the longest x2 21.6 us: on_device(): gate_up_all[1]]
  transfers between devices with their start and end apart: 28 -> 25, of which waited for: 25 -> 16; matrix products, arithmetic and copies ran while one was open for 12% -> 14% of each run, Pallas kernels for 0% -> 0%
where the time goes in v1:
time: 744 us; the launch traced here: 735 us
  waiting for transfers between devices  338 us (45%)
  blocking collectives  140 us (19%)
  local copies, waits for them, and re-layouts  126 us (17%)
  matrix products  41.1 us (6%)
  other arithmetic  32.5 us (4%)
  Pallas kernels  31.9 us (4%)
  between operations  19.4 us (3%)
    all_gather x4, waiting for transfers between devices, line_gather(): parts = lax.all_gather(rows.reshape(2, BLK, width), LINE_AXES, axis=1)  87.5 us
    reduce_scatter x4, waiting for transfers between devices, reduce_rows(): lax.psum_scatter(part.astype(BF16), 'dp', scatter_dimension=0, tiled=True)  78.2 us
    psum x1, blocking collectives, on_device(): lax.psum(jnp.concatenate([attn_gain_part, ffn_gain_part, q_gain_part, k_g...  64.4 us
    reduce_scatter x3, waiting for transfers between devices, reduce_rows(): return lax.psum_scatter(rows, 'z', scatter_dimension=0, tiled=True)  61.3 us
    reduce_scatter x4, waiting for transfers between devices, line_scatter(): lax.psum_scatter(parts.reshape(LINE * 2 * BLK, width), LINE_AXES, scatter...  51.4 us
    dot_general x12, matrix products, dot(): lax.dot_general(left, right, (((left_dim,), (right_dim,)), ((), ())), pre...  41.1 us
    all_gather x1, blocking collectives, on_device(): out_all = lax.all_gather(out_rows, ctx, axis=0).reshape(4, 4, 2, 8, 1024)  30.2 us
    convert_element_type x1, local copies, waits for them, and re-layouts, on_device(): gate_up_all.transpose(3, 0, 2, 4, 1, 5).reshape(2, 256, 4608).astype(F32)  26.8 us
  transfers between devices with their start and end apart: 25, of which 16 were waited for; matrix products, arithmetic and copies ran while one was open for 14% of the time, Pallas kernels for 0%

profile of v1, /device:TPU:1, one launch (start us, length us, event | category | flops | bytes accessed | tf_op | source)
XLA Modules:
  0.0 735.5 jit_solution(9080693761837406284)
XLA Ops:
  11.5 3.4 add.242
  16.4 13.4 %all-reduce.4 = bf16[2176]{0:T(1024)(128)(2,1)S(1)} all-reduce(bf16[2176]{0:T(1024)(128)(2,1)S(1)} %dynamic-update-slice), channel_id=2, replica_groups=mesh['dp'=4,'z'=4,'x'=4,'core'=2] {'dp'}, use_global_device_ids=true, to_apply=%add.4 | all-reduce | flops 2176 | bytes 8704
  34.0 10.5 %all_gather.58 = bf16[1024,256]{1,0:T(8,128)(2,1)S(1)} all-gather(bf16[256,256]{1,0:T(8,128)(2,1)S(1)} %pad_maximum_fusion.9), channel_id=1, replica_groups=mesh['dp'=4,'z'=4,'x'=4,'core'=2] {'dp'}, dimensions={0}, use_global_device_ids=true | all-gather | bytes 655360 | tf_op jit(solution)/shard_map/all_gather | solution.py:225
  44.6 2.2 multiply_reduce_fusion
  46.9 2.1 fusion.2
  52.3 3.1 broadcast_add_fusion.ko_ref
  56.1 9.4 %all_gather.63 = bf16[128,1024]{1,0:T(8,128)(2,1)S(1)} all-gather(bf16[32,1024]{1,0:T(8,128)(2,1)S(1)} %collective-permute-done), channel_id=1, replica_groups=mesh['dp'=4,'z'=4,'x'=4,'core'=2] {'dp'}, dimensions={0}, use_global_device_ids=true | all-gather | bytes 327680 | tf_op jit(solution)/shard_map/all_gather | solution.py:227
  67.9 11.6 %all-gather.19.cloned.1.call-done.kv_ref = bf16[4,128,1024]{2,1,0:T(8,128)(2,1)} async-done(((bf16[1,128,1024]{2,1,0:T(8,128)(2,1)}), bf16[4,128,1024]{2,1,0:T(8,128)(2,1)}) %all-gather.19.cloned.1.call-update) | async-done | bytes 1048592 | tf_op jit(solution)/shard_map/all_gather | solution.py:261
  79.5 1.6 copy-done.2
  81.1 1.2 copy-done.5
  82.3 11.1 %shard_map.246 = (f32[128,1024]{1,0:T(8,128)S(1)}, bf16[128,1024]{1,0:T(8,128)(2,1)S(1)}, f32[2,1024]{1,0:T(2,128)S(1)}) custom-call(bf16[128,1024]{1,0:T(8,128)(2,1)S(1)} %bitcast.162, bf16[4,128,1024]{2,1,0:T(8,128)(2,1)S(1)} %copy-done.5, s32[1,1024]{1,0:T(1,128)S(1)} %get-tuple-element.59.qo_ref, s32[4,1024,1]{2,1,0:T(8,128)S(1)} %copy-done.2), custom_call_target="tpu_custom_call" | custom-call | flops 2000000000 | bytes 4000000 | tf_op jit(solution)/shard_map/pallas_call | solution.py:86
  94.2 1.5 copy.58
  95.8 4.3 copy.60
  100.1 4.3 copy.59
  107.1 20.8 %reduce-scatter.15.cloned.1.call-done = bf16[128,1024]{1,0:T(8,128)(2,1)} async-done(((bf16[1024,1024]{1,0:T(8,128)(2,1)}), bf16[128,1024]{1,0:T(8,128)(2,1)}) %reduce-scatter.15.cloned.1.call-update) | async-done | bytes 262160 | tf_op jit(solution)/shard_map/reduce_scatter | solution.py:165
  129.6 1.8 multiply_convert_fusion.1
  133.5 9.4 %all-gather.23.cloned.1.call-done = bf16[1024,1152]{0,1:T(8,128)(2,1)} async-done(((bf16[256,1152]{0,1:T(8,128)(2,1)}), bf16[1024,1152]{0,1:T(8,128)(2,1)}) %all-gather.23.cloned.1.call-update) | async-done | bytes 2359312 | tf_op jit(solution)/shard_map/all_gather | solution.py:235
  142.9 30.0 %all-gather.21.cloned.1.call-done = bf16[2,8,64,1024]{3,2,1,0:T(8,128)(2,1)} async-done(((bf16[2,1,64,1024]{3,2,1,0:T(8,128)(2,1)}), bf16[2,8,64,1024]{3,2,1,0:T(8,128)(2,1)}) %all-gather.21.cloned.1.call-update) | async-done | bytes 2097168 | tf_op jit(solution)/shard_map/all_gather | solution.py:158
  172.9 7.4 %fusion.56 = f32[1024,1152]{1,0:T(8,128)} fusion(bf16[1024,1024]{1,0:T(8,128)(2,1)} %bitcast.207, bf16[1024,1152]{0,1:T(8,128)(2,1)} %all-gather.23.cloned.1.call-done), kind=kOutput, calls=%fused_computation.141 | convolution fusion | flops 2415919104 | bytes 9175040 | tf_op jit(solution)/shard_map/dot_general | solution.py:28
  180.3 17.1 %all-gather.25.cloned.1.call-done = bf16[576,1024]{1,0:T(8,128)(2,1)} async-done(((bf16[144,1024]{1,0:T(8,128)(2,1)}), bf16[576,1024]{1,0:T(8,128)(2,1)}) %all-gather.25.cloned.1.call-update) | async-done | bytes 1179664 | tf_op jit(solution)/shard_map/all_gather | solution.py:241
  197.4 30.0 %all-gather.27.cloned.1.call-done = bf16[2,8,64,1024]{3,2,1,0:T(8,128)(2,1)} async-done(((bf16[2,1,64,1024]{3,2,1,0:T(8,128)(2,1)}), bf16[2,8,64,1024]{3,2,1,0:T(8,128)(2,1)}) %all-gather.27.cloned.1.call-update) | async-done | bytes 2097168 | tf_op jit(solution)/shard_map/all_gather | solution.py:158
  227.3 7.1 fusion.5
  234.4 3.2 convolution_convert_fusion.1
  237.7 1.6 copy.63
  239.3 30.5 %reduce-scatter.19.cloned.1.call-done = bf16[128,1024]{1,0:T(8,128)(2,1)} async-done(((bf16[1024,1024]{1,0:T(8,128)(2,1)}), bf16[128,1024]{1,0:T(8,128)(2,1)}) %reduce-scatter.19.cloned.1.call-update) | async-done | bytes 262160 | tf_op jit(solution)/shard_map/reduce_scatter | solution.py:165
  269.8 1.8 fusion.12
  272.3 2.0 fusion.49
  274.4 27.6 %all-gather.29.cloned.1.call-done = bf16[2,8,64,1024]{3,2,1,0:T(8,128)(2,1)} async-done(((bf16[2,1,64,1024]{3,2,1,0:T(8,128)(2,1)}), bf16[2,8,64,1024]{3,2,1,0:T(8,128)(2,1)}) %all-gather.29.cloned.1.call-update) | async-done | bytes 2097168 | tf_op jit(solution)/shard_map/all_gather | solution.py:158
  302.0 2.5 convolution_convert_fusion.8.grad_ref
  305.5 20.8 %shard_map.247 = (f32[128,1024]{1,0:T(8,128)S(1)}, bf16[4,128,1024]{2,1,0:T(8,128)(2,1)S(1)}) custom-call(bf16[128,1024]{1,0:T(8,128)(2,1)S(1)} %bitcast.163, bf16[4,128,1024]{2,1,0:T(8,128)(2,1)S(1)} %copy-done.6, s32[1,1024]{1,0:T(1,128)S(1)} %get-tuple-element.59.qo_ref, s32[4,1024,1]{2,1,0:T(8,128)S(1)} %copy-done.3, f32[128,1024]{1,0:T(8,128)S(1)} %copy-done.8, ...), custom_call_target="tpu_custom_call" | custom-call | flops 4000000000 | bytes 6000000 | tf_op jit(solution)/shard_map/pallas_call | solution.py:139
  329.2 20.1 %reduce-scatter.21.cloned.1.call-done = bf16[1,128,1024]{2,1,0:T(8,128)(2,1)} async-done(((bf16[4,128,1024]{2,1,0:T(8,128)(2,1)}), bf16[1,128,1024]{2,1,0:T(8,128)(2,1)}) %reduce-scatter.21.cloned.1.call-update) | async-done | bytes 262160 | tf_op jit(solution)/shard_map/reduce_scatter | solution.py:288
  351.3 3.3 convolution_convert_fusion.6
  354.7 6.2 convolution_convert_fusion
  361.0 4.6 convolution_convert_fusion.5
  365.6 1.2 convolution_convert_fusion.7
  366.9 8.7 %reduce-scatter.25.cloned.1.call-done = bf16[256,256]{1,0:T(8,128)(2,1)} async-done(((bf16[1024,256]{1,0:T(8,128)(2,1)}), bf16[256,256]{1,0:T(8,128)(2,1)}) %reduce-scatter.25.cloned.1.call-update) | async-done | bytes 131088 | tf_op jit(solution)/shard_map/reduce_scatter | solution.py:308
  375.6 36.2 %reduce-scatter.33.cloned.1.call-done = bf16[256,1152]{1,0:T(8,128)(2,1)} async-done(((bf16[1024,1152]{1,0:T(8,128)(2,1)}), bf16[256,1152]{1,0:T(8,128)(2,1)}) %reduce-scatter.33.cloned.1.call-update) | async-done | bytes 589840 | tf_op jit(solution)/shard_map/reduce_scatter | solution.py:308
  411.9 25.2 %reduce-scatter.37.cloned.1.call-done = bf16[144,1024]{1,0:T(8,128)(2,1)} async-done(((bf16[576,1024]{1,0:T(8,128)(2,1)}), bf16[144,1024]{1,0:T(8,128)(2,1)}) %reduce-scatter.37.cloned.1.call-update) | async-done | bytes 294928 | tf_op jit(solution)/shard_map/reduce_scatter | solution.py:308
  437.1 11.9 %fusion = bf16[40,1024]{1,0:T(8,128)(2,1)S(1)} fusion(bf16[144,1024]{1,0:T(8,128)(2,1)} %reduce-scatter.37.cloned.1.call-done), kind=kCustom, calls=%all-reduce-scatter | all-reduce-scatter fusion | flops 163841 | bytes 377344
  449.0 2.5 collective-permute-start.2
  451.5 8.1 %reduce-scatter.29.cloned.1.call-done = bf16[32,1024]{1,0:T(8,128)(2,1)} async-done(((bf16[128,1024]{1,0:T(8,128)(2,1)}), bf16[32,1024]{1,0:T(8,128)(2,1)}) %reduce-scatter.29.cloned.1.call-update) | async-done | bytes 65552 | tf_op jit(solution)/shard_map/reduce_scatter | solution.py:308
  461.9 20.9 %reduce-scatter.27.cloned.1.call-done = bf16[64,256]{1,0:T(8,128)(2,1)} async-done(((bf16[256,256]{1,0:T(8,128)(2,1)}), bf16[64,256]{1,0:T(8,128)(2,1)}) %reduce-scatter.27.cloned.1.call-update) | async-done | bytes 32784 | tf_op jit(solution)/shard_map/reduce_scatter | solution.py:309
  483.6 1.6 copy.64
  485.2 3.5 convolution_convert_fusion.3
  488.7 1.6 copy.61
  490.3 18.8 %reduce-scatter.35.cloned.1.call-done = bf16[64,1152]{1,0:T(8,128)(2,1)} async-done(((bf16[256,1152]{1,0:T(8,128)(2,1)}), bf16[64,1152]{1,0:T(8,128)(2,1)}) %reduce-scatter.35.cloned.1.call-update) | async-done | bytes 147472 | tf_op jit(solution)/shard_map/reduce_scatter | solution.py:309
  509.2 21.6 %reduce-scatter.31.cloned.1.call-done = bf16[8,1024]{1,0:T(8,128)(2,1)} async-done(((bf16[32,1024]{1,0:T(8,128)(2,1)}), bf16[8,1024]{1,0:T(8,128)(2,1)}) %reduce-scatter.31.cloned.1.call-update) | async-done | bytes 16400 | tf_op jit(solution)/shard_map/reduce_scatter | solution.py:309
  530.8 1.4 collective-permute-start.1
  532.2 4.7 copy_bitcast_fusion
  536.9 5.2 reshape.483
  542.1 30.2 %all-gather.2 = bf16[256,1024]{1,0:T(8,128)(2,1)S(1)} all-gather(bf16[8,1024]{1,0:T(8,128)(2,1)S(1)} %collective-permute-done.1), channel_id=4, replica_groups=mesh['dp'=4,'z'=4,'x'=4,'core'=2] {'z','x','core'}, dimensions={0}, use_global_device_ids=true | all-gather | bytes 540672 | tf_op jit(solution)/shard_map/all_gather | solution.py:320
  573.6 1.8 copy.65
  575.5 1.2 copy.80
  576.7 1.3 fusion.51
  578.0 1.6 copy.66
  582.0 1.2 fusion.13
  583.3 64.4 %psum.7 = f32[2176]{0:T(1024)S(1)} all-reduce(f32[2176]{0:T(1024)S(1)} %concatenate.47), channel_id=1, replica_groups=mesh['dp'=4,'z'=4,'x'=4,'core'=2] {'dp','z','x','core'}, use_global_device_ids=true, to_apply=%region_18.19 | all-reduce | flops 2176 | bytes 17408 | tf_op jit(solution)/shard_map/psum | solution.py:299
  650.3 2.2 fusion.22
  652.6 26.8 %reshape.484 = f32[4,8,64,2,4,144]{5,4,3,2,1,0:T(4,128)} reshape(bf16[2048,1152]{1,0:T(8,128)(2,1)} %all-gather.33.cloned.1.call-done) | data formatting | bytes 14155776 | tf_op jit(solution)/shard_map/convert_element_type | solution.py:317
  679.3 10.0 %fusion.50 = (f32[1,4,64,4,8,144]{5,3,0,2,4,1:T(4,128)}, f32[1,4,64,4,8,144]{5,3,0,2,4,1:T(4,128)S(1)}) fusion(f32[2,4,64,4,8,144]{5,3,0,2,4,1:T(4,128)} %bitcast.164), kind=kLoop, calls=%fused_computation.135 | loop fusion | bytes 18874368 | tf_op jit(solution)/shard_map/slice | solution.py:336
  689.3 8.2 %copy.69 = f32[1,4,64,4,8,144]{5,4,3,2,1,0:T(8,128)} copy(f32[1,4,64,4,8,144]{5,3,0,2,4,1:T(4,128)S(1)} %get-tuple-element.61) | data formatting | bytes 9437184 | tf_op jit(solution)/shard_map/slice | solution.py:335
  697.5 9.2 %squeeze.14 = f32[256,4608]{1,0:T(8,128)} reshape(f32[1,4,64,4,8,144]{5,4,3,2,1,0:T(8,128)} %copy.69) | data formatting | bytes 9437184 | tf_op jit(solution)/shard_map/squeeze | solution.py:335
  706.7 11.5 %copy.70 = f32[1,4,64,4,8,144]{5,4,3,2,1,0:T(8,128)} copy(f32[1,4,64,4,8,144]{5,3,0,2,4,1:T(4,128)} %get-tuple-element.60) | data formatting | bytes 9437184 | tf_op jit(solution)/shard_map/slice | solution.py:336
  718.3 9.2 %squeeze.15 = f32[256,4608]{1,0:T(8,128)} reshape(f32[1,4,64,4,8,144]{5,4,3,2,1,0:T(8,128)} %copy.70) | data formatting | bytes 9437184 | tf_op jit(solution)/shard_map/squeeze | solution.py:336
  (251 shorter events, 36.8 us)
Async XLA Ops:
  8.0 123.5 %copy-start = (bf16[1152,1024]{1,0:T(8,128)(2,1)S(1)}, bf16[1152,1024]{1,0:T(8,128)(2,1)}, u32[]{:S(2)}) copy-start(bf16[1152,1024]{1,0:T(8,128)(2,1)} %param.28) | copy-start | bytes 7077892
  8.0 6.8 copy-start.57
  8.0 22.5 %copy-start.55 = (s32[64]{0:T(128)S(1)}, s32[64]{0:T(128)}, u32[]{:S(2)}) copy-start(s32[64]{0:T(128)} %param.17) | copy-start | bytes 772
  8.1 8.1 %copy-start.48 = (bf16[16]{0:T(256)(128)(2,1)S(1)}, bf16[16]{0:T(256)(128)(2,1)}, u32[]{:S(2)}) copy-start(bf16[16]{0:T(256)(128)(2,1)} %param.24) | copy-start | bytes 100
  8.1 8.1 %copy-start.49 = (bf16[16]{0:T(256)(128)(2,1)S(1)}, bf16[16]{0:T(256)(128)(2,1)}, u32[]{:S(2)}) copy-start(bf16[16]{0:T(256)(128)(2,1)} %param.23) | copy-start | bytes 100
  8.1 8.1 %copy-start.50 = (bf16[256]{0:T(256)(128)(2,1)S(1)}, bf16[256]{0:T(256)(128)(2,1)}, u32[]{:S(2)}) copy-start(bf16[256]{0:T(256)(128)(2,1)} %param.25) | copy-start | bytes 1540
  8.1 8.1 %copy-start.51 = (bf16[256]{0:T(256)(128)(2,1)S(1)}, bf16[256]{0:T(256)(128)(2,1)}, u32[]{:S(2)}) copy-start(bf16[256]{0:T(256)(128)(2,1)} %param.18) | copy-start | bytes 1540
  8.1 23.9 %copy-start.56 = (s32[1,128]{1,0:T(1,128)S(1)}, s32[1,128]{1,0:T(1,128)}, u32[]{:S(2)}) copy-start(s32[1,128]{1,0:T(1,128)} %param.16) | copy-start | bytes 1540
  8.1 36.5 %all-gather.17.cloned.1.call-start = ((), (), s32[]{:S(2)}) async-start(), calls=%async_computation.12 | async-start | bytes 2359296 | tf_op jit(solution)/shard_map/all_gather | solution.py:158
  8.8 70.7 %all-gather.19.cloned.1.call-start = ((), (), s32[]{:S(2)}) async-start(), calls=%async_computation.13 | async-start | bytes 1310720 | tf_op jit(solution)/shard_map/all_gather | solution.py:261
  9.7 46.3 %collective-permute-start = (bf16[32,1024]{1,0:T(8,128)(2,1)S(1)}, bf16[32,1024]{1,0:T(8,128)(2,1)S(1)}, u32[]{:S(2)}, u32[]{:S(2)}) collective-permute-start(bf16[32,1024]{1,0:T(8,128)(2,1)S(1)} %constant_dynamic-slice_fusion.3), channel_id=1, source_target_pairs={{0,0},{2,32},{4,64},{6,96},{32,2},{34,34},{36,66},{38,98},{64,4},{... | collective-permute-start | bytes 196616 | tf_op jit(solution)/shard_map/ppermute | solution.py:228
  30.5 18.6 %copy-start.31 = (f32[1,2,4,128]{3,1,2,0:T(2,128)}, f32[1,2,4,128]{3,1,2,0:T(2,128)S(1)}, u32[]{:S(2)}) copy-start(f32[1,2,4,128]{3,1,2,0:T(2,128)S(1)} %copy.75) | copy-start | bytes 12292
  31.4 18.6 %copy-start.38 = (f32[64]{0:T(128)}, f32[64]{0:T(128)S(1)}, u32[]{:S(2)}) copy-start(f32[64]{0:T(128)S(1)} %mul.483) | copy-start | bytes 772
  32.1 23.4 %copy-start.42 = (f32[32]{0:T(128)}, f32[32]{0:T(128)S(1)}, u32[]{:S(2)}) copy-start(f32[32]{0:T(128)S(1)} %multiply_power_fusion) | copy-start | bytes 388
  44.6 4.5 copy-start.17
  44.6 10.8 %copy-start.27 = (f32[1,1024]{1,0:T(1,128)}, f32[1,1024]{1,0:T(1,128)S(1)}, u32[]{:S(2)}) copy-start(f32[1,1024]{1,0:T(1,128)S(1)} %get-tuple-element.58) | copy-start | bytes 12292
  49.9 5.5 copy-start.33
  50.8 4.6 copy-start.29
  52.3 75.7 %reduce-scatter.15.cloned.1.call-start = ((), (), s32[]{:S(2)}) async-start(), calls=%async_computation.14 | async-start | bytes 2359296 | tf_op jit(solution)/shard_map/reduce_scatter | solution.py:165
  56.0 23.5 %copy-start.21 = (f32[32,1024]{1,0:T(8,128)}, f32[32,1024]{1,0:T(8,128)S(1)}, u32[]{:S(2)}) copy-start(f32[32,1024]{1,0:T(8,128)S(1)} %get-tuple-element.86) | copy-start | bytes 393220
  56.1 11.7 %copy-start.36 = (f32[64]{0:T(128)}, f32[64]{0:T(128)S(1)}, u32[]{:S(2)}) copy-start(f32[64]{0:T(128)S(1)} %mul.460) | copy-start | bytes 772
  66.6 26.9 %copy-start.23 = (f32[2,1024]{1,0:T(2,128)}, f32[2,1024]{1,0:T(2,128)S(1)}, u32[]{:S(2)}) copy-start(f32[2,1024]{1,0:T(2,128)S(1)} %fusion.41) | copy-start | bytes 24580
  95.8 47.1 %all-gather.23.cloned.1.call-start = ((), (), s32[]{:S(2)}) async-start(), calls=%async_computation.16 | async-start | bytes 2949120 | tf_op jit(solution)/shard_map/all_gather | solution.py:235
  104.4 23.6 %copy-start.11 = (bf16[1,128,1024]{2,1,0:T(8,128)(2,1)S(1)}, bf16[1,128,1024]{2,1,0:T(8,128)(2,1)}, u32[]{:S(2)}) copy-start(bf16[1,128,1024]{2,1,0:T(8,128)(2,1)} %param.15) | copy-start | bytes 786436
  106.4 66.5 %all-gather.21.cloned.1.call-start = ((), (), s32[]{:S(2)}) async-start(), calls=%async_computation.15 | async-start | bytes 2359296 | tf_op jit(solution)/shard_map/all_gather | solution.py:158
  131.4 65.9 %all-gather.25.cloned.1.call-start = ((), (), s32[]{:S(2)}) async-start(), calls=%async_computation.17 | async-start | bytes 1474560 | tf_op jit(solution)/shard_map/all_gather | solution.py:241
  132.3 95.1 %all-gather.27.cloned.1.call-start = ((), (), s32[]{:S(2)}) async-start(), calls=%async_computation.19 | async-start | bytes 2359296 | tf_op jit(solution)/shard_map/all_gather | solution.py:158
  133.0 136.8 %reduce-scatter.19.cloned.1.call-start = ((), (), s32[]{:S(2)}) async-start(), calls=%async_computation.20 | async-start | bytes 2359296 | tf_op jit(solution)/shard_map/reduce_scatter | solution.py:165
  227.3 7.1 copy-start.53
  237.6 32.2 %copy-start.15 = (bf16[128,1024]{1,0:T(8,128)(2,1)S(1)}, bf16[128,1024]{1,0:T(8,128)(2,1)}, u32[]{:S(2)}) copy-start(bf16[128,1024]{1,0:T(8,128)(2,1)} %reduce-scatter.15.cloned.1.call-done) | copy-start | bytes 786436
  239.2 65.2 %copy-start.3 = (s32[4,1024,1]{2,1,0:T(8,128)S(1)}, s32[4,1024,1]{2,1,0:T(8,128)}, u32[]{:S(2)}) copy-start(s32[4,1024,1]{2,1,0:T(8,128)} %broadcast_add_fusion.ko_ref) | copy-start | bytes 49156
  239.2 62.7 %all-gather.29.cloned.1.call-start = ((), (), s32[]{:S(2)}) async-start(), calls=%async_computation.21 | async-start | bytes 2359296 | tf_op jit(solution)/shard_map/all_gather | solution.py:158
  274.3 75.0 %reduce-scatter.21.cloned.1.call-start = ((), (), s32[]{:S(2)}) async-start(), calls=%async_computation.22 | async-start | bytes 1310720 | tf_op jit(solution)/shard_map/reduce_scatter | solution.py:288
  327.3 48.2 %reduce-scatter.25.cloned.1.call-start = ((), (), s32[]{:S(2)}) async-start(), calls=%async_computation.24 | async-start | bytes 655360 | tf_op jit(solution)/shard_map/reduce_scatter | solution.py:308
  327.6 22.8 %copy-start.28 = (f32[1,1024]{1,0:T(1,128)S(1)}, f32[1,1024]{1,0:T(1,128)}, u32[]{:S(2)}) copy-start(f32[1,1024]{1,0:T(1,128)} %copy-done.27) | copy-start | bytes 12292
  328.7 21.7 %copy-start.43 = (f32[32]{0:T(128)S(1)}, f32[32]{0:T(128)}, u32[]{:S(2)}) copy-start(f32[32]{0:T(128)} %copy-done.42) | copy-start | bytes 388
  328.7 22.2 %copy-start.30 = (f32[1024]{0:T(1024)S(1)}, f32[1024]{0:T(1024)}, u32[]{:S(2)}) copy-start(f32[1024]{0:T(1024)} %copy-done.29) | copy-start | bytes 12292
  328.7 22.2 %copy-start.39 = (f32[64]{0:T(128)S(1)}, f32[64]{0:T(128)}, u32[]{:S(2)}) copy-start(f32[64]{0:T(128)} %copy-done.38) | copy-start | bytes 772
  328.8 22.3 %copy-start.34 = (f32[1024]{0:T(1024)S(1)}, f32[1024]{0:T(1024)}, u32[]{:S(2)}) copy-start(f32[1024]{0:T(1024)} %copy-done.33) | copy-start | bytes 12292
  354.6 57.2 %reduce-scatter.33.cloned.1.call-start = ((), (), s32[]{:S(2)}) async-start(), calls=%async_computation.28 | async-start | bytes 2949120 | tf_op jit(solution)/shard_map/reduce_scatter | solution.py:308
  360.9 76.2 %reduce-scatter.37.cloned.1.call-start = ((), (), s32[]{:S(2)}) async-start(), calls=%async_computation.30 | async-start | bytes 1474560 | tf_op jit(solution)/shard_map/reduce_scatter | solution.py:308
  361.0 4.7 copy-start.13
  365.5 94.2 %copy-start.47 = (u32[128]{0:T(128)S(1)}, u32[128]{0:T(128)}, u32[]{:S(2)}) copy-start(u32[128]{0:T(128)} %constant.106) | copy-start | bytes 1540
  365.6 117.3 %copy-start.18 = (bf16[1024,256]{1,0:T(8,128)(2,1)S(1)}, bf16[1024,256]{1,0:T(8,128)(2,1)}, u32[]{:S(2)}) copy-start(bf16[1024,256]{1,0:T(8,128)(2,1)} %copy-done.17) | copy-start | bytes 1572868
  365.6 94.1 %reduce-scatter.29.cloned.1.call-start = ((), (), s32[]{:S(2)}) async-start(), calls=%async_computation.26 | async-start | bytes 327680 | tf_op jit(solution)/shard_map/reduce_scatter | solution.py:308
  366.8 115.9 %reduce-scatter.27.cloned.1.call-start = ((), (), s32[]{:S(2)}) async-start(), calls=%async_computation.25 | async-start | bytes 163840 | tf_op jit(solution)/shard_map/reduce_scatter | solution.py:309
  375.6 133.6 %reduce-scatter.35.cloned.1.call-start = ((), (), s32[]{:S(2)}) async-start(), calls=%async_computation.29 | async-start | bytes 737280 | tf_op jit(solution)/shard_map/reduce_scatter | solution.py:309
  411.9 119.0 %reduce-scatter.31.cloned.1.call-start = ((), (), s32[]{:S(2)}) async-start(), calls=%async_computation.27 | async-start | bytes 81920 | tf_op jit(solution)/shard_map/reduce_scatter | solution.py:309
  449.0 12.0 %collective-permute-start.2 = (bf16[12,1024]{1,0:T(8,128)(2,1)S(1)}, bf16[12,1024]{1,0:T(8,128)(2,1)S(1)}, u32[]{:S(2)}, u32[]{:S(2)}) collective-permute-start(bf16[12,1024]{1,0:T(8,128)(2,1)S(1)} %slice.131), channel_id=1, source_target_pairs={{0,8},{8,16},{16,24},{1,9},{9,17},{17,25},{2,10},{10,18},{18,26},{... | collective-permute-start | bytes 73736
  459.7 72.5 %all-gather.35.cloned.1.call-start = ((), (), s32[]{:S(2)}) async-start(), calls=%async_computation.33 | async-start | bytes 2703360 | tf_op jit(solution)/shard_map/all_gather | solution.py:318
  461.8 111.7 %all-gather.31.cloned.1.call-start = ((), (), s32[]{:S(2)}) async-start(), calls=%async_computation.31 | async-start | bytes 1081344 | tf_op jit(solution)/shard_map/all_gather | solution.py:322
  482.8 99.3 %reduce-scatter.23.cloned.1.call-start = ((), (), s32[]{:S(2)}) async-start(), calls=%async_computation.23 | async-start | bytes 2359296 | tf_op jit(solution)/shard_map/reduce_scatter | solution.py:165
  485.2 165.1 %reduce-scatter.17.cloned.1.call-start = ((), (), s32[]{:S(2)}) async-start(), calls=%async_computation.18 | async-start | bytes 2359296 | tf_op jit(solution)/shard_map/reduce_scatter | solution.py:165
  488.7 20.5 %copy-start.52 = (f32[128]{0:T(128)S(1)}, f32[128]{0:T(128)}, u32[]{:S(2)}) copy-start(f32[128]{0:T(128)} %get-tuple-element.57) | copy-start | bytes 1540
  490.3 162.3 %all-gather.33.cloned.1.call-start = ((), (), s32[]{:S(2)}) async-start(), calls=%async_computation.32 | async-start | bytes 4866048 | tf_op jit(solution)/shard_map/all_gather | solution.py:316
  530.8 11.3 %collective-permute-start.1 = (bf16[8,1024]{1,0:T(8,128)(2,1)}, bf16[8,1024]{1,0:T(8,128)(2,1)S(1)}, u32[]{:S(2)}, u32[]{:S(2)}) collective-permute-start(bf16[8,1024]{1,0:T(8,128)(2,1)} %reduce-scatter.31.cloned.1.call-done), channel_id=1, source_target_pairs={{0,0},{2,32},{4,64},{6,96},{32,2},{34,34},{36,66},{38,98},{64,4},{... | collective-permute-start | bytes 49160 | tf_op jit(solution)/shard_map/ppermute | solution.py:313
  578.0 4.0 copy-start.12
  578.0 4.0 copy-start.32
  579.6 70.7 %copy-start.16 = (bf16[128,1024]{1,0:T(8,128)(2,1)S(1)}, bf16[128,1024]{1,0:T(8,128)(2,1)}, u32[]{:S(2)}) copy-start(bf16[128,1024]{1,0:T(8,128)(2,1)} %reduce-scatter.15.cloned.1.call-done) | copy-start | bytes 786436
  579.6 70.7 %copy-start.19 = (bf16[1,128,1024]{2,1,0:T(8,128)(2,1)S(1)}, bf16[1,128,1024]{2,1,0:T(8,128)(2,1)}, u32[]{:S(2)}) copy-start(bf16[1,128,1024]{2,1,0:T(8,128)(2,1)} %param.29) | copy-start | bytes 786436
  579.6 70.7 %copy-start.20 = (bf16[128,1024]{1,0:T(8,128)(2,1)S(1)}, bf16[128,1024]{1,0:T(8,128)(2,1)}, u32[]{:S(2)}) copy-start(bf16[128,1024]{1,0:T(8,128)(2,1)} %reduce-scatter.19.cloned.1.call-done) | copy-start | bytes 786436
  579.6 70.7 %copy-start.41 = (f32[128]{0:T(128)S(1)}, f32[128]{0:T(128)}, u32[]{:S(2)}) copy-start(f32[128]{0:T(128)} %copy-done.40) | copy-start | bytes 1540
  579.6 70.7 %copy-start.45 = (f32[128]{0:T(128)S(1)}, f32[128]{0:T(128)}, u32[]{:S(2)}) copy-start(f32[128]{0:T(128)} %copy-done.44) | copy-start | bytes 1540
  718.3 9.2 %copy-start.1 = (bf16[1152,1024]{1,0:T(8,128)(2,1)S(1)}, bf16[1152,1024]{1,0:T(8,128)(2,1)}, u32[]{:S(2)}) copy-start(bf16[1152,1024]{1,0:T(8,128)(2,1)} %param.28) | copy-start | bytes 7077892
  (22 other events, 41.5 us)
Sparse Core Ops, SparseCore 0:
  10.6 28.7 all-gather.16
  52.4 27.0 all-gather.18
  95.9 31.9 reduce-scatter.14
  239.3 30.4 reduce-scatter.18
  327.5 21.7 reduce-scatter.20
  463.0 48.2 all-gather.34
  513.6 41.7 all-gather.30
  557.6 48.8 all-gather.32
Sparse Core Ops, SparseCore 1:
  106.5 36.4 all-gather.22
  145.0 27.8 all-gather.20
  175.0 22.3 all-gather.24
  199.1 28.2 all-gather.26
  274.4 27.5 all-gather.28
  354.7 20.8 reduce-scatter.24
  378.5 33.3 reduce-scatter.32
  414.9 22.2 reduce-scatter.36
  440.1 19.5 reduce-scatter.28
  462.0 20.7 reduce-scatter.26
  485.1 24.0 reduce-scatter.34
  511.7 19.1 reduce-scatter.30
  533.7 33.3 reduce-scatter.22
  570.1 38.3 reduce-scatter.16

commit v2 on v1

v2 whole, which is shorter than its diff:
```python
import functools

import jax
import jax.numpy as jnp
import numpy as np
from jax import lax
from jax.experimental import pallas as pl
from jax.experimental.pallas import tpu as pltpu
from jax.sharding import Mesh, PartitionSpec as P

HD = 64
BLK = 64
GROUPS = 8
HALF = 256
ROWS = 512
PIECE = 528

NORM_EPS = 1e-05
ROPE_BASE = 1000000.0
EXP2_SCALE = float(HD**-0.5 * np.log2(np.e))
SCORE_SCALE = HD**-0.5

F32 = jnp.float32
BF16 = jnp.bfloat16
VMEM = pl.BlockSpec(memory_space=pltpu.VMEM)
ANY = pl.BlockSpec(memory_space=pl.ANY)


def dot(left, right, left_dim=1, right_dim=0):
    return lax.dot_general(
        left, right, (((left_dim,), (right_dim,)), ((), ())), preferred_element_type=F32
    )


def rms_scale(values, gain):
    return values * lax.rsqrt(jnp.mean(values * values, axis=-1, keepdims=True) + NORM_EPS) * gain


def head_norm_rope(raw, gain, cosine, sine):
    scaled = (
        raw
        * lax.rsqrt(jnp.mean(raw * raw, axis=1, keepdims=True) + NORM_EPS)
        * gain[None, :, None]
    )
    front = scaled[:, : HD // 2]
    back = scaled[:, HD // 2 :]
    return jnp.concatenate([front * cosine - back * sine, back * cosine + front * sine], axis=1)


def scores_of(keys_t, queries_t):
    return dot(keys_t, queries_t, 0, 0)


def head_pair(ref, kv_head, cols):
    first = 2 * kv_head * HD
    return jnp.concatenate(
        [ref[first : first + HD, cols], ref[first + HD : first + 2 * HD, cols]], axis=1
    )


def attend_kernel(q_ref, kv_ref, qo_ref, ko_ref, mixed_ref, low_ref, log_ref):
    for half in range(2):
        cols = slice(half * HALF, (half + 1) * HALF)
        q_order = jnp.concatenate([qo_ref[:, cols]] * 2, axis=1)
        for kv_head in range(2):
            q_t = head_pair(q_ref, kv_head, cols)

            def group(g, carried):
                acc, total = carried
                for k_half in range(half + 1):
                    keys = slice(k_half * HALF, (k_half + 1) * HALF)
                    probs = jnp.exp2(
                        scores_of(kv_ref[g, kv_head, 0:HD, keys], q_t) * EXP2_SCALE
                    )
                    if k_half == half:
                        allowed = ko_ref[g, keys, :] <= q_order
                        probs = jnp.where(allowed, probs, 0.0)
                    total = total + jnp.sum(probs, axis=0, keepdims=True)
                    acc = acc + dot(kv_ref[g, kv_head, HD : 2 * HD, keys], probs.astype(BF16))
                return acc, total

            acc, total = lax.fori_loop(
                0,
                GROUPS,
                group,
                (jnp.zeros((HD, 2 * HALF), F32), jnp.zeros((1, 2 * HALF), F32)),
            )
            mixed = acc / total
            logs = jnp.log2(total)
            for head in range(2):
                at = 2 * kv_head + head
                rows = slice(at * HD, (at + 1) * HD)
                part = mixed[:, head * HALF : (head + 1) * HALF]
                mixed_ref[rows, cols] = part
                low_ref[rows, cols] = part.astype(BF16)
                log_ref[at : at + 1, cols] = logs[:, head * HALF : (head + 1) * HALF]


def attend(q_t, kv_all, q_order, k_order):
    return pl.pallas_call(
        attend_kernel,
        out_shape=(
            jax.ShapeDtypeStruct((4 * HD, ROWS), F32),
            jax.ShapeDtypeStruct((4 * HD, ROWS), BF16),
            jax.ShapeDtypeStruct((4, ROWS), F32),
        ),
        in_specs=[VMEM] * 4,
        out_specs=(VMEM,) * 3,
        compiler_params=pltpu.CompilerParams(vmem_limit_bytes=40 * 2**20),
        cost_estimate=pl.CostEstimate(
            flops=2 * 10**9, bytes_accessed=4 * 10**6, transcendentals=6 * 10**6
        ),
    )(q_t, kv_all, q_order, k_order)


def attend_back_kernel(
    q_ref, kv_ref, qo_ref, ko_ref, mixed_ref, log_ref, grad_ref, dq_ref, dkv_ref, dkv_acc
):
    dkv_acc[...] = jnp.zeros_like(dkv_acc)
    for half in range(2):
        cols = slice(half * HALF, (half + 1) * HALF)
        q_order = jnp.concatenate([qo_ref[:, cols]] * 2, axis=1)
        for kv_head in range(2):
            q_t = head_pair(q_ref, kv_head, cols)
            grad_t = head_pair(grad_ref, kv_head, cols)
            at = 2 * kv_head
            log_total = jnp.concatenate(
                [log_ref[at : at + 1, cols], log_ref[at + 1 : at + 2, cols]], axis=1
            )
            prob_dot = jnp.sum(
                head_pair(mixed_ref, kv_head, cols) * grad_t.astype(F32), axis=0, keepdims=True
            )

            def group(g, dq):
                for k_half in range(half + 1):
                    keys = slice(k_half * HALF, (k_half + 1) * HALF)
                    k_t = kv_ref[g, kv_head, 0:HD, keys]
                    v_t = kv_ref[g, kv_head, HD : 2 * HD, keys]
                    probs = jnp.exp2(scores_of(k_t, q_t) * EXP2_SCALE - log_total)
                    if k_half == half:
                        allowed = ko_ref[g, keys, :] <= q_order
                        probs = jnp.where(allowed, probs, 0.0)
                    dkv_acc[g, kv_head, HD : 2 * HD, keys] += dot(
                        grad_t, probs.astype(BF16), 1, 1
                    )
                    score_grad = (probs * (scores_of(v_t, grad_t) - prob_dot)).astype(BF16)
                    dkv_acc[g, kv_head, 0:HD, keys] += dot(q_t, score_grad, 1, 1)
                    dq = dq + dot(k_t, score_grad)
                return dq

            dq = lax.fori_loop(0, GROUPS, group, jnp.zeros((HD, 2 * HALF), F32))
            for head in range(2):
                rows = slice((at + head) * HD, (at + head + 1) * HD)
                dq_ref[rows, cols] = dq[:, head * HALF : (head + 1) * HALF] * SCORE_SCALE

    def finish(g, unused):
        for kv_head in range(2):
            dkv_ref[g, kv_head, 0:HD, :] = (dkv_acc[g, kv_head, 0:HD, :] * SCORE_SCALE).astype(
                BF16
            )
            dkv_ref[g, kv_head, HD : 2 * HD, :] = dkv_acc[g, kv_head, HD : 2 * HD, :].astype(BF16)
        return unused

    lax.fori_loop(0, GROUPS, finish, 0)


def attend_back(q_t, kv_all, q_order, k_order, mixed, log_total, mixed_grad):
    return pl.pallas_call(
        attend_back_kernel,
        out_shape=(
            jax.ShapeDtypeStruct((4 * HD, ROWS), F32),
            jax.ShapeDtypeStruct((GROUPS, 2, 2 * HD, ROWS), BF16),
        ),
        in_specs=[VMEM] * 7,
        out_specs=(VMEM,) * 2,
        scratch_shapes=[pltpu.VMEM((GROUPS, 2, 2 * HD, ROWS), F32)],
        compiler_params=pltpu.CompilerParams(vmem_limit_bytes=40 * 2**20),
        cost_estimate=pl.CostEstimate(
            flops=4 * 10**9, bytes_accessed=6 * 10**6, transcendentals=6 * 10**6
        ),
    )(q_t, kv_all, q_order, k_order, mixed, log_total, mixed_grad)


def ring(axis):
    me = lax.axis_index(axis)
    return me, lax.rem(me + 1, 4), lax.rem(me + 2, 4), lax.rem(me + 3, 4)


def meet(partners):
    barrier = pltpu.get_barrier_semaphore()
    for partner in partners:
        pl.semaphore_signal(
            barrier, inc=1, device_id=partner, device_id_type=pl.DeviceIdType.MESH
        )
    pl.semaphore_wait(barrier, len(partners))


class Sends:
    def __init__(self, send_sems, recv_sems):
        self.send_sems, self.recv_sems, self.started = send_sems, recv_sems, []

    def __call__(self, source, target, partner):
        at = len(self.started)
        copy = pltpu.make_async_remote_copy(
            src_ref=source,
            dst_ref=target,
            send_sem=self.send_sems.at[at],
            recv_sem=self.recv_sems.at[at],
            device_id=partner,
            device_id_type=pl.DeviceIdType.MESH,
        )
        copy.start()
        self.started.append(copy)
        return copy

    def finish(self):
        for copy in self.started:
            copy.wait_send()


def gather_kernel(axis, sibling, at, src, out, send_sems, recv_sems, local_sems):
    me, right, far, left = ring(axis)
    core = lax.axis_index("core")
    to_right, to_left, to_sib = {axis: right}, {axis: left}, {"core": 1 - core}
    meet([to_right, to_left] + ([to_sib] if sibling else []))
    send = Sends(send_sems, recv_sems)
    from_sib = []

    def share(place, half, source=None):
        if sibling:
            target = at(out, place, core, half)
            from_sib.append(send(target if source is None else source, target, to_sib))

    def own_to(half, partner):
        return send(src.at[half], at(out, me, core, half), partner)

    right0 = own_to(0, to_right)
    left1 = own_to(1, to_left)
    right1 = own_to(1, to_right)
    left0 = own_to(0, to_left)
    own = [
        pltpu.make_async_copy(src.at[h], at(out, me, core, h), local_sems.at[h]) for h in range(2)
    ]
    for copy in own:
        copy.start()
    for h in range(2):
        share(me, h, src.at[h])
    right0.wait_recv()
    far0 = send(at(out, left, core, 0), at(out, left, core, 0), to_right)
    share(left, 0)
    left1.wait_recv()
    far1 = send(at(out, right, core, 1), at(out, right, core, 1), to_left)
    share(right, 1)
    right1.wait_recv()
    share(left, 1)
    left0.wait_recv()
    share(right, 0)
    far0.wait_recv()
    share(far, 0)
    far1.wait_recv()
    share(far, 1)
    for copy in from_sib:
        copy.wait_recv()
    for copy in own:
        copy.wait()
    send.finish()


def gather_call(kernel_id, axis, sibling, at, src, out_shape):
    return pl.pallas_call(
        functools.partial(gather_kernel, axis, sibling, at),
        out_shape=jax.ShapeDtypeStruct(out_shape, BF16),
        in_specs=[ANY],
        out_specs=ANY,
        scratch_shapes=[
            pltpu.SemaphoreType.DMA((14 if sibling else 6,)),
            pltpu.SemaphoreType.DMA((14 if sibling else 6,)),
            pltpu.SemaphoreType.DMA((2,)),
        ],
        compiler_params=pltpu.CompilerParams(collective_id=kernel_id, has_side_effects=True),
    )(src)


def line_gather(kernel_id, rows):
    width = rows.shape[1]
    gathered = gather_call(
        kernel_id,
        "x",
        False,
        lambda out, place, core, half: out.at[half, place],
        rows.reshape(2, BLK, width),
        (2, 4, BLK, width),
    )
    return gathered.reshape(ROWS, width)


def sequence_gather(kernel_id, kv):
    gathered = gather_call(
        kernel_id,
        "z",
        True,
        lambda out, place, core, half: out.at[place, core, half],
        kv,
        (4, 2, 2, 2 * HD, ROWS),
    )
    return gathered.reshape(GROUPS, 2, 2 * HD, ROWS)


def add_low(left, right):
    return (left.astype(F32) + right.astype(F32)).astype(BF16)


def line_scatter_kernel(part, out, pair, self_rows, far_in, left_in, right_in, sends, recvs, loads):
    me, right, far, left = ring("x")
    to_right, to_left = {"x": right}, {"x": left}
    local = [
        pltpu.make_async_copy(part.at[0, right], pair.at[0], loads.at[0]),
        pltpu.make_async_copy(part.at[1, left], pair.at[1], loads.at[1]),
        pltpu.make_async_copy(part.at[0, me], self_rows.at[0], loads.at[2]),
        pltpu.make_async_copy(part.at[1, me], self_rows.at[1], loads.at[3]),
    ]
    for copy in local:
        copy.start()
    meet([to_right, to_left])
    send = Sends(sends, recvs)
    far0 = send(part.at[0, far], far_in.at[0], to_right)
    far1 = send(part.at[1, far], far_in.at[1], to_left)
    right1 = send(part.at[1, right], left_in.at[1], to_right)
    left0 = send(part.at[0, left], right_in.at[0], to_left)
    local[0].wait()
    far0.wait_recv()
    pair[0] = add_low(pair[0], far_in[0])
    right0 = send(pair.at[0], left_in.at[0], to_right)
    local[1].wait()
    far1.wait_recv()
    pair[1] = add_low(pair[1], far_in[1])
    left1 = send(pair.at[1], right_in.at[1], to_left)
    local[2].wait()
    local[3].wait()
    right1.wait_recv()
    left0.wait_recv()
    right0.wait_recv()
    left1.wait_recv()
    for h in range(2):
        out[h] = (
            self_rows[h].astype(F32) + left_in[h].astype(F32) + right_in[h].astype(F32)
        )
    send.finish()


def line_scatter(kernel_id, partial):
    width = partial.shape[1]
    buffer = pltpu.VMEM((2, BLK, width), BF16)
    return pl.pallas_call(
        line_scatter_kernel,
        out_shape=jax.ShapeDtypeStruct((2, BLK, width), F32),
        in_specs=[ANY],
        out_specs=VMEM,
        scratch_shapes=[buffer] * 5
        + [
            pltpu.SemaphoreType.DMA((6,)),
            pltpu.SemaphoreType.DMA((6,)),
            pltpu.SemaphoreType.DMA((4,)),
        ],
        compiler_params=pltpu.CompilerParams(
            collective_id=kernel_id, has_side_effects=True, vmem_limit_bytes=32 * 2**20
        ),
    )(partial.reshape(2, 4, BLK, width)).reshape(2 * BLK, width)


class RingSum:
    def __init__(self, send, axis, chunk, far_in, left_in, right_in):
        self.send, self.chunk = send, chunk
        self.far_in, self.left_in, self.right_in = far_in, left_in, right_in
        self.me, self.right, self.far, self.left = ring(axis)
        self.to_right, self.to_left = {axis: self.right}, {axis: self.left}

    def begin(self):
        send, chunk = self.send, self.chunk
        self.far0 = send(chunk(self.far, 0), self.far_in(0), self.to_right)
        self.far1 = send(chunk(self.far, 1), self.far_in(1), self.to_left)
        self.right1 = send(chunk(self.right, 1), self.left_in(1), self.to_right)
        self.left0 = send(chunk(self.left, 0), self.right_in(0), self.to_left)

    def middle(self):
        send, chunk = self.send, self.chunk
        self.far0.wait_recv()
        mine = chunk(self.right, 0)
        mine[...] = add_low(mine[...], self.far_in(0)[...])
        self.right0 = send(mine, self.left_in(0), self.to_right)
        self.far1.wait_recv()
        mine = chunk(self.left, 1)
        mine[...] = add_low(mine[...], self.far_in(1)[...])
        self.left1 = send(mine, self.right_in(1), self.to_left)

    def end(self, store):
        self.right1.wait_recv()
        self.left0.wait_recv()
        self.right0.wait_recv()
        self.left1.wait_recv()
        for h in range(2):
            store(
                h,
                self.chunk(self.me, h)[...].astype(F32)
                + self.left_in(h)[...].astype(F32)
                + self.right_in(h)[...].astype(F32),
            )


def sequence_scatter_kernel(
    part, out, own, other, far_in, left_in, right_in, sends, recvs, loads
):
    core = lax.axis_index("core")
    me, right, far, left = ring("z")
    order = (far, right, left, me)
    local = [
        pltpu.make_async_copy(part.at[place, core], own.at[place], loads.at[i])
        for i, place in enumerate(order)
    ]
    for copy in local:
        copy.start()
    to_sib = {"core": 1 - core}
    meet([{"z": right}, {"z": left}, to_sib])
    send = Sends(sends, recvs)
    shared = [send(part.at[place, 1 - core], other.at[place], to_sib) for place in order]

    def merge(i):
        local[i].wait()
        shared[i].wait_recv()
        own[order[i]] = add_low(own[order[i]], other[order[i]])

    ring_sum = RingSum(
        send,
        "z",
        lambda place, h: own.at[place, h],
        lambda h: far_in.at[h],
        lambda h: left_in.at[h],
        lambda h: right_in.at[h],
    )
    for i in range(3):
        merge(i)
    ring_sum.begin()
    merge(3)
    ring_sum.middle()

    def store(h, value):
        out[h] = value

    ring_sum.end(store)
    send.finish()


def sequence_scatter(kernel_id, partial):
    buffer = pltpu.VMEM((2, 2 * HD, ROWS), BF16)
    wide = pltpu.VMEM((4, 2, 2 * HD, ROWS), BF16)
    return pl.pallas_call(
        sequence_scatter_kernel,
        out_shape=jax.ShapeDtypeStruct((2, 2 * HD, ROWS), F32),
        in_specs=[ANY],
        out_specs=VMEM,
        scratch_shapes=[wide, wide, buffer, buffer, buffer]
        + [
            pltpu.SemaphoreType.DMA((10,)),
            pltpu.SemaphoreType.DMA((10,)),
            pltpu.SemaphoreType.DMA((4,)),
        ],
        compiler_params=pltpu.CompilerParams(
            collective_id=kernel_id, has_side_effects=True, vmem_limit_bytes=32 * 2**20
        ),
    )(partial.reshape(4, 2, 2, 2 * HD, ROWS))


def grads_kernel(
    gu, qkv, down, out, result,
    gu_own, gu_sib, qkv_own, qkv_sib, down_own, down_sib, out_own, out_sib,
    packed, far_a, left_a, right_a, mid, far_b, left_b, right_b,
    sends, recvs, loads,
):
    core = lax.axis_index("core")
    me_y, right_y, far_y, left_y = ring("dp")
    me_z, right_z, far_z, left_z = ring("z")
    to_sib = {"core": 1 - core}
    views = [
        (lambda c: gu.at[:, :, c], gu_own, gu_sib),
        (lambda c: qkv.at[:, :, c], qkv_own, qkv_sib),
        (lambda c: down.at[:, c], down_own, down_sib),
        (lambda c: out.at[:, c], out_own, out_sib),
    ]
    local = [
        pltpu.make_async_copy(view(core), mine, loads.at[i])
        for i, (view, mine, unused) in enumerate(views)
    ]
    for copy in local:
        copy.start()
    meet([{"dp": right_y}, {"dp": left_y}, {"z": right_z}, {"z": left_z}, to_sib])
    send = Sends(sends, recvs)
    shared = [send(view(1 - core), theirs, to_sib) for view, unused, theirs in views]
    for copy in local:
        copy.wait()
    for copy in shared:
        copy.wait_recv()

    def pack(y, unused):
        for z in range(4):
            for s in range(2):
                for t in range(9):
                    cols = slice(s * 1152 + t * 128, s * 1152 + (t + 1) * 128)
                    packed[s, y, z, t * 32 : (t + 1) * 32, :] = add_low(
                        gu_own[y, z, :, cols], gu_sib[y, z, :, cols]
                    )
                for t in range(2):
                    cols = slice(s * 256 + t * 128, s * 256 + (t + 1) * 128)
                    packed[s, y, z, 288 + t * 32 : 320 + t * 32, :] = add_low(
                        qkv_own[y, z, :, cols], qkv_sib[y, z, :, cols]
                    )
                cols = slice(s * 512 + z * 128, s * 512 + (z + 1) * 128)
                packed[s, y, z, 352:496, :] = add_low(down_own[y, :, cols], down_sib[y, :, cols])
                packed[s, y, z, 496:528, :] = add_low(out_own[y, :, cols], out_sib[y, :, cols])
        return unused

    lax.fori_loop(0, 4, pack, 0)

    two = (pl.ds(0, 2), pl.ds(2, 2))
    rows = (pl.ds(0, 272), pl.ds(272, 256))
    first = [
        RingSum(
            send,
            "dp",
            lambda place, h: packed.at[0, place, two[h]],
            lambda h: far_a.at[0, h],
            lambda h: left_a.at[0, h],
            lambda h: right_a.at[0, h],
        ),
        RingSum(
            send,
            "z",
            lambda place, h: packed.at[1, two[h], place],
            lambda h: far_a.at[1, h],
            lambda h: left_a.at[1, h],
            lambda h: right_a.at[1, h],
        ),
    ]
    second = [
        RingSum(
            send,
            axis,
            lambda place, h, s=s: mid.at[s, place, rows[h]],
            lambda h, s=s: far_b.at[s, rows[h]],
            lambda h, s=s: left_b.at[s, rows[h]],
            lambda h, s=s: right_b.at[s, rows[h]],
        )
        for s, axis in enumerate(("z", "dp"))
    ]
    for step in first:
        step.begin()
    for step in first:
        step.middle()
    for s in range(2):

        def keep(h, value, s=s):
            mid[s, 2 * h : 2 * h + 2] = value.astype(BF16)

        first[s].end(keep)
        second[s].begin()
    for step in second:
        step.middle()
    for s in range(2):

        def keep_last(h, value, s=s):
            result[s, rows[h], :] = value.astype(BF16)

        second[s].end(keep_last)
    send.finish()


def sum_grads(kernel_id, gu, qkv, down, out):
    def vm(*shape):
        return pltpu.VMEM(shape, BF16)

    return pl.pallas_call(
        grads_kernel,
        out_shape=jax.ShapeDtypeStruct((2, PIECE, 128), BF16),
        in_specs=[ANY] * 4,
        out_specs=VMEM,
        scratch_shapes=[
            vm(4, 4, 32, 2304), vm(4, 4, 32, 2304),
            vm(4, 4, 32, 512), vm(4, 4, 32, 512),
            vm(4, 144, 1024), vm(4, 144, 1024),
            vm(4, 32, 1024), vm(4, 32, 1024),
            vm(2, 4, 4, PIECE, 128),
            vm(2, 2, 2, PIECE, 128), vm(2, 2, 2, PIECE, 128), vm(2, 2, 2, PIECE, 128),
            vm(2, 4, PIECE, 128),
            vm(2, PIECE, 128), vm(2, PIECE, 128), vm(2, PIECE, 128),
            pltpu.SemaphoreType.DMA((28,)),
            pltpu.SemaphoreType.DMA((28,)),
            pltpu.SemaphoreType.DMA((4,)),
        ],
        compiler_params=pltpu.CompilerParams(
            collective_id=kernel_id, has_side_effects=True, vmem_limit_bytes=48 * 2**20
        ),
    )(
        gu.reshape(4, 4, 2, 32, 2304),
        qkv.reshape(4, 4, 2, 32, 512),
        down.reshape(4, 2, 144, 1024),
        out.reshape(4, 2, 32, 1024),
    )


class RingCopy:
    def __init__(self, send, axis, place_of):
        self.send, self.at = send, place_of
        self.me, self.right, self.far, self.left = ring(axis)
        self.to_right, self.to_left = {axis: self.right}, {axis: self.left}

    def begin(self):
        me = self.me
        self.right0 = self.send(self.at(me, 0), self.at(me, 0), self.to_right)
        self.left1 = self.send(self.at(me, 1), self.at(me, 1), self.to_left)
        self.right1 = self.send(self.at(me, 1), self.at(me, 1), self.to_right)
        self.left0 = self.send(self.at(me, 0), self.at(me, 0), self.to_left)

    def middle(self):
        self.right0.wait_recv()
        self.far0 = self.send(self.at(self.left, 0), self.at(self.left, 0), self.to_right)
        self.left1.wait_recv()
        self.far1 = self.send(self.at(self.right, 1), self.at(self.right, 1), self.to_left)

    def near(self):
        self.right1.wait_recv()
        self.left0.wait_recv()

    def end(self):
        self.far0.wait_recv()
        self.far1.wait_recv()


def spread_kernel(piece, out, sends, recvs, loads):
    core = lax.axis_index("core")
    me_x, right_x, far_x, left_x = ring("x")
    me_z, right_z, far_z, left_z = ring("z")
    to_sib = {"core": 1 - core}
    own = [
        pltpu.make_async_copy(piece.at[s], out.at[s, core, me_z, me_x], loads.at[s])
        for s in range(2)
    ]
    for copy in own:
        copy.start()
    meet([{"x": right_x}, {"x": left_x}, {"z": right_z}, {"z": left_z}, to_sib])
    send = Sends(sends, recvs)
    rows = (pl.ds(0, 272), pl.ds(272, 256))
    two = (pl.ds(0, 2), pl.ds(2, 2))
    first = [
        RingCopy(send, "z", lambda place, h: out.at[0, core, place, me_x, rows[h]]),
        RingCopy(send, "x", lambda place, h: out.at[1, core, me_z, place, rows[h]]),
    ]
    second = [
        RingCopy(send, "x", lambda place, h: out.at[0, core, two[h], place]),
        RingCopy(send, "z", lambda place, h: out.at[1, core, place, two[h]]),
    ]
    for copy in own:
        copy.wait()
    for step in first:
        step.begin()
    for step in first:
        step.middle()
    for s in range(2):
        first[s].near()
        first[s].end()
        second[s].begin()
    shared = []

    def share(view):
        shared.append(send(view, view, to_sib))

    share(out.at[0, core, :, me_x])
    share(out.at[1, core, me_z])
    for step in second:
        step.middle()
    for s in range(2):
        second[s].near()
        if s == 0:
            share(out.at[0, core, :, left_x])
            share(out.at[0, core, :, right_x])
        else:
            share(out.at[1, core, left_z])
            share(out.at[1, core, right_z])
    for s in range(2):
        second[s].end()
        share(out.at[0, core, :, far_x] if s == 0 else out.at[1, core, far_z])
    for copy in shared:
        copy.wait_recv()
    send.finish()


def spread(kernel_id, piece):
    return pl.pallas_call(
        spread_kernel,
        out_shape=jax.ShapeDtypeStruct((2, 2, 4, 4, PIECE, 128), BF16),
        in_specs=[ANY],
        out_specs=ANY,
        scratch_shapes=[
            pltpu.SemaphoreType.DMA((32,)),
            pltpu.SemaphoreType.DMA((32,)),
            pltpu.SemaphoreType.DMA((2,)),
        ],
        compiler_params=pltpu.CompilerParams(collective_id=kernel_id, has_side_effects=True),
    )(piece)


def unpack_rows_kernel(pieces, gate, up, query, key, value):
    for x in range(4):
        for t in range(9):
            cols = slice(x * 1152 + t * 128, x * 1152 + (t + 1) * 128)
            gate[:, cols] = pieces[0, 0, 0, x, t * 32 : (t + 1) * 32, :].astype(F32)
            up[:, cols] = pieces[1, 0, 0, x, t * 32 : (t + 1) * 32, :].astype(F32)
        for t in range(2):
            cols = slice(x * 256 + t * 128, x * 256 + (t + 1) * 128)
            query[:, cols] = pieces[0, 0, 0, x, 288 + t * 32 : 320 + t * 32, :].astype(F32)
        cols = slice(x * 128, (x + 1) * 128)
        key[:, cols] = pieces[1, 0, 0, x, 288:320, :].astype(F32)
        value[:, cols] = pieces[1, 0, 0, x, 320:352, :].astype(F32)


def unpack_columns_kernel(pieces, down, out):
    for s in range(2):
        for z in range(4):
            cols = slice(s * 512 + z * 128, s * 512 + (z + 1) * 128)
            down[:, cols] = pieces[s, 0, z, 0, 352:496, :].astype(F32)
            out[:, cols] = pieces[s, 0, z, 0, 496:528, :].astype(F32)


def unpack(pieces):
    rows = pl.pallas_call(
        unpack_rows_kernel,
        grid=(4, 2),
        out_shape=tuple(
            jax.ShapeDtypeStruct((256, width), F32) for width in (4608, 4608, 1024, 512, 512)
        ),
        in_specs=[pl.BlockSpec((2, 1, 1, 4, PIECE, 128), lambda z, c: (0, c, z, 0, 0, 0))],
        out_specs=tuple(
            pl.BlockSpec((32, width), lambda z, c: (2 * z + c, 0))
            for width in (4608, 4608, 1024, 512, 512)
        ),
        compiler_params=pltpu.CompilerParams(vmem_limit_bytes=32 * 2**20),
    )(pieces)
    columns = pl.pallas_call(
        unpack_columns_kernel,
        grid=(4, 2),
        out_shape=(
            jax.ShapeDtypeStruct((1152, 1024), F32),
            jax.ShapeDtypeStruct((256, 1024), F32),
        ),
        in_specs=[pl.BlockSpec((2, 1, 4, 1, PIECE, 128), lambda x, c: (0, c, 0, x, 0, 0))],
        out_specs=(
            pl.BlockSpec((144, 1024), lambda x, c: (2 * x + c, 0)),
            pl.BlockSpec((32, 1024), lambda x, c: (2 * x + c, 0)),
        ),
        compiler_params=pltpu.CompilerParams(vmem_limit_bytes=32 * 2**20),
    )(pieces)
    return rows + columns


SWAP = [(a * 4 + b, b * 4 + a) for a in range(4) for b in range(4)]


def on_device(
    hidden_in,
    positions,
    block_of,
    attn_gain,
    query_weight,
    key_weight,
    value_weight,
    out_weight,
    query_gain,
    key_gain,
    ffn_gain,
    gate_weight,
    up_weight,
    down_weight,
    cotangent,
):
    z_at = lax.axis_index("z")
    x_at = lax.axis_index("x")
    core_at = lax.axis_index("core")
    dp_at = lax.axis_index("dp")

    hidden_rows = hidden_in[0]
    grad_rows = cotangent[0]

    in_block = jnp.arange(BLK, dtype=jnp.int32)
    blocks = block_of.reshape(4, 4, 2, 2).transpose(0, 2, 3, 1)
    order_all = (blocks[..., None] * BLK + in_block).reshape(GROUPS, ROWS)
    own_order = lax.dynamic_index_in_dim(order_all, z_at * 2 + core_at, 0, keepdims=True)
    k_order = order_all.reshape(GROUPS, ROWS, 1)
    own_slot = 2 * (z_at * 8 + x_at * 2 + core_at)
    first_block = lax.dynamic_index_in_dim(block_of, own_slot, 0, keepdims=False)
    offset = positions[0, 0] - first_block * BLK
    frequency = ROPE_BASE ** (-2.0 * jnp.arange(HD // 2, dtype=F32) / HD)
    angles = (own_order + offset).astype(F32) * frequency[:, None]
    cosine, sine = jnp.cos(angles), jnp.sin(angles)

    def columns(weight, width):
        return lax.dynamic_slice_in_dim(weight, x_at * width, width, axis=1)

    def swapped_rows(weight, rows):
        own = lax.dynamic_slice_in_dim(weight, x_at * rows, rows, axis=0)
        return lax.all_gather(lax.ppermute(own, ("dp", "x"), SWAP), "dp", axis=0, tiled=True)

    gains = lax.all_gather(
        jnp.concatenate([attn_gain, ffn_gain, query_gain, key_gain]), "dp", axis=0
    ).astype(F32)
    attn_gain_all = gains[:, 0:256].reshape(1024)
    ffn_gain_all = gains[:, 256:512].reshape(1024)
    query_gain_all = gains[:, 512:528].reshape(HD)
    key_gain_all = gains[:, 528:544].reshape(HD)
    qkv_weight = lax.all_gather(
        jnp.concatenate(
            [columns(query_weight, 256), columns(key_weight, 128), columns(value_weight, 128)],
            axis=1,
        ),
        "dp",
        axis=0,
        tiled=True,
    )
    out_slice = swapped_rows(out_weight, 64)
    gate_up = lax.all_gather(
        jnp.concatenate([columns(gate_weight, 1152), columns(up_weight, 1152)], axis=1),
        "dp",
        axis=0,
        tiled=True,
    )
    down_slice = swapped_rows(down_weight, 288)

    hidden = hidden_rows.astype(F32)
    line_rows = line_gather(0, jnp.concatenate([hidden_rows, grad_rows], axis=1))
    line_hidden = line_rows[:, 0:1024]
    branch_low = line_rows[:, 1024:2048]
    attn_in = rms_scale(line_hidden.astype(F32), attn_gain_all).astype(BF16)
    qkv_t = dot(qkv_weight, attn_in, 0, 1)
    q_rot, q_back = jax.vjp(
        lambda r, g: head_norm_rope(r, g, cosine, sine),
        qkv_t[0:256].reshape(4, HD, ROWS),
        query_gain_all,
    )
    k_rot, k_back = jax.vjp(
        lambda r, g: head_norm_rope(r, g, cosine, sine),
        qkv_t[256:384].reshape(2, HD, ROWS),
        key_gain_all,
    )
    q_low = q_rot.reshape(4 * HD, ROWS).astype(BF16)
    kv_low = jnp.concatenate([k_rot, qkv_t[384:512].reshape(2, HD, ROWS)], axis=1).astype(BF16)
    kv_all = sequence_gather(1, kv_low)
    mixed, attn_low, log_total = attend(q_low, kv_all, own_order, k_order)
    after_attn = hidden + line_scatter(2, dot(attn_low, out_slice, 0, 0).astype(BF16))
    normed_ffn, norm_ffn_back = jax.vjp(rms_scale, after_attn, ffn_gain_all)
    ffn_in = line_gather(3, normed_ffn.astype(BF16))
    gate_up_proj = dot(ffn_in, gate_up)
    gate_proj = gate_up_proj[:, :1152]
    up_proj = gate_up_proj[:, 1152:]
    activated, swiglu_back = jax.vjp(lambda g, u: jax.nn.silu(g) * u, gate_proj, up_proj)
    activated_low = activated.astype(BF16)
    layer_out = (
        after_attn + line_scatter(4, dot(activated_low, down_slice).astype(BF16))
    ).astype(BF16)

    residual_grad = grad_rows.astype(F32)
    activated_grad = dot(branch_low, down_slice, 1, 1)
    gate_grad, up_grad = swiglu_back(activated_grad)
    gate_up_grad = jnp.concatenate([gate_grad, up_grad], axis=1).astype(BF16)
    ffn_in_grad = line_scatter(5, dot(gate_up_grad, gate_up, 1, 1).astype(BF16))
    mid_part, ffn_gain_part = norm_ffn_back(ffn_in_grad)
    mid_grad = residual_grad + mid_part
    branch_attn = line_gather(6, mid_grad.astype(BF16))
    mixed_grad = dot(out_slice, branch_attn, 1, 1).astype(BF16)
    q_grad, kv_grad_all = attend_back(
        q_low, kv_all, own_order, k_order, mixed, log_total, mixed_grad
    )
    kv_grad = sequence_scatter(7, kv_grad_all)
    q_pre, q_gain_part = q_back(q_grad.reshape(4, HD, ROWS))
    k_pre, k_gain_part = k_back(kv_grad[:, 0:HD])
    qkv_pre = jnp.concatenate(
        [
            q_pre.reshape(4 * HD, ROWS),
            k_pre.reshape(2 * HD, ROWS),
            kv_grad[:, HD:].reshape(2 * HD, ROWS),
        ],
        axis=0,
    ).astype(BF16)
    attn_in_grad = line_scatter(8, dot(qkv_pre, qkv_weight, 0, 1).astype(BF16))
    unused, norm_attn_back = jax.vjp(rms_scale, hidden, attn_gain_all)
    hidden_part, attn_gain_part = norm_attn_back(attn_in_grad)
    input_grad = (mid_grad + hidden_part).astype(BF16)

    gain_sums = lax.psum(
        jnp.concatenate([attn_gain_part, ffn_gain_part, q_gain_part, k_gain_part]),
        ("dp", "z", "x", "core"),
    )

    def own_slice(begin, size):
        return lax.dynamic_slice_in_dim(
            gain_sums[begin : begin + size], dp_at * (size // 4), size // 4
        )

    own_piece = sum_grads(
        9,
        dot(ffn_in, gate_up_grad, 0, 0).astype(BF16),
        dot(attn_in, qkv_pre, 0, 1).astype(BF16),
        dot(activated_low, branch_low, 0, 0).astype(BF16),
        dot(attn_low, branch_attn).astype(BF16),
    )
    swapped = lax.ppermute(own_piece[:, 352:], ("dp", "x"), SWAP)
    pieces = spread(10, jnp.concatenate([own_piece[:, :352], swapped], axis=1))
    gate_all, up_all, query_all, key_all, value_all, down_all, out_all = unpack(pieces)
    return (
        layer_out[None],
        input_grad[None],
        own_slice(0, 1024),
        query_all,
        key_all,
        value_all,
        out_all,
        own_slice(2048, 64),
        own_slice(2112, 64),
        own_slice(1024, 1024),
        gate_all,
        up_all,
        down_all,
    )


def solution(mesh):
    fine = Mesh(mesh.devices.reshape(4, 4, 4, 2), ("dp", "z", "x", "core"))
    ctx = ("z", "x", "core")
    rows = P("dp", ctx, None)
    vector, matrix = P("dp"), P("dp", None)
    return jax.shard_map(
        on_device,
        mesh=fine,
        in_specs=(rows, P("dp", ctx), P(), vector)
        + (matrix,) * 4
        + (vector,) * 3
        + (matrix,) * 3
        + (rows,),
        out_specs=(rows, rows, vector) + (matrix,) * 4 + (vector,) * 3 + (matrix,) * 3,
        check_vma=False,
    )
```

time: 744 us -> 479 us (0.64)
  waiting for transfers between devices: 338 us -> 0.08 us
  Pallas kernels: 31.9 us -> 274 us
  local copies, waits for them, and re-layouts: 126 us -> 28.7 us
  blocking collectives: 140 us -> 104 us
  other arithmetic: 32.5 us -> 12.3 us
    pallas_call x2 -> x15, Pallas kernels: 31.9 us -> 274 us  [the longest x4 66.9 us: gather_call(): pl.pallas_call(functools.partial(gather_kernel, axis, sibling, at), out_s...]
    reduce_scatter x12 -> x0, waiting for transfers between devices: 211 us -> none  [the longest x4 78.2 us: reduce_rows(): lax.psum_scatter(part.astype(BF16), 'dp', scatter_dimension=0, tiled=True)]
    all_gather x10 -> x3, waiting for transfers between devices: 126 us -> 0.02 us  [the longest x1 0.02 us: on_device(): lax.all_gather(jnp.concatenate([columns(query_weight, 256), columns(key_w...]
    all_gather x3 -> x1, blocking collectives: 50.1 us -> 13.7 us  [swapped_rows(): lax.all_gather(lax.ppermute(own, ('dp', 'x'), SWAP), 'dp', axis=0, tiled=...]
    convert_element_type x4 -> x0, local copies, waits for them, and re-layouts: 34.9 us -> none  [the longest x1 26.8 us: on_device(): gate_up_all.transpose(3, 0, 2, 4, 1, 5).reshape(2, 256, 4608).astype(F32)]
    slice x10 -> x8, local copies, waits for them, and re-layouts: 33.1 us -> 0.72 us  [the longest x1 0.67 us: on_device(): kv_grad[:, HD:].reshape(2 * HD, ROWS)]
    squeeze x2 -> x0, local copies, waits for them, and re-layouts: 18.4 us -> none  [the longest x1 9.22 us: on_device(): gate_up_all[0]]
    convert_element_type x6 -> x3, other arithmetic: 11.8 us -> 2.89 us  [the longest x1 1.16 us: on_device(): input_grad = (mid_grad + hidden_part).astype(BF16)]
  transfers between devices with their start and end apart: 25 -> 6, of which waited for: 16 -> 0; matrix products, arithmetic and copies ran while one was open for 14% -> 6% of each run, Pallas kernels for 0% -> 18%
where the time goes in v2:
time: 479 us; the launch traced here: 478 us
  Pallas kernels  274 us (57%)
  blocking collectives  104 us (22%)
  matrix products  35.2 us (7%)
  local copies, waits for them, and re-layouts  28.7 us (6%)
  between operations  16.2 us (3%)
  other arithmetic  12.3 us (3%)
  starting transfers between devices  7.41 us (2%)
    pallas_call x4, Pallas kernels, gather_call(): pl.pallas_call(functools.partial(gather_kernel, axis, sibling, at), out_s...  66.9 us
    psum x1, blocking collectives, on_device(): lax.psum(jnp.concatenate([attn_gain_part, ffn_gain_part, q_gain_part, k_g...  64.2 us
    pallas_call x4, Pallas kernels, line_scatter(): pl.pallas_call(line_scatter_kernel, out_shape=jax.ShapeDtypeStruct((2, BL...  49.2 us
    pallas_call x1, Pallas kernels, spread(): pl.pallas_call(spread_kernel, out_shape=jax.ShapeDtypeStruct((2, 2, 4, 4,...  45.2 us
    pallas_call x1, Pallas kernels, sum_grads(): pl.pallas_call(grads_kernel, out_shape=jax.ShapeDtypeStruct((2, PIECE, 12...  37.9 us
    dot_general x12, matrix products, dot(): lax.dot_general(left, right, (((left_dim,), (right_dim,)), ((), ())), pre...  35.2 us
    pallas_call x1, Pallas kernels, attend_back(): pl.pallas_call(attend_back_kernel, out_shape=(jax.ShapeDtypeStruct((4 * H...  30.3 us
    unnamed x1, blocking collectives  25.6 us
  transfers between devices with their start and end apart: 6, of which 0 were waited for; matrix products, arithmetic and copies ran while one was open for 6% of the time, Pallas kernels for 18%

profile of v2, /device:TPU:1, one launch (start us, length us, event | category | flops | bytes accessed | tf_op | source)
XLA Modules:
  0.0 477.5 jit_solution(18002252620502827730)
XLA Ops:
  7.2 1.1 constant_dynamic-slice_fusion.6
  8.3 0.9 constant_dynamic-slice_fusion.4
  9.2 0.7 pad_maximum_fusion.9
  10.0 1.3 constant_dynamic-slice_fusion.1
  11.4 1.1 pad_maximum_fusion.5
  12.6 1.0 constant_dynamic-slice_fusion.3
  13.6 0.7 collective-permute-start
  14.3 0.9 constant_dynamic-slice_fusion
  15.2 6.0 %collective-permute-start.1 = (bf16[288,1024]{1,0:T(8,128)(2,1)}, bf16[288,1024]{1,0:T(8,128)(2,1)}, u32[]{:S(2)}, u32[]{:S(2)}) collective-permute-start(bf16[288,1024]{1,0:T(8,128)(2,1)} %constant_dynamic-slice_fusion), channel_id=1, source_target_pairs={{0,0},{2,32},{4,64},{6,96},{32,2},{34,34},{36,66},{38,98},{64,4},{... | collective-permute-start | bytes 1769480 | tf_op jit(solution)/shard_map/ppermute | solution.py:808
  21.6 2.1 add.239
  23.7 0.6 dynamic-slice
  25.2 25.6 %all-reduce.4 = bf16[2176]{0:T(1024)(128)(2,1)S(1)} all-reduce(bf16[2176]{0:T(1024)(128)(2,1)S(1)} %dynamic-update-slice), channel_id=2, replica_groups=mesh['dp'=4,'z'=4,'x'=4,'core'=2] {'dp'}, use_global_device_ids=true, to_apply=%add.4 | all-reduce | flops 2176 | bytes 8704
  51.1 0.8 pad_maximum_fusion.6.src
  52.0 24.2 %shard_map.246 = bf16[2,4,64,2048]{3,2,1,0:T(8,128)(2,1)} custom-call(bf16[2,64,2048]{2,1,0:T(8,128)(2,1)} %pad_maximum_fusion.6.src), custom_call_target="tpu_custom_call" | custom-call | tf_op jit(solution)/shard_map/pallas_call | solution.py:270
  76.2 0.6 dynamic_slice.45
  78.0 1.5 broadcast_add_fusion.ko_ref
  80.0 13.7 %all_gather.21 = bf16[256,1024]{1,0:T(8,128)(2,1)} all-gather(bf16[64,1024]{1,0:T(8,128)(2,1)S(1)} %collective-permute-done), channel_id=1, replica_groups=mesh['dp'=4,'z'=4,'x'=4,'core'=2] {'dp'}, dimensions={0}, use_global_device_ids=true | all-gather | bytes 655360 | tf_op jit(solution)/shard_map/all_gather | solution.py:808
  93.8 2.4 fusion.29
  96.5 0.8 pad_maximum_fusion.11.src
  97.3 20.3 %shard_map.247 = bf16[4,2,2,128,512]{4,3,2,1,0:T(8,128)(2,1)} custom-call(bf16[2,128,512]{2,1,0:T(8,128)(2,1)} %pad_maximum_fusion.11.src), custom_call_target="tpu_custom_call" | custom-call | tf_op jit(solution)/shard_map/pallas_call | solution.py:270
  119.2 1.6 copy-done.5
  120.8 17.3 %shard_map.248 = (f32[256,512]{1,0:T(8,128)S(1)}, bf16[256,512]{1,0:T(8,128)(2,1)S(1)}, f32[4,512]{1,0:T(4,128)S(1)}) custom-call(bf16[256,512]{1,0:T(8,128)(2,1)S(1)} %bitcast.113, bf16[8,2,128,512]{3,2,1,0:T(8,128)(2,1)S(1)} %bitcast.105, s32[1,512]{1,0:T(1,128)S(1)} %get-tuple-element.46.qo_ref, s32[8,512,1]{2,1,0:T(8,128)S(1)} %copy-done.5), custom_call_target="tpu_custom_call" | custom-call | flops 2000000000 | bytes 4000000 | tf_op jit(solution)/shard_map/pallas_call | solution.py:100
  138.6 13.0 %shard_map.249 = f32[2,64,1024]{2,1,0:T(8,128)S(1)} custom-call(bf16[2,4,64,1024]{3,2,1,0:T(8,128)(2,1)S(1)} %bitcast.101), custom_call_target="tpu_custom_call" | custom-call | tf_op jit(solution)/shard_map/pallas_call | solution.py:354
  151.8 0.8 multiply_convert_fusion.2.src
  152.6 11.5 %shard_map.250 = bf16[2,4,64,1024]{3,2,1,0:T(8,128)(2,1)} custom-call(bf16[2,64,1024]{2,1,0:T(8,128)(2,1)} %multiply_convert_fusion.2.src), custom_call_target="tpu_custom_call" | custom-call | tf_op jit(solution)/shard_map/pallas_call | solution.py:270
  164.8 7.5 %fusion.43 = f32[512,2304]{1,0:T(8,128)} fusion(bf16[512,1024]{1,0:T(8,128)(2,1)} %bitcast.133, bf16[1024,2304]{1,0:T(8,128)(2,1)} %all-gather.7.cloned.1.call-done), kind=kOutput, calls=%fused_computation.128 | convolution fusion | flops 2415919104 | bytes 10485760 | tf_op jit(solution)/shard_map/dot_general | solution.py:30
  172.2 6.8 %fusion.2 = (bf16[512,1152]{1,0:T(8,128)(2,1)S(1)}, bf16[512,1152]{1,0:T(8,128)(2,1)S(1)}, bf16[512,1152]{1,0:T(8,128)(2,1)}) fusion(f32[512,2304]{1,0:T(8,128)} %fusion.43, bf16[1152,1024]{1,0:T(8,128)(2,1)} %all-gather.9.cloned.1.call-done, bf16[512,2048]{1,0:T(8,128)(2,1)} %bitcast.127), kind=kOutput, calls=%fused_computation.7 | convolution fusion | flops 1217396736 | bytes 11665408 | tf_op jit(solution)/shard_map/dot_general | solution.py:30
  179.1 2.6 fusion.8
  181.8 11.2 %shard_map.252 = f32[2,64,1024]{2,1,0:T(8,128)S(1)} custom-call(bf16[2,4,64,1024]{3,2,1,0:T(8,128)(2,1)S(1)} %bitcast.111), custom_call_target="tpu_custom_call" | custom-call | tf_op jit(solution)/shard_map/pallas_call | solution.py:354
  193.0 0.7 multiply_reduce_fusion.1
  194.3 0.9 fusion.22.src
  195.2 10.8 %shard_map.253 = bf16[2,4,64,1024]{3,2,1,0:T(8,128)(2,1)} custom-call(bf16[2,64,1024]{2,1,0:T(8,128)(2,1)} %fusion.22.src), custom_call_target="tpu_custom_call" | custom-call | tf_op jit(solution)/shard_map/pallas_call | solution.py:270
  206.1 1.9 convolution_convert_fusion.7.grad_ref
  208.0 1.6 copy-done.6
  209.6 0.9 copy-done.11
  210.5 1.0 copy-done.13
  211.5 30.3 %shard_map.254 = (f32[256,512]{1,0:T(8,128)S(1)}, bf16[8,2,128,512]{3,2,1,0:T(8,128)(2,1)S(1)}) custom-call(bf16[256,512]{1,0:T(8,128)(2,1)S(1)} %bitcast.114, bf16[8,2,128,512]{3,2,1,0:T(8,128)(2,1)S(1)} %bitcast.106, s32[1,512]{1,0:T(1,128)S(1)} %get-tuple-element.46.qo_ref, s32[8,512,1]{2,1,0:T(8,128)S(1)} %copy-done.6, f32[256,512]{1,0:T(8,128)S(1)} %copy-done.13, ...), custom_call_target="tpu_custom_call" | custom-call | flops 4000000000 | bytes 6000000 | tf_op jit(solution)/shard_map/pallas_call | solution.py:168
  241.9 17.6 %shard_map.255 = f32[2,128,512]{2,1,0:T(8,128)S(1)} custom-call(bf16[4,2,2,128,512]{4,3,2,1,0:T(8,128)(2,1)S(1)} %bitcast.104), custom_call_target="tpu_custom_call" | custom-call | tf_op jit(solution)/shard_map/pallas_call | solution.py:456
  259.5 0.7 slice.153
  260.3 0.6 reduce_sum.126
  260.9 6.1 %convolution_convert_fusion = bf16[1024,2304]{1,0:T(8,128)(2,1)} fusion(bf16[512,1024]{1,0:T(8,128)(2,1)S(1)} %bitcast.134, bf16[512,1152]{1,0:T(8,128)(2,1)} %copy-done.68, bf16[512,1152]{1,0:T(8,128)(2,1)} %copy-done.67), kind=kOutput, calls=%fused_computation | convolution fusion | flops 2422996992 | bytes 8126464 | tf_op jit(solution)/shard_map/dot_general | solution.py:30
  267.5 0.7 multiply_reduce_fusion.6
  268.9 0.9 copy-done.23
  269.8 1.9 convolution_convert_fusion.4
  271.7 0.8 convolution_convert_fusion.5
  272.5 12.9 %shard_map.256 = f32[2,64,1024]{2,1,0:T(8,128)S(1)} custom-call(bf16[2,4,64,1024]{3,2,1,0:T(8,128)(2,1)S(1)} %bitcast.109), custom_call_target="tpu_custom_call" | custom-call | tf_op jit(solution)/shard_map/pallas_call | solution.py:354
  285.6 2.8 convolution_convert_fusion.1
  288.5 1.5 convolution_convert_fusion.2
  290.1 12.0 %shard_map.251 = f32[2,64,1024]{2,1,0:T(8,128)S(1)} custom-call(bf16[2,4,64,1024]{3,2,1,0:T(8,128)(2,1)S(1)} %bitcast.110), custom_call_target="tpu_custom_call" | custom-call | tf_op jit(solution)/shard_map/pallas_call | solution.py:354
  302.5 64.2 %psum.7 = f32[2176]{0:T(1024)S(1)} all-reduce(f32[2176]{0:T(1024)S(1)} %concatenate.49), channel_id=1, replica_groups=mesh['dp'=4,'z'=4,'x'=4,'core'=2] {'dp','z','x','core'}, use_global_device_ids=true, to_apply=%region_13.14 | all-reduce | flops 2176 | bytes 17408 | tf_op jit(solution)/shard_map/psum | solution.py:895
  366.7 1.7 copy-done.3
  368.4 1.2 copy-done.7
  369.6 37.9 %shard_map.257 = bf16[2,528,128]{2,1,0:T(8,128)(2,1)S(1)} custom-call(bf16[4,4,2,32,2304]{4,3,2,1,0:T(8,128)(2,1)} %bitcast.125, bf16[4,4,2,32,512]{4,3,2,1,0:T(8,128)(2,1)S(1)} %bitcast.108, bf16[4,2,144,1024]{3,2,1,0:T(8,128)(2,1)S(1)} %bitcast.102, bf16[4,2,32,1024]{3,2,1,0:T(8,128)(2,1)S(1)} %bitcast.103), custom_call_target="tpu_custom_call" | custom-call | tf_op jit(solution)/shard_map/pallas_call | solution.py:580
  407.6 0.7 collective-permute-start.2
  408.3 1.2 fusion.20
  409.6 0.6 dynamic_slice.51
  410.1 0.6 dynamic_slice.52
  410.7 0.6 dynamic_slice.50
  411.4 0.6 dynamic_slice.53
  412.0 0.7 pad_maximum_fusion.8.piece
  412.7 45.2 %shard_map.258.pieces = bf16[2,2,4,4,528,128]{5,4,3,2,1,0:T(8,128)(2,1)} custom-call(bf16[2,528,128]{2,1,0:T(8,128)(2,1)} %pad_maximum_fusion.8.piece), custom_call_target="tpu_custom_call" | custom-call | tf_op jit(solution)/shard_map/pallas_call | solution.py:696
  457.9 3.4 copy-done.2
  461.4 5.3 %shard_map.259 = (f32[256,4608]{1,0:T(8,128)}, f32[256,4608]{1,0:T(8,128)}, f32[256,1024]{1,0:T(8,128)}, f32[256,512]{1,0:T(8,128)}, f32[256,512]{1,0:T(8,128)}) custom-call(bf16[2,2,4,4,528,128]{5,4,3,2,1,0:T(8,128)(2,1)S(1)} %copy-done.2), custom_call_target="tpu_custom_call" | custom-call | tf_op jit(solution)/shard_map/pallas_call | solution.py:733
  466.7 4.3 shard_map.260
  (201 shorter events, 7.5 us)
Async XLA Ops:
  7.2 7.1 %copy-start = (bf16[1152,1024]{1,0:T(8,128)(2,1)S(1)}, bf16[1152,1024]{1,0:T(8,128)(2,1)}, u32[]{:S(2)}) copy-start(bf16[1152,1024]{1,0:T(8,128)(2,1)} %param.28) | copy-start | bytes 7077892
  7.2 86.6 %all-gather.5.cloned.1.call-start = ((), (), s32[]{:S(2)}) async-start(), calls=%async_computation | async-start | bytes 1310720 | tf_op jit(solution)/shard_map/all_gather | solution.py:817
  10.0 154.8 %all-gather.7.cloned.1.call-start = ((), (), s32[]{:S(2)}) async-start(), calls=%async_computation.1 | async-start | bytes 5898240 | tf_op jit(solution)/shard_map/all_gather | solution.py:827
  11.4 9.8 %copy-start.63 = (s32[64]{0:T(128)S(1)}, s32[64]{0:T(128)}, u32[]{:S(2)}) copy-start(s32[64]{0:T(128)} %param.17) | copy-start | bytes 772
  12.5 11.2 %copy-start.65 = (u32[128]{0:T(128)S(1)}, u32[128]{0:T(128)}, u32[]{:S(2)}) copy-start(u32[128]{0:T(128)} %constant.99) | copy-start | bytes 1540
  12.5 12.5 %copy-start.56 = (bf16[16]{0:T(256)(128)(2,1)S(1)}, bf16[16]{0:T(256)(128)(2,1)}, u32[]{:S(2)}) copy-start(bf16[16]{0:T(256)(128)(2,1)} %param.24) | copy-start | bytes 100
  12.5 12.5 %copy-start.57 = (bf16[16]{0:T(256)(128)(2,1)S(1)}, bf16[16]{0:T(256)(128)(2,1)}, u32[]{:S(2)}) copy-start(bf16[16]{0:T(256)(128)(2,1)} %param.23) | copy-start | bytes 100
  12.5 12.5 %copy-start.58 = (bf16[256]{0:T(256)(128)(2,1)S(1)}, bf16[256]{0:T(256)(128)(2,1)}, u32[]{:S(2)}) copy-start(bf16[256]{0:T(256)(128)(2,1)} %param.25) | copy-start | bytes 1540
  12.5 12.5 %copy-start.59 = (bf16[256]{0:T(256)(128)(2,1)S(1)}, bf16[256]{0:T(256)(128)(2,1)}, u32[]{:S(2)}) copy-start(bf16[256]{0:T(256)(128)(2,1)} %param.18) | copy-start | bytes 1540
  12.5 38.6 %copy-start.14 = (bf16[1,128,1024]{2,1,0:T(8,128)(2,1)S(1)}, bf16[1,128,1024]{2,1,0:T(8,128)(2,1)}, u32[]{:S(2)}) copy-start(bf16[1,128,1024]{2,1,0:T(8,128)(2,1)} %param.15) | copy-start | bytes 786436
  12.5 38.6 %copy-start.24 = (bf16[1,128,1024]{2,1,0:T(8,128)(2,1)S(1)}, bf16[1,128,1024]{2,1,0:T(8,128)(2,1)}, u32[]{:S(2)}) copy-start(bf16[1,128,1024]{2,1,0:T(8,128)(2,1)} %param.29) | copy-start | bytes 786436
  12.5 159.7 %all-gather.9.cloned.1.call-start = ((), (), s32[]{:S(2)}) async-start(), calls=%async_computation.2 | async-start | bytes 2949120 | tf_op jit(solution)/shard_map/all_gather | solution.py:808
  13.6 66.4 %collective-permute-start = (bf16[64,1024]{1,0:T(8,128)(2,1)S(1)}, bf16[64,1024]{1,0:T(8,128)(2,1)S(1)}, u32[]{:S(2)}, u32[]{:S(2)}) collective-permute-start(bf16[64,1024]{1,0:T(8,128)(2,1)S(1)} %constant_dynamic-slice_fusion.3), channel_id=1, source_target_pairs={{0,0},{2,32},{4,64},{6,96},{32,2},{34,34},{36,66},{38,98},{64,4},{... | collective-permute-start | bytes 393224 | tf_op jit(solution)/shard_map/ppermute | solution.py:808
  15.2 78.6 %collective-permute-start.1 = (bf16[288,1024]{1,0:T(8,128)(2,1)}, bf16[288,1024]{1,0:T(8,128)(2,1)}, u32[]{:S(2)}, u32[]{:S(2)}) collective-permute-start(bf16[288,1024]{1,0:T(8,128)(2,1)} %constant_dynamic-slice_fusion), channel_id=1, source_target_pairs={{0,0},{2,32},{4,64},{6,96},{32,2},{34,34},{36,66},{38,98},{64,4},{... | collective-permute-start | bytes 1769480 | tf_op jit(solution)/shard_map/ppermute | solution.py:808
  23.7 54.0 %copy-start.64 = (s32[1,128]{1,0:T(1,128)S(1)}, s32[1,128]{1,0:T(1,128)}, u32[]{:S(2)}) copy-start(s32[1,128]{1,0:T(1,128)} %param.16) | copy-start | bytes 1540
  51.0 42.8 %copy-start.35 = (f32[1,2,4,128]{3,1,2,0:T(2,128)}, f32[1,2,4,128]{3,1,2,0:T(2,128)S(1)}, u32[]{:S(2)}) copy-start(f32[1,2,4,128]{3,1,2,0:T(2,128)S(1)} %copy.31) | copy-start | bytes 12292
  51.1 66.6 %copy-start.45 = (f32[64]{0:T(128)}, f32[64]{0:T(128)S(1)}, u32[]{:S(2)}) copy-start(f32[64]{0:T(128)S(1)} %mul.526) | copy-start | bytes 772
  77.0 19.4 %copy-start.47 = (f32[64]{0:T(128)}, f32[64]{0:T(128)S(1)}, u32[]{:S(2)}) copy-start(f32[64]{0:T(128)S(1)} %mul.551) | copy-start | bytes 772
  77.7 2.1 copy-start.22
  80.0 13.8 %copy-start.52 = (f32[512]{0:T(512)}, f32[512]{0:T(512)S(1)}, u32[]{:S(2)}) copy-start(f32[512]{0:T(512)S(1)} %add_rsqrt_fusion) | copy-start | bytes 6148
  96.2 21.5 %copy-start.18 = (f32[512,512]{1,0:T(8,128)}, f32[512,512]{1,0:T(8,128)S(1)}, u32[]{:S(2)}) copy-start(f32[512,512]{1,0:T(8,128)S(1)} %fusion.29) | copy-start | bytes 3145732
  96.3 21.3 %copy-start.38 = (f32[2,512]{1,0:T(2,128)}, f32[2,512]{1,0:T(2,128)S(1)}, u32[]{:S(2)}) copy-start(f32[2,512]{1,0:T(2,128)S(1)} %multiply_reduce_fusion.8) | copy-start | bytes 12292
  96.3 21.3 %copy-start.33 = (f32[2,512]{1,0:T(2,128)}, f32[2,512]{1,0:T(2,128)S(1)}, u32[]{:S(2)}) copy-start(f32[2,512]{1,0:T(2,128)S(1)} %fusion.32) | copy-start | bytes 12292
  117.6 1.6 copy-start.4
  118.5 19.6 %copy-start.10 = (bf16[4,64,512]{2,1,0:T(8,128)(2,1)}, bf16[4,64,512]{2,1,0:T(8,128)(2,1)S(1)}, u32[]{:S(2)}) copy-start(bf16[4,64,512]{2,1,0:T(8,128)(2,1)S(1)} %pad_maximum_fusion.10) | copy-start | bytes 786436
  119.2 1.6 copy-start.5
  120.8 17.3 %copy-start.21 = (bf16[256,1024]{1,0:T(8,128)(2,1)S(1)}, bf16[256,1024]{1,0:T(8,128)(2,1)}, u32[]{:S(2)}) copy-start(bf16[256,1024]{1,0:T(8,128)(2,1)} %all_gather.21) | copy-start | bytes 1572868
  138.1 13.5 %copy-start.12 = (f32[256,512]{1,0:T(8,128)}, f32[256,512]{1,0:T(8,128)S(1)}, u32[]{:S(2)}) copy-start(f32[256,512]{1,0:T(8,128)S(1)} %get-tuple-element.26.mixed_ref) | copy-start | bytes 1572868
  138.1 13.5 %copy-start.15 = (bf16[1,128,1024]{2,1,0:T(8,128)(2,1)S(1)}, bf16[1,128,1024]{2,1,0:T(8,128)(2,1)}, u32[]{:S(2)}) copy-start(bf16[1,128,1024]{2,1,0:T(8,128)(2,1)} %param.15) | copy-start | bytes 786436
  151.8 20.4 %copy-start.43 = (f32[2,64]{1,0:T(2,128)}, f32[2,64]{1,0:T(2,128)S(1)}, u32[]{:S(2)}) copy-start(f32[2,64]{1,0:T(2,128)S(1)} %multiply_reduce_fusion.4) | copy-start | bytes 1540
  151.8 20.4 %copy-start.40 = (f32[2,64]{1,0:T(2,128)}, f32[2,64]{1,0:T(2,128)S(1)}, u32[]{:S(2)}) copy-start(f32[2,64]{1,0:T(2,128)S(1)} %get-tuple-element.71) | copy-start | bytes 1540
  172.2 6.9 %copy-start.60 = (bf16[1024,2304]{1,0:T(8,128)(2,1)S(1)}, bf16[1024,2304]{1,0:T(8,128)(2,1)}, u32[]{:S(2)}) copy-start(bf16[1024,2304]{1,0:T(8,128)(2,1)} %all-gather.7.cloned.1.call-done) | copy-start | bytes 14155780
  179.1 2.7 copy-start.67
  179.1 2.7 copy-start.68
  179.1 13.9 %copy-start.16 = (bf16[1,128,1024]{2,1,0:T(8,128)(2,1)S(1)}, bf16[1,128,1024]{2,1,0:T(8,128)(2,1)}, u32[]{:S(2)}) copy-start(bf16[1,128,1024]{2,1,0:T(8,128)(2,1)} %param.15) | copy-start | bytes 786436
  179.1 13.9 %copy-start.41 = (f32[2,64]{1,0:T(2,128)S(1)}, f32[2,64]{1,0:T(2,128)}, u32[]{:S(2)}) copy-start(f32[2,64]{1,0:T(2,128)} %copy-done.40) | copy-start | bytes 1540
  181.8 12.0 %copy-start.44 = (f32[2,64]{1,0:T(2,128)S(1)}, f32[2,64]{1,0:T(2,128)}, u32[]{:S(2)}) copy-start(f32[2,64]{1,0:T(2,128)} %copy-done.43) | copy-start | bytes 1540
  181.8 12.5 %copy-start.25 = (bf16[1,128,1024]{2,1,0:T(8,128)(2,1)S(1)}, bf16[1,128,1024]{2,1,0:T(8,128)(2,1)}, u32[]{:S(2)}) copy-start(bf16[1,128,1024]{2,1,0:T(8,128)(2,1)} %param.29) | copy-start | bytes 786436
  208.0 1.6 copy-start.6
  241.9 17.7 %copy-start.8 = (f32[256,512]{1,0:T(8,128)}, f32[256,512]{1,0:T(8,128)S(1)}, u32[]{:S(2)}) copy-start(f32[256,512]{1,0:T(8,128)S(1)} %get-tuple-element.28) | copy-start | bytes 1572868
  241.9 18.4 %copy-start.50 = (f32[2,64]{1,0:T(2,128)S(1)}, f32[2,64]{1,0:T(2,128)}, u32[]{:S(2)}) copy-start(f32[2,64]{1,0:T(2,128)} %copy-done.49) | copy-start | bytes 1540
  241.9 19.0 %copy-start.27 = (bf16[2,4,64,1024]{3,2,1,0:T(8,128)(2,1)S(1)}, bf16[2,4,64,1024]{3,2,1,0:T(8,128)(2,1)}, u32[]{:S(2)}) copy-start(bf16[2,4,64,1024]{3,2,1,0:T(8,128)(2,1)} %shard_map.250) | copy-start | bytes 3145732
  260.9 6.1 %copy-start.20 = (bf16[2,4,64,1024]{3,2,1,0:T(8,128)(2,1)S(1)}, bf16[2,4,64,1024]{3,2,1,0:T(8,128)(2,1)}, u32[]{:S(2)}) copy-start(bf16[2,4,64,1024]{3,2,1,0:T(8,128)(2,1)} %shard_map.253) | copy-start | bytes 3145732
  260.9 6.6 %copy-start.19 = (f32[512,512]{1,0:T(8,128)S(1)}, f32[512,512]{1,0:T(8,128)}, u32[]{:S(2)}) copy-start(f32[512,512]{1,0:T(8,128)} %copy-done.18) | copy-start | bytes 3145732
  260.9 6.6 %slice-start = ((f32[512,512]{1,0:T(8,128)}), f32[128,512]{1,0:T(8,128)S(1)}, s32[]{:S(2)}) async-start(f32[512,512]{1,0:T(8,128)} %copy-done.18), calls=%async_computation.3 | async-start | bytes 524288 | tf_op jit(solution)/shard_map/slice | solution.py:848
  260.9 6.7 %copy-start.34 = (f32[2,512]{1,0:T(2,128)S(1)}, f32[2,512]{1,0:T(2,128)}, u32[]{:S(2)}) copy-start(f32[2,512]{1,0:T(2,128)} %copy-done.33) | copy-start | bytes 12292
  260.9 6.7 %copy-start.48 = (f32[64]{0:T(128)S(1)}, f32[64]{0:T(128)}, u32[]{:S(2)}) copy-start(f32[64]{0:T(128)} %copy-done.47) | copy-start | bytes 772
  268.2 1.6 copy-start.23
  268.2 1.6 copy-start.30
  268.2 1.6 copy-start.36
  269.8 1.9 copy-start.62
  271.7 13.7 %copy-start.17 = (bf16[1,128,1024]{2,1,0:T(8,128)(2,1)S(1)}, bf16[1,128,1024]{2,1,0:T(8,128)(2,1)}, u32[]{:S(2)}) copy-start(bf16[1,128,1024]{2,1,0:T(8,128)(2,1)} %param.15) | copy-start | bytes 786436
  271.7 13.9 %copy-start.66 = (bf16[512,1152]{1,0:T(8,128)(2,1)S(1)}, bf16[512,1152]{1,0:T(8,128)(2,1)}, u32[]{:S(2)}) copy-start(bf16[512,1152]{1,0:T(8,128)(2,1)} %get-tuple-element.49) | copy-start | bytes 3538948
  285.6 2.9 copy-start.61
  290.1 12.3 %copy-start.42 = (f32[1024]{0:T(1024)S(1)}, f32[1024]{0:T(1024)}, u32[]{:S(2)}) copy-start(f32[1024]{0:T(1024)} %get-tuple-element.37) | copy-start | bytes 12292
  290.1 12.3 %copy-start.51 = (f32[64]{0:T(128)S(1)}, f32[64]{0:T(128)}, u32[]{:S(2)}) copy-start(f32[64]{0:T(128)} %get-tuple-element.41) | copy-start | bytes 772
  366.7 1.7 copy-start.3
  369.6 38.6 %copy-start.54 = (f32[128]{0:T(128)S(1)}, f32[128]{0:T(128)}, u32[]{:S(2)}) copy-start(f32[128]{0:T(128)} %add.230) | copy-start | bytes 1540
  369.6 38.7 %copy-start.55 = (f32[128]{0:T(128)S(1)}, f32[128]{0:T(128)}, u32[]{:S(2)}) copy-start(f32[128]{0:T(128)} %reduce_sum.126) | copy-start | bytes 1540
  369.6 38.7 %copy-start.26 = (bf16[1,128,1024]{2,1,0:T(8,128)(2,1)S(1)}, bf16[1,128,1024]{2,1,0:T(8,128)(2,1)}, u32[]{:S(2)}) copy-start(bf16[1,128,1024]{2,1,0:T(8,128)(2,1)} %param.29) | copy-start | bytes 786436
  369.6 38.7 %copy-start.37 = (f32[1,2,4,128]{3,1,2,0:T(2,128)S(1)}, f32[1,2,4,128]{3,1,2,0:T(2,128)}, u32[]{:S(2)}) copy-start(f32[1,2,4,128]{3,1,2,0:T(2,128)} %copy-done.35) | copy-start | bytes 12292
  407.6 4.4 collective-permute-start.2
  457.9 3.5 copy-start.2
  461.4 9.6 %copy-start.1 = (bf16[1152,1024]{1,0:T(8,128)(2,1)S(1)}, bf16[1152,1024]{1,0:T(8,128)(2,1)}, u32[]{:S(2)}) copy-start(bf16[1152,1024]{1,0:T(8,128)(2,1)} %param.28) | copy-start | bytes 7077892
  (13 other events, 14.8 us)
Sparse Core Ops, SparseCore 0:
  10.3 50.7 all-gather.4
  63.3 59.9 all-gather.6
  125.0 33.5 all-gather.8

commit v3 on v2

v3 whole, which is shorter than its diff:
```python
import functools

import jax
import jax.numpy as jnp
import numpy as np
from jax import lax
from jax.experimental import pallas as pl
from jax.experimental.pallas import tpu as pltpu
from jax.sharding import Mesh, PartitionSpec as P

HD = 64
BLK = 64
GROUPS = 8
HALF = 256
ROWS = 512
FF_PIECE = 432
PIECE = 96

NORM_EPS = 1e-05
ROPE_BASE = 1000000.0
EXP2_SCALE = float(HD**-0.5 * np.log2(np.e))
SCORE_SCALE = HD**-0.5

F32 = jnp.float32
BF16 = jnp.bfloat16
VMEM = pl.BlockSpec(memory_space=pltpu.VMEM)
ANY = pl.BlockSpec(memory_space=pl.ANY)


def dot(left, right, left_dim=1, right_dim=0):
    return lax.dot_general(
        left, right, (((left_dim,), (right_dim,)), ((), ())), preferred_element_type=F32
    )


def rms_scale(values, gain):
    return values * lax.rsqrt(jnp.mean(values * values, axis=-1, keepdims=True) + NORM_EPS) * gain


def head_norm_rope(raw, gain, cosine, sine):
    scaled = (
        raw
        * lax.rsqrt(jnp.mean(raw * raw, axis=1, keepdims=True) + NORM_EPS)
        * gain[None, :, None]
    )
    front = scaled[:, : HD // 2]
    back = scaled[:, HD // 2 :]
    return jnp.concatenate([front * cosine - back * sine, back * cosine + front * sine], axis=1)


def scores_of(keys_t, queries_t):
    return dot(keys_t, queries_t, 0, 0)


def head_pair(ref, kv_head, cols):
    first = 2 * kv_head * HD
    return jnp.concatenate(
        [ref[first : first + HD, cols], ref[first + HD : first + 2 * HD, cols]], axis=1
    )


def attend_kernel(q_ref, kv_ref, qo_ref, ko_ref, mixed_ref, low_ref, log_ref):
    for half in range(2):
        cols = slice(half * HALF, (half + 1) * HALF)
        q_order = jnp.concatenate([qo_ref[:, cols]] * 2, axis=1)
        queries = [head_pair(q_ref, kv_head, cols) for kv_head in range(2)]

        def group(g, carried):
            carried = list(carried)
            for k_half in range(half + 1):
                keys = slice(k_half * HALF, (k_half + 1) * HALF)
                for kv_head in range(2):
                    acc, total = carried[kv_head]
                    probs = jnp.exp2(
                        scores_of(kv_ref[g, kv_head, 0:HD, keys], queries[kv_head]) * EXP2_SCALE
                    )
                    if k_half == half:
                        allowed = ko_ref[g, keys, :] <= q_order
                        probs = jnp.where(allowed, probs, 0.0)
                    total = total + jnp.sum(probs, axis=0, keepdims=True)
                    acc = acc + dot(kv_ref[g, kv_head, HD : 2 * HD, keys], probs.astype(BF16))
                    carried[kv_head] = (acc, total)
            return tuple(carried)

        start = (jnp.zeros((HD, 2 * HALF), F32), jnp.zeros((1, 2 * HALF), F32))
        sums = lax.fori_loop(0, GROUPS, group, (start, start))
        for kv_head, (acc, total) in enumerate(sums):
            mixed = acc / total
            logs = jnp.log2(total)
            for head in range(2):
                at = 2 * kv_head + head
                rows = slice(at * HD, (at + 1) * HD)
                part = mixed[:, head * HALF : (head + 1) * HALF]
                mixed_ref[rows, cols] = part
                low_ref[rows, cols] = part.astype(BF16)
                log_ref[at : at + 1, cols] = logs[:, head * HALF : (head + 1) * HALF]


def attend(q_t, kv_all, q_order, k_order):
    return pl.pallas_call(
        attend_kernel,
        out_shape=(
            jax.ShapeDtypeStruct((4 * HD, ROWS), F32),
            jax.ShapeDtypeStruct((4 * HD, ROWS), BF16),
            jax.ShapeDtypeStruct((4, ROWS), F32),
        ),
        in_specs=[VMEM] * 4,
        out_specs=(VMEM,) * 3,
        compiler_params=pltpu.CompilerParams(vmem_limit_bytes=40 * 2**20),
        cost_estimate=pl.CostEstimate(
            flops=2 * 10**9, bytes_accessed=4 * 10**6, transcendentals=6 * 10**6
        ),
    )(q_t, kv_all, q_order, k_order)


def ring(axis):
    me = lax.axis_index(axis)
    return me, lax.rem(me + 1, 4), lax.rem(me + 2, 4), lax.rem(me + 3, 4)


def meet(partners):
    barrier = pltpu.get_barrier_semaphore()
    for partner in partners:
        pl.semaphore_signal(
            barrier, inc=1, device_id=partner, device_id_type=pl.DeviceIdType.MESH
        )
    pl.semaphore_wait(barrier, len(partners))


class Sends:
    def __init__(self, send_sems, recv_sems):
        self.send_sems, self.recv_sems, self.started = send_sems, recv_sems, []

    def __call__(self, source, target, partner):
        at = len(self.started)
        copy = pltpu.make_async_remote_copy(
            src_ref=source,
            dst_ref=target,
            send_sem=self.send_sems.at[at],
            recv_sem=self.recv_sems.at[at],
            device_id=partner,
            device_id_type=pl.DeviceIdType.MESH,
        )
        copy.start()
        self.started.append(copy)
        return copy

    def finish(self):
        for copy in self.started:
            copy.wait_send()


class RingGather:
    def __init__(self, send, axis, at, own, sibling=False, share_own=False):
        self.send, self.axis, self.own = send, axis, own
        self.me, self.right, self.far, self.left = ring(axis)
        self.to_right, self.to_left = {axis: self.right}, {axis: self.left}
        core = lax.axis_index("core")
        self.to_sib = {"core": 1 - core}
        self.at = lambda place, half: at(place, core, half)
        self.sibling, self.share_own = sibling, share_own
        self.from_sib = []

    def share(self, place, half, source=None):
        if self.sibling:
            target = self.at(place, half)
            source = target if source is None else source
            self.from_sib.append(self.send(source, target, self.to_sib))

    def begin(self):
        def own_to(half, partner):
            return self.send(self.own(half), self.at(self.me, half), partner)

        self.right0 = own_to(0, self.to_right)
        self.left1 = own_to(1, self.to_left)
        self.right1 = own_to(1, self.to_right)
        self.left0 = own_to(0, self.to_left)
        if self.share_own:
            for half in range(2):
                self.share(self.me, half, self.own(half))

    def middle(self):
        self.right0.wait_recv()
        passed = self.at(self.left, 0)
        self.far0 = self.send(passed, passed, self.to_right)
        self.left1.wait_recv()
        passed = self.at(self.right, 1)
        self.far1 = self.send(passed, passed, self.to_left)
        self.share(self.left, 0)
        self.share(self.right, 1)

    def near(self):
        self.right1.wait_recv()
        self.share(self.left, 1)
        self.left0.wait_recv()
        self.share(self.right, 0)

    def end(self):
        self.far0.wait_recv()
        self.share(self.far, 0)
        self.far1.wait_recv()
        self.share(self.far, 1)

    def finish(self):
        for copy in self.from_sib:
            copy.wait_recv()


def run_gathers(gathers):
    for step in ("begin", "middle", "near", "end", "finish"):
        for gather in gathers:
            getattr(gather, step)()


def sems(count):
    return pltpu.SemaphoreType.DMA((count,))


def rows_half(rows):
    return lambda half: (pl.ds(half * rows, rows), slice(None))


def columns_half(columns):
    return lambda half: (slice(None), pl.ds(half * columns, columns))


def weight_gather(send, src, out, half_of):
    core = lax.axis_index("core")
    return RingGather(
        send,
        "dp",
        lambda place, core, half: out.at[(place, core) + half_of(half)],
        lambda half: src.at[(core,) + half_of(half)],
        sibling=True,
    )


def around(axes, sibling=True):
    partners = []
    for axis in axes:
        unused, right, unused, left = ring(axis)
        partners += [{axis: right}, {axis: left}]
    return partners + ([{"core": 1 - lax.axis_index("core")}] if sibling else [])


def start_kernel(hidden, qkv, gains, hidden_out, qkv_out, gains_out, sends, recvs, loads):
    me_x, me_y = lax.axis_index("x"), lax.axis_index("dp")
    far_y = lax.rem(me_y + 2, 4)
    own = [
        pltpu.make_async_copy(hidden, hidden_out.at[:, me_x], loads.at[0]),
        pltpu.make_async_copy(qkv, qkv_out.at[me_y], loads.at[1]),
        pltpu.make_async_copy(gains, gains_out.at[me_y], loads.at[2]),
    ]
    for copy in own:
        copy.start()
    partners = around(["x", "dp"])
    meet(partners + [{"dp": far_y}])
    send = Sends(sends, recvs)
    direct = [
        send(gains, gains_out.at[me_y], partner) for partner in partners[2:4] + [{"dp": far_y}]
    ]
    run_gathers(
        [
            weight_gather(send, qkv, qkv_out, rows_half(64)),
            RingGather(
                send,
                "x",
                lambda place, core, half: hidden_out.at[half, place],
                lambda half: hidden.at[half],
            ),
        ]
    )
    for copy in direct:
        copy.wait_recv()
    for copy in own:
        copy.wait()
    send.finish()


def start_gather(kernel_id, hidden_rows, qkv, gains):
    hidden, qkv, gains = pl.pallas_call(
        start_kernel,
        out_shape=(
            jax.ShapeDtypeStruct((2, 4, BLK, 1024), BF16),
            jax.ShapeDtypeStruct((4, 2, 128, 512), BF16),
            jax.ShapeDtypeStruct((4, 16, 128), BF16),
        ),
        in_specs=[VMEM] * 3,
        out_specs=(ANY,) * 3,
        scratch_shapes=[sems(21), sems(21), sems(3)],
        compiler_params=pltpu.CompilerParams(collective_id=kernel_id, has_side_effects=True),
    )(hidden_rows.reshape(2, BLK, 1024), qkv.reshape(2, 128, 512), gains)
    return hidden.reshape(ROWS, 1024), qkv.reshape(1024, 512), gains


def line_gather_kernel(src, up, out, up_all, sends, recvs, loads):
    own = [
        pltpu.make_async_copy(src, out.at[:, lax.axis_index("x")], loads.at[0]),
        pltpu.make_async_copy(up, up_all.at[lax.axis_index("dp")], loads.at[1]),
    ]
    for copy in own:
        copy.start()
    meet(around(["x", "dp"]))
    send = Sends(sends, recvs)
    run_gathers(
        [
            line_ring(send, src, out),
            weight_gather(send, up, up_all, rows_half(64)),
        ]
    )
    for copy in own:
        copy.wait()
    send.finish()


def line_ring(send, src, out):
    return RingGather(
        send, "x", lambda place, core, half: out.at[half, place], lambda half: src.at[half]
    )


def line_gather(kernel_id, rows, up):
    width = rows.shape[1]
    gathered, up_all = pl.pallas_call(
        line_gather_kernel,
        out_shape=(
            jax.ShapeDtypeStruct((2, 4, BLK, width), BF16),
            jax.ShapeDtypeStruct((4, 2, 128, 1152), BF16),
        ),
        in_specs=[VMEM] * 2,
        out_specs=(ANY,) * 2,
        scratch_shapes=[sems(18), sems(18), sems(2)],
        compiler_params=pltpu.CompilerParams(collective_id=kernel_id, has_side_effects=True),
    )(rows.reshape(2, BLK, width), up.reshape(2, 128, 1152))
    return gathered.reshape(ROWS, width), up_all.reshape(1024, 1152)


def line_gather_pack_kernel(
    src, gate, up, down, out, packed_y, packed_z,
    gu_own, gu_sib, down_own, down_sib, sends, recvs, loads,
):
    core = lax.axis_index("core")
    to_sib = {"core": 1 - core}
    views = [
        (lambda c: gate.at[:, :, c], gu_own.at[0], gu_sib.at[0]),
        (lambda c: up.at[:, :, c], gu_own.at[1], gu_sib.at[1]),
        (lambda c: down.at[:, c], down_own, down_sib),
    ]
    local = [
        pltpu.make_async_copy(view(core), mine, loads.at[i])
        for i, (view, mine, unused) in enumerate(views)
    ]
    local.append(pltpu.make_async_copy(src, out.at[:, lax.axis_index("x")], loads.at[3]))
    for copy in local:
        copy.start()
    meet(around(["x"]))
    send = Sends(sends, recvs)
    line = line_ring(send, src, out)
    line.begin()
    shared = [send(view(1 - core), theirs, to_sib) for view, unused, theirs in views]
    line.middle()
    for copy in local:
        copy.wait()
    for copy in shared:
        copy.wait_recv()

    def pack(y, unused):
        for z in range(4):
            for s in range(2):

                def put(rows, value):
                    if s == 0:
                        packed_y[y, z, rows, :] = value
                    else:
                        packed_z[z, y, rows, :] = value

                for t in range(9):
                    cols = slice(t * 128, (t + 1) * 128)
                    put(
                        slice(t * 32, (t + 1) * 32),
                        add_low(gu_own[s, y, z, :, cols], gu_sib[s, y, z, :, cols]),
                    )
                cols = slice(s * 512 + z * 128, s * 512 + (z + 1) * 128)
                put(slice(288, 432), add_low(down_own[y, :, cols], down_sib[y, :, cols]))
        return unused

    lax.fori_loop(0, 4, pack, 0)
    line.near()
    line.end()
    send.finish()


def line_gather_pack(kernel_id, rows, gate, up, down):
    def vm(*shape):
        return pltpu.VMEM(shape, BF16)

    gathered, packed_y, packed_z = pl.pallas_call(
        line_gather_pack_kernel,
        out_shape=(jax.ShapeDtypeStruct((2, 4, BLK, 1024), BF16),)
        + (jax.ShapeDtypeStruct((4, 4, FF_PIECE, 128), BF16),) * 2,
        in_specs=[VMEM] + [ANY] * 3,
        out_specs=(ANY, VMEM, VMEM),
        scratch_shapes=[
            vm(2, 4, 4, 32, 1152), vm(2, 4, 4, 32, 1152),
            vm(4, 144, 1024), vm(4, 144, 1024),
            sems(9), sems(9), sems(4),
        ],
        compiler_params=pltpu.CompilerParams(
            collective_id=kernel_id, has_side_effects=True, vmem_limit_bytes=40 * 2**20
        ),
    )(
        rows.reshape(2, BLK, 1024),
        gate.reshape(4, 4, 2, 32, 1152),
        up.reshape(4, 4, 2, 32, 1152),
        down.reshape(4, 2, 144, 1024),
    )
    return gathered.reshape(ROWS, 1024), packed_y, packed_z


def sequence_gather_kernel(
    kv, gate, out, kv_all, gate_all, out_all, sends, recvs, loads
):
    me_z, me_y = lax.axis_index("z"), lax.axis_index("dp")
    core = lax.axis_index("core")
    own = [
        pltpu.make_async_copy(kv, kv_all.at[me_z, core], loads.at[0]),
        pltpu.make_async_copy(gate, gate_all.at[me_y], loads.at[1]),
        pltpu.make_async_copy(out, out_all.at[me_y], loads.at[2]),
    ]
    for copy in own:
        copy.start()
    meet(around(["z", "dp"]))
    send = Sends(sends, recvs)
    run_gathers(
        [
            RingGather(
                send,
                "z",
                lambda place, core, half: kv_all.at[place, core, half],
                lambda half: kv.at[half],
                sibling=True,
                share_own=True,
            ),
            weight_gather(send, out, out_all, columns_half(512)),
            weight_gather(send, gate, gate_all, rows_half(64)),
        ]
    )
    for copy in own:
        copy.wait()
    send.finish()


def sequence_gather(kernel_id, kv, gate, out):
    kv_all, gate_all, out_all = pl.pallas_call(
        sequence_gather_kernel,
        out_shape=(
            jax.ShapeDtypeStruct((4, 2, 2, 2 * HD, ROWS), BF16),
            jax.ShapeDtypeStruct((4, 2, 128, 1152), BF16),
            jax.ShapeDtypeStruct((4, 2, 32, 1024), BF16),
        ),
        in_specs=[VMEM] * 3,
        out_specs=(ANY,) * 3,
        scratch_shapes=[sems(38), sems(38), sems(3)],
        compiler_params=pltpu.CompilerParams(collective_id=kernel_id, has_side_effects=True),
    )(kv, gate.reshape(2, 128, 1152), out.reshape(2, 32, 1024))
    return (
        kv_all.reshape(GROUPS, 2, 2 * HD, ROWS),
        gate_all.reshape(1024, 1152),
        out_all.reshape(256, 1024),
    )


def add_low(left, right):
    return (left.astype(F32) + right.astype(F32)).astype(BF16)


def line_scatter_kernel(rider, *refs):
    inputs, outputs = {None: (1, 1), "down": (2, 2), "pieces": (3, 3)}[rider]
    part, *riding = refs[:inputs]
    out, *riding_out = refs[inputs : inputs + outputs]
    pair, self_rows, far_in, left_in, right_in, sends, recvs, loads = refs[inputs + outputs :]
    me, right, far, left = ring("x")
    to_right, to_left = {"x": right}, {"x": left}
    local = [
        pltpu.make_async_copy(part.at[0, right], pair.at[0], loads.at[0]),
        pltpu.make_async_copy(part.at[1, left], pair.at[1], loads.at[1]),
        pltpu.make_async_copy(part.at[0, me], self_rows.at[0], loads.at[2]),
        pltpu.make_async_copy(part.at[1, me], self_rows.at[1], loads.at[3]),
    ]
    for i, (source, target) in enumerate(zip(riding, riding_out)):
        place = lax.axis_index("dp" if rider == "down" else ("z", "x")[i])
        local.append(pltpu.make_async_copy(source, target.at[place], loads.at[4 + i]))
    for copy in local:
        copy.start()
    if rider == "down":
        meet(around(["x", "dp"]))
    else:
        meet(around(["x", "z"] if rider else ["x"], sibling=False))
    send = Sends(sends, recvs)
    far0 = send(part.at[0, far], far_in.at[0], to_right)
    far1 = send(part.at[1, far], far_in.at[1], to_left)
    right1 = send(part.at[1, right], left_in.at[1], to_right)
    left0 = send(part.at[0, left], right_in.at[0], to_left)
    rings = []
    if rider == "down":
        rings = [weight_gather(send, riding[0], riding_out[0], columns_half(512))]
    elif rider == "pieces":
        rows = (pl.ds(0, 224), pl.ds(224, 208))
        rings = [
            RingGather(
                send,
                axis,
                lambda place, core, half, i=i: riding_out[i].at[place, rows[half]],
                lambda half, i=i: riding[i].at[rows[half]],
            )
            for i, axis in enumerate(("z", "x"))
        ]
    for gather in rings:
        gather.begin()
    local[0].wait()
    far0.wait_recv()
    pair[0] = add_low(pair[0], far_in[0])
    right0 = send(pair.at[0], left_in.at[0], to_right)
    local[1].wait()
    far1.wait_recv()
    pair[1] = add_low(pair[1], far_in[1])
    left1 = send(pair.at[1], right_in.at[1], to_left)
    for gather in rings:
        gather.middle()
    for gather in rings:
        gather.near()
    for copy in local[2:]:
        copy.wait()
    right1.wait_recv()
    left0.wait_recv()
    right0.wait_recv()
    left1.wait_recv()
    for h in range(2):
        out[h] = self_rows[h].astype(F32) + left_in[h].astype(F32) + right_in[h].astype(F32)
    for gather in rings:
        gather.end()
    for gather in rings:
        gather.finish()
    send.finish()


def line_scatter(kernel_id, partial, rider=None, riding=()):
    width = partial.shape[1]
    buffer = pltpu.VMEM((2, BLK, width), BF16)
    count = {None: 6, "down": 18, "pieces": 18}[rider]
    gathered = {None: (), "down": ((4, 2, 144, 1024),), "pieces": ((4, FF_PIECE, 128),) * 2}
    result = pl.pallas_call(
        functools.partial(line_scatter_kernel, rider),
        out_shape=(jax.ShapeDtypeStruct((2, BLK, width), F32),)
        + tuple(jax.ShapeDtypeStruct(shape, BF16) for shape in gathered[rider]),
        in_specs=[ANY] + [VMEM] * len(riding),
        out_specs=(VMEM,) + (ANY,) * len(riding),
        scratch_shapes=[buffer] * 5 + [sems(count), sems(count), sems(6)],
        compiler_params=pltpu.CompilerParams(
            collective_id=kernel_id, has_side_effects=True, vmem_limit_bytes=32 * 2**20
        ),
    )(partial.reshape(2, 4, BLK, width), *riding)
    summed = result[0].reshape(2 * BLK, width)
    return (summed, *result[1:]) if rider else summed


class RingSum:
    def __init__(self, send, axis, chunk, far_in, left_in, right_in):
        self.send, self.chunk = send, chunk
        self.far_in, self.left_in, self.right_in = far_in, left_in, right_in
        self.me, self.right, self.far, self.left = ring(axis)
        self.to_right, self.to_left = {axis: self.right}, {axis: self.left}

    def begin(self):
        send, chunk = self.send, self.chunk
        self.far0 = send(chunk(self.far, 0), self.far_in(0), self.to_right)
        self.far1 = send(chunk(self.far, 1), self.far_in(1), self.to_left)
        self.right1 = send(chunk(self.right, 1), self.left_in(1), self.to_right)
        self.left0 = send(chunk(self.left, 0), self.right_in(0), self.to_left)

    def middle(self):
        send, chunk = self.send, self.chunk
        self.far0.wait_recv()
        mine = chunk(self.right, 0)
        mine[...] = add_low(mine[...], self.far_in(0)[...])
        self.right0 = send(mine, self.left_in(0), self.to_right)
        self.far1.wait_recv()
        mine = chunk(self.left, 1)
        mine[...] = add_low(mine[...], self.far_in(1)[...])
        self.left1 = send(mine, self.right_in(1), self.to_left)

    def end(self, store):
        self.right1.wait_recv()
        self.left0.wait_recv()
        self.right0.wait_recv()
        self.left1.wait_recv()
        for h in range(2):
            store(
                h,
                self.chunk(self.me, h)[...].astype(F32)
                + self.left_in(h)[...].astype(F32)
                + self.right_in(h)[...].astype(F32),
            )


class PieceSums:
    def __init__(
        self, send, packed, far_a, left_a, right_a, mid, far_b, left_b, right_b, rows, order
    ):
        self.send, self.mid = send, mid
        two = (pl.ds(0, 2), pl.ds(2, 2))
        chunks = (
            lambda place, h: packed.at[0, place, two[h]],
            lambda place, h: packed.at[(1, two[h], place) if order else (1, place, two[h])],
        )
        self.first = [
            RingSum(
                send,
                axis,
                chunks[s],
                lambda h, s=s: far_a.at[s, h],
                lambda h, s=s: left_a.at[s, h],
                lambda h, s=s: right_a.at[s, h],
            )
            for s, axis in enumerate(("dp", "z"))
        ]
        self.second = [
            RingSum(
                send,
                axis,
                lambda place, h, s=s: mid.at[s, place, rows[h]],
                lambda h, s=s: far_b.at[s, rows[h]],
                lambda h, s=s: left_b.at[s, rows[h]],
                lambda h, s=s: right_b.at[s, rows[h]],
            )
            for s, axis in enumerate(("z", "dp"))
        ]

    def begin(self):
        for step in self.first:
            step.begin()

    def middle(self):
        for step in self.first:
            step.middle()

    def turn(self):
        for s in range(2):

            def keep(h, value, s=s):
                self.mid[s, 2 * h : 2 * h + 2] = value.astype(BF16)

            self.first[s].end(keep)
            self.second[s].begin()

    def late(self):
        for step in self.second:
            step.middle()

    def end(self, keep):
        for s in range(2):
            self.second[s].end(functools.partial(keep, s))


def piece_buffers(rows):
    def vm(*shape):
        return pltpu.VMEM(shape, BF16)

    return (
        [vm(2, 4, 4, rows, 128)]
        + [vm(2, 2, 2, rows, 128)] * 3
        + [vm(2, 4, rows, 128)]
        + [vm(2, rows, 128)] * 3
    )


def attend_back_kernel(
    q_ref, kv_ref, qo_ref, ko_ref, mixed_ref, log_ref, grad_ref, packed_y, packed_z,
    dq_ref, dkv_ref, piece_ref,
    dkv_acc, packed, far_a, left_a, right_a, mid, far_b, left_b, right_b, sends, recvs, loads,
):
    local = [
        pltpu.make_async_copy(source, packed.at[i], loads.at[i])
        for i, source in enumerate((packed_y, packed_z))
    ]
    for copy in local:
        copy.start()
    meet(around(["dp", "z"], sibling=False))
    for copy in local:
        copy.wait()
    shares = (pl.ds(0, 224), pl.ds(224, 208))
    sums = PieceSums(
        Sends(sends, recvs), packed, far_a, left_a, right_a, mid, far_b, left_b, right_b, shares, 0
    )
    sums.begin()

    dkv_acc[...] = jnp.zeros_like(dkv_acc)
    for half in range(2):
        cols = slice(half * HALF, (half + 1) * HALF)
        q_order = jnp.concatenate([qo_ref[:, cols]] * 2, axis=1)
        queries = [head_pair(q_ref, kv_head, cols) for kv_head in range(2)]
        grads = [head_pair(grad_ref, kv_head, cols) for kv_head in range(2)]
        logs = [
            jnp.concatenate([log_ref[at : at + 1, cols], log_ref[at + 1 : at + 2, cols]], axis=1)
            for at in (0, 2)
        ]
        dots = [
            jnp.sum(
                head_pair(mixed_ref, kv_head, cols) * grads[kv_head].astype(F32),
                axis=0,
                keepdims=True,
            )
            for kv_head in range(2)
        ]

        def group(g, carried):
            carried = list(carried)
            for k_half in range(half + 1):
                keys = slice(k_half * HALF, (k_half + 1) * HALF)
                for kv_head in range(2):
                    q_t, grad_t = queries[kv_head], grads[kv_head]
                    k_t = kv_ref[g, kv_head, 0:HD, keys]
                    v_t = kv_ref[g, kv_head, HD : 2 * HD, keys]
                    probs = jnp.exp2(scores_of(k_t, q_t) * EXP2_SCALE - logs[kv_head])
                    if k_half == half:
                        allowed = ko_ref[g, keys, :] <= q_order
                        probs = jnp.where(allowed, probs, 0.0)
                    score_grad = (probs * (scores_of(v_t, grad_t) - dots[kv_head])).astype(BF16)
                    dkv_acc[g, kv_head, HD : 2 * HD, keys] += dot(
                        grad_t, probs.astype(BF16), 1, 1
                    )
                    dkv_acc[g, kv_head, 0:HD, keys] += dot(q_t, score_grad, 1, 1)
                    carried[kv_head] = carried[kv_head] + dot(k_t, score_grad)
            return tuple(carried)

        start = jnp.zeros((HD, 2 * HALF), F32)
        if half == 0:
            query_grads = lax.fori_loop(0, GROUPS, group, (start, start))
            sums.middle()
        else:
            query_grads = lax.fori_loop(0, GROUPS // 2, group, (start, start))
            sums.turn()
            query_grads = lax.fori_loop(GROUPS // 2, GROUPS, group, query_grads)
        for kv_head, dq in enumerate(query_grads):
            for head in range(2):
                at = 2 * kv_head + head
                rows = slice(at * HD, (at + 1) * HD)
                dq_ref[rows, cols] = dq[:, head * HALF : (head + 1) * HALF] * SCORE_SCALE

    def finish(g, unused):
        for kv_head in range(2):
            dkv_ref[g, kv_head, 0:HD, :] = (dkv_acc[g, kv_head, 0:HD, :] * SCORE_SCALE).astype(
                BF16
            )
            dkv_ref[g, kv_head, HD : 2 * HD, :] = dkv_acc[g, kv_head, HD : 2 * HD, :].astype(BF16)
        return unused

    sums.late()
    lax.fori_loop(0, GROUPS, finish, 0)

    def keep(s, half, value):
        piece_ref[s, shares[half], :] = value.astype(BF16)

    sums.end(keep)
    sums.send.finish()


def attend_back(kernel_id, q_t, kv_all, q_order, k_order, mixed, log_total, mixed_grad, packed):
    return pl.pallas_call(
        attend_back_kernel,
        out_shape=(
            jax.ShapeDtypeStruct((4 * HD, ROWS), F32),
            jax.ShapeDtypeStruct((GROUPS, 2, 2 * HD, ROWS), BF16),
            jax.ShapeDtypeStruct((2, FF_PIECE, 128), BF16),
        ),
        in_specs=[VMEM] * 7 + [ANY] * 2,
        out_specs=(VMEM,) * 3,
        scratch_shapes=[pltpu.VMEM((GROUPS, 2, 2 * HD, ROWS), F32)]
        + piece_buffers(FF_PIECE)
        + [sems(24), sems(24), sems(2)],
        compiler_params=pltpu.CompilerParams(
            collective_id=kernel_id, has_side_effects=True, vmem_limit_bytes=48 * 2**20
        ),
    )(q_t, kv_all, q_order, k_order, mixed, log_total, mixed_grad, *packed)


def sequence_scatter_kernel(
    part, out, own, other, far_in, left_in, right_in, sends, recvs, loads
):
    core = lax.axis_index("core")
    me, right, far, left = ring("z")
    order = (far, right, left, me)
    local = [
        pltpu.make_async_copy(part.at[place, core], own.at[place], loads.at[i])
        for i, place in enumerate(order)
    ]
    for copy in local:
        copy.start()
    to_sib = {"core": 1 - core}
    meet([{"z": right}, {"z": left}, to_sib])
    send = Sends(sends, recvs)
    shared = [send(part.at[place, 1 - core], other.at[place], to_sib) for place in order]

    def merge(i):
        local[i].wait()
        shared[i].wait_recv()
        own[order[i]] = add_low(own[order[i]], other[order[i]])

    ring_sum = RingSum(
        send,
        "z",
        lambda place, h: own.at[place, h],
        lambda h: far_in.at[h],
        lambda h: left_in.at[h],
        lambda h: right_in.at[h],
    )
    for i in range(3):
        merge(i)
    ring_sum.begin()
    merge(3)
    ring_sum.middle()

    def store(h, value):
        out[h] = value

    ring_sum.end(store)
    send.finish()


def sequence_scatter(kernel_id, partial):
    buffer = pltpu.VMEM((2, 2 * HD, ROWS), BF16)
    wide = pltpu.VMEM((4, 2, 2 * HD, ROWS), BF16)
    return pl.pallas_call(
        sequence_scatter_kernel,
        out_shape=jax.ShapeDtypeStruct((2, 2 * HD, ROWS), F32),
        in_specs=[ANY],
        out_specs=VMEM,
        scratch_shapes=[wide, wide, buffer, buffer, buffer]
        + [
            pltpu.SemaphoreType.DMA((10,)),
            pltpu.SemaphoreType.DMA((10,)),
            pltpu.SemaphoreType.DMA((4,)),
        ],
        compiler_params=pltpu.CompilerParams(
            collective_id=kernel_id, has_side_effects=True, vmem_limit_bytes=32 * 2**20
        ),
    )(partial.reshape(4, 2, 2, 2 * HD, ROWS))


def grads_kernel(
    qkv, out, gains, ff_a, ff_b, result, gain_sums, ff_out,
    qkv_own, qkv_sib, out_own, out_sib, gain_slots,
    packed, far_a, left_a, right_a, mid, far_b, left_b, right_b,
    sends, recvs, loads,
):
    core = lax.axis_index("core")
    to_sib = {"core": 1 - core}
    views = [
        (lambda c: qkv.at[:, :, c], qkv_own, qkv_sib),
        (lambda c: out.at[:, c], out_own, out_sib),
    ]
    local = [
        pltpu.make_async_copy(view(core), mine, loads.at[i])
        for i, (view, mine, unused) in enumerate(views)
    ]
    local += [
        pltpu.make_async_copy(
            ff_a, ff_out.at[0, core, :, lax.axis_index("x")], loads.at[2]
        ),
        pltpu.make_async_copy(ff_b, ff_out.at[1, core, lax.axis_index("z")], loads.at[3]),
    ]
    for copy in local:
        copy.start()
    peers = {axis: [{axis: place} for place in ring(axis)[1:]] for axis in ("z", "dp", "x")}
    meet(peers["z"] + peers["dp"] + peers["x"] + [to_sib])
    send = Sends(sends, recvs)

    def gain_begin(step, axis, value):
        place = lax.axis_index(axis)
        gain_slots[step, place] = value
        slot = gain_slots.at[step, place]
        return [send(slot, slot, to) for to in ([to_sib] if axis == "core" else peers[axis])]

    def gain_end(step, copies):
        for copy in copies:
            copy.wait_recv()
        total = gain_slots[step, 0] + gain_slots[step, 1]
        for place in range(2, 4 if step else 2):
            total = total + gain_slots[step, place]
        return total

    gain_copies = gain_begin(0, "core", gains[...])
    shared = [send(view(1 - core), theirs, to_sib) for view, unused, theirs in views]
    two = (pl.ds(0, 2), pl.ds(2, 2))
    bulk = [
        RingGather(
            send,
            "x",
            lambda place, core, half: ff_out.at[0, core, two[half], place],
            lambda half: ff_a.at[two[half]],
            sibling=True,
            share_own=True,
        ),
        RingGather(
            send,
            "z",
            lambda place, core, half: ff_out.at[1, core, place, two[half]],
            lambda half: ff_b.at[two[half]],
            sibling=True,
            share_own=True,
        ),
    ]
    for gather in bulk:
        gather.begin()
    for copy in local:
        copy.wait()
    for copy in shared:
        copy.wait_recv()

    def pack(y, unused):
        for z in range(4):
            for s in range(2):
                for t in range(2):
                    cols = slice(s * 256 + t * 128, s * 256 + (t + 1) * 128)
                    packed[s, y, z, t * 32 : (t + 1) * 32, :] = add_low(
                        qkv_own[y, z, :, cols], qkv_sib[y, z, :, cols]
                    )
                cols = slice(s * 512 + z * 128, s * 512 + (z + 1) * 128)
                packed[s, y, z, 64:96, :] = add_low(out_own[y, :, cols], out_sib[y, :, cols])
        return unused

    lax.fori_loop(0, 4, pack, 0)
    rows = (pl.ds(0, 48), pl.ds(48, 48))
    sums = PieceSums(
        send, packed, far_a, left_a, right_a, mid, far_b, left_b, right_b, rows, 1
    )
    sums.begin()
    gain_copies = gain_begin(1, "z", gain_end(0, gain_copies))
    sums.middle()
    for gather in bulk:
        gather.middle()
    gain_copies = gain_begin(2, "dp", gain_end(1, gain_copies))
    sums.turn()
    gain_copies = gain_begin(3, "x", gain_end(2, gain_copies))
    for gather in bulk:
        gather.near()
    sums.late()

    def keep(s, half, value):
        result[s, rows[half], :] = value.astype(BF16)

    sums.end(keep)
    gain_sums[...] = gain_end(3, gain_copies)
    for gather in bulk:
        gather.end()
    for gather in bulk:
        gather.finish()
    send.finish()


def sum_grads(kernel_id, qkv, out, gains, ff_a, ff_b):
    def vm(*shape):
        return pltpu.VMEM(shape, BF16)

    return pl.pallas_call(
        grads_kernel,
        out_shape=(
            jax.ShapeDtypeStruct((2, PIECE, 128), BF16),
            jax.ShapeDtypeStruct((24, 128), F32),
            jax.ShapeDtypeStruct((2, 2, 4, 4, FF_PIECE, 128), BF16),
        ),
        in_specs=[ANY] * 2 + [VMEM] * 3,
        out_specs=(VMEM, VMEM, ANY),
        scratch_shapes=[
            vm(4, 4, 32, 512), vm(4, 4, 32, 512),
            vm(4, 32, 1024), vm(4, 32, 1024),
            pltpu.VMEM((4, 4, 24, 128), F32),
        ]
        + piece_buffers(PIECE)
        + [sems(64), sems(64), sems(4)],
        compiler_params=pltpu.CompilerParams(
            collective_id=kernel_id, has_side_effects=True, vmem_limit_bytes=48 * 2**20
        ),
    )(qkv.reshape(4, 4, 2, 32, 512), out.reshape(4, 2, 32, 1024), gains, ff_a, ff_b)


class RingCopy:
    def __init__(self, send, axis, place_of):
        self.send, self.at = send, place_of
        self.me, self.right, self.far, self.left = ring(axis)
        self.to_right, self.to_left = {axis: self.right}, {axis: self.left}

    def begin(self):
        me = self.me
        self.right0 = self.send(self.at(me, 0), self.at(me, 0), self.to_right)
        self.left1 = self.send(self.at(me, 1), self.at(me, 1), self.to_left)
        self.right1 = self.send(self.at(me, 1), self.at(me, 1), self.to_right)
        self.left0 = self.send(self.at(me, 0), self.at(me, 0), self.to_left)

    def middle(self):
        self.right0.wait_recv()
        self.far0 = self.send(self.at(self.left, 0), self.at(self.left, 0), self.to_right)
        self.left1.wait_recv()
        self.far1 = self.send(self.at(self.right, 1), self.at(self.right, 1), self.to_left)

    def near(self):
        self.right1.wait_recv()
        self.left0.wait_recv()

    def end(self):
        self.far0.wait_recv()
        self.far1.wait_recv()


def spread_kernel(piece, out, sends, recvs, loads):
    core = lax.axis_index("core")
    me_x, me_z = lax.axis_index("x"), lax.axis_index("z")
    to_sib = {"core": 1 - core}
    own = [
        pltpu.make_async_copy(piece.at[s], out.at[s, core, me_z, me_x], loads.at[s])
        for s in range(2)
    ]
    for copy in own:
        copy.start()
    meet(around(["x", "z"]))
    send = Sends(sends, recvs)
    rows = (pl.ds(0, 48), pl.ds(48, 48))
    two = (pl.ds(0, 2), pl.ds(2, 2))
    first = [
        RingCopy(send, "z", lambda place, h: out.at[0, core, place, me_x, rows[h]]),
        RingCopy(send, "x", lambda place, h: out.at[1, core, me_z, place, rows[h]]),
    ]
    second = [
        RingCopy(send, "x", lambda place, h: out.at[0, core, two[h], place]),
        RingCopy(send, "z", lambda place, h: out.at[1, core, place, two[h]]),
    ]
    shared = []

    def share(s, place):
        view = out.at[0, core, :, place] if s == 0 else out.at[1, core, place]
        shared.append(send(view, view, to_sib))

    for copy in own:
        copy.wait()
    for step in first:
        step.begin()
    for step in first:
        step.middle()
    for s in range(2):
        first[s].near()
        first[s].end()
        second[s].begin()
        share(s, second[s].me)
    for step in second:
        step.middle()
    for s in range(2):
        second[s].near()
        share(s, second[s].left)
        share(s, second[s].right)
    for s in range(2):
        second[s].end()
        share(s, second[s].far)
    for copy in shared:
        copy.wait_recv()
    send.finish()


def spread(kernel_id, piece):
    return pl.pallas_call(
        spread_kernel,
        out_shape=jax.ShapeDtypeStruct((2, 2, 4, 4, PIECE, 128), BF16),
        in_specs=[VMEM],
        out_specs=ANY,
        scratch_shapes=[sems(32), sems(32), sems(2)],
        compiler_params=pltpu.CompilerParams(collective_id=kernel_id, has_side_effects=True),
    )(piece)


def unpack_rows_kernel(ff_pieces, pieces, gate, up, query, key, value):
    for x in range(4):
        for t in range(9):
            cols = slice(x * 1152 + t * 128, x * 1152 + (t + 1) * 128)
            gate[:, cols] = ff_pieces[0, 0, 0, x, t * 32 : (t + 1) * 32, :].astype(F32)
            up[:, cols] = ff_pieces[1, 0, 0, x, t * 32 : (t + 1) * 32, :].astype(F32)
        for t in range(2):
            cols = slice(x * 256 + t * 128, x * 256 + (t + 1) * 128)
            query[:, cols] = pieces[0, 0, 0, x, t * 32 : (t + 1) * 32, :].astype(F32)
        cols = slice(x * 128, (x + 1) * 128)
        key[:, cols] = pieces[1, 0, 0, x, 0:32, :].astype(F32)
        value[:, cols] = pieces[1, 0, 0, x, 32:64, :].astype(F32)


def unpack_columns_kernel(ff_pieces, pieces, down, out):
    for s in range(2):
        for z in range(4):
            cols = slice(s * 512 + z * 128, s * 512 + (z + 1) * 128)
            down[:, cols] = ff_pieces[s, 0, z, 0].astype(F32)
            out[:, cols] = pieces[s, 0, z, 0].astype(F32)


def unpack(ff_pieces, pieces):
    rows = pl.pallas_call(
        unpack_rows_kernel,
        grid=(4, 2),
        out_shape=tuple(
            jax.ShapeDtypeStruct((256, width), F32) for width in (4608, 4608, 1024, 512, 512)
        ),
        in_specs=[
            pl.BlockSpec((2, 1, 1, 4, 288, 128), lambda z, c: (0, c, z, 0, 0, 0)),
            pl.BlockSpec((2, 1, 1, 4, PIECE, 128), lambda z, c: (0, c, z, 0, 0, 0)),
        ],
        out_specs=tuple(
            pl.BlockSpec((32, width), lambda z, c: (2 * z + c, 0))
            for width in (4608, 4608, 1024, 512, 512)
        ),
        compiler_params=pltpu.CompilerParams(vmem_limit_bytes=32 * 2**20),
    )(ff_pieces, pieces)
    columns = pl.pallas_call(
        unpack_columns_kernel,
        grid=(4, 2),
        out_shape=(
            jax.ShapeDtypeStruct((1152, 1024), F32),
            jax.ShapeDtypeStruct((256, 1024), F32),
        ),
        in_specs=[
            pl.BlockSpec((2, 1, 4, 1, 144, 128), lambda x, c: (0, c, 0, x, 2, 0)),
            pl.BlockSpec((2, 1, 4, 1, 32, 128), lambda x, c: (0, c, 0, x, 2, 0)),
        ],
        out_specs=(
            pl.BlockSpec((144, 1024), lambda x, c: (2 * x + c, 0)),
            pl.BlockSpec((32, 1024), lambda x, c: (2 * x + c, 0)),
        ),
        compiler_params=pltpu.CompilerParams(vmem_limit_bytes=32 * 2**20),
    )(ff_pieces, pieces)
    return rows + columns


def after(value, anchor):
    return lax.optimization_barrier((value, anchor))[0]


SWAP = [(a * 4 + b, b * 4 + a) for a in range(4) for b in range(4)]


def on_device(
    hidden_in,
    positions,
    block_of,
    attn_gain,
    query_weight,
    key_weight,
    value_weight,
    out_weight,
    query_gain,
    key_gain,
    ffn_gain,
    gate_weight,
    up_weight,
    down_weight,
    cotangent,
):
    z_at = lax.axis_index("z")
    x_at = lax.axis_index("x")
    core_at = lax.axis_index("core")
    dp_at = lax.axis_index("dp")

    hidden_rows = hidden_in[0]
    grad_rows = cotangent[0]

    in_block = jnp.arange(BLK, dtype=jnp.int32)
    blocks = block_of.reshape(4, 4, 2, 2).transpose(0, 2, 3, 1)
    order_all = (blocks[..., None] * BLK + in_block).reshape(GROUPS, ROWS)
    own_order = lax.dynamic_index_in_dim(order_all, z_at * 2 + core_at, 0, keepdims=True)
    k_order = order_all.reshape(GROUPS, ROWS, 1)
    own_slot = 2 * (z_at * 8 + x_at * 2 + core_at)
    first_block = lax.dynamic_index_in_dim(block_of, own_slot, 0, keepdims=False)
    offset = positions[0, 0] - first_block * BLK
    frequency = ROPE_BASE ** (-2.0 * jnp.arange(HD // 2, dtype=F32) / HD)
    angles = (own_order + offset).astype(F32) * frequency[:, None]
    cosine, sine = jnp.cos(angles), jnp.sin(angles)

    def columns(weight, width):
        return lax.dynamic_slice_in_dim(weight, x_at * width, width, axis=1)

    def swapped_rows(weight, rows):
        own = lax.dynamic_slice_in_dim(weight, x_at * rows, rows, axis=0)
        return lax.ppermute(own, ("dp", "x"), SWAP)

    gains_own = jnp.pad(
        jnp.concatenate([attn_gain, ffn_gain, query_gain, key_gain]), (0, 2048 - 544)
    )
    qkv_own = jnp.concatenate(
        [columns(query_weight, 256), columns(key_weight, 128), columns(value_weight, 128)],
        axis=1,
    )

    hidden = hidden_rows.astype(F32)
    line_hidden, qkv_weight, gains = start_gather(
        0, hidden_rows, qkv_own, gains_own.reshape(16, 128)
    )
    gains = gains.reshape(4, 2048).astype(F32)
    attn_gain_all = gains[:, 0:256].reshape(1024)
    ffn_gain_all = gains[:, 256:512].reshape(1024)
    query_gain_all = gains[:, 512:528].reshape(HD)
    key_gain_all = gains[:, 528:544].reshape(HD)
    out_own = swapped_rows(after(out_weight, line_hidden), 64)
    down_own = swapped_rows(after(down_weight, line_hidden), 288)
    branch_low = lax.all_gather(after(grad_rows, line_hidden).reshape(2, BLK, 1024), "x", axis=1).reshape(ROWS, 1024)
    attn_in = rms_scale(line_hidden.astype(F32), attn_gain_all).astype(BF16)
    qkv_t = dot(qkv_weight, attn_in, 0, 1)
    q_rot, q_back = jax.vjp(
        lambda r, g: head_norm_rope(r, g, cosine, sine),
        qkv_t[0:256].reshape(4, HD, ROWS),
        query_gain_all,
    )
    k_rot, k_back = jax.vjp(
        lambda r, g: head_norm_rope(r, g, cosine, sine),
        qkv_t[256:384].reshape(2, HD, ROWS),
        key_gain_all,
    )
    q_low = q_rot.reshape(4 * HD, ROWS).astype(BF16)
    kv_low = jnp.concatenate([k_rot, qkv_t[384:512].reshape(2, HD, ROWS)], axis=1).astype(BF16)
    kv_all, gate_slice, out_slice = sequence_gather(
        1, kv_low, columns(gate_weight, 1152), out_own
    )
    mixed, attn_low, log_total = attend(q_low, kv_all, own_order, k_order)
    attn_rows, down_slice = line_scatter(
        2, dot(attn_low, out_slice, 0, 0).astype(BF16), "down", (down_own.reshape(2, 144, 1024),)
    )
    down_slice = down_slice.reshape(1152, 1024)
    after_attn = hidden + attn_rows
    normed_ffn, norm_ffn_back = jax.vjp(rms_scale, after_attn, ffn_gain_all)
    ffn_in, up_slice = line_gather(3, normed_ffn.astype(BF16), columns(up_weight, 1152))
    gate_proj = dot(ffn_in, gate_slice)
    up_proj = dot(ffn_in, up_slice)
    activated, swiglu_back = jax.vjp(lambda g, u: jax.nn.silu(g) * u, gate_proj, up_proj)
    activated_low = activated.astype(BF16)
    residual_grad = grad_rows.astype(F32)
    activated_grad = dot(branch_low, down_slice, 1, 1)
    gate_grad, up_grad = swiglu_back(activated_grad)
    gate_grad_low = gate_grad.astype(BF16)
    up_grad_low = up_grad.astype(BF16)
    ffn_in_grad = line_scatter(
        5,
        (dot(gate_grad_low, gate_slice, 1, 1) + dot(up_grad_low, up_slice, 1, 1)).astype(BF16),
    )
    mid_part, ffn_gain_part = norm_ffn_back(ffn_in_grad)
    mid_grad = residual_grad + mid_part
    branch_attn, packed_y, packed_z = line_gather_pack(
        6,
        mid_grad.astype(BF16),
        dot(ffn_in, gate_grad_low, 0, 0).astype(BF16),
        dot(ffn_in, up_grad_low, 0, 0).astype(BF16),
        dot(activated_low, branch_low, 0, 0).astype(BF16),
    )
    branch_attn, late_activated = lax.optimization_barrier((branch_attn, activated_low))
    out_part = dot(late_activated, down_slice).astype(BF16).reshape(2, 4, BLK, 1024)
    branch_attn, out_part = lax.optimization_barrier((branch_attn, out_part))
    layer_out = (
        after_attn
        + lax.psum_scatter(
            out_part.transpose(1, 0, 2, 3).reshape(ROWS, 1024),
            "x",
            scatter_dimension=0,
            tiled=True,
        ).astype(F32)
    ).astype(BF16)

    mixed_grad = dot(out_slice, branch_attn, 1, 1).astype(BF16)
    q_grad, kv_grad_all, ff_piece = attend_back(
        11, q_low, kv_all, own_order, k_order, mixed, log_total, mixed_grad, (packed_y, packed_z)
    )
    ff_swapped = lax.ppermute(ff_piece[:, 288:], ("dp", "x"), SWAP)
    ff_piece = jnp.concatenate([ff_piece[:, :288], ff_swapped], axis=1)
    kv_grad = sequence_scatter(7, kv_grad_all)
    q_pre, q_gain_part = q_back(q_grad.reshape(4, HD, ROWS))
    k_pre, k_gain_part = k_back(kv_grad[:, 0:HD])
    qkv_pre = jnp.concatenate(
        [
            q_pre.reshape(4 * HD, ROWS),
            k_pre.reshape(2 * HD, ROWS),
            kv_grad[:, HD:].reshape(2 * HD, ROWS),
        ],
        axis=0,
    ).astype(BF16)
    attn_in_grad, ff_a, ff_b = line_scatter(
        8,
        dot(qkv_pre, qkv_weight, 0, 1).astype(BF16),
        "pieces",
        (ff_piece[0], ff_piece[1]),
    )
    unused, norm_attn_back = jax.vjp(rms_scale, hidden, attn_gain_all)
    hidden_part, attn_gain_part = norm_attn_back(attn_in_grad)
    input_grad = (mid_grad + hidden_part).astype(BF16)

    gain_parts = jnp.concatenate([attn_gain_part, ffn_gain_part, q_gain_part, k_gain_part])
    gain_parts = jnp.pad(gain_parts, (0, 3072 - 2176)).reshape(24, 128)

    def own_slice(begin, size):
        return lax.dynamic_slice_in_dim(
            gain_sums[begin : begin + size], dp_at * (size // 4), size // 4
        )

    own_piece, gain_sums, ff_pieces = sum_grads(
        9,
        dot(attn_in, qkv_pre, 0, 1).astype(BF16),
        dot(attn_low, branch_attn).astype(BF16),
        gain_parts,
        ff_a,
        ff_b,
    )
    gain_sums = gain_sums.reshape(3072)
    swapped = lax.ppermute(own_piece[:, 64:], ("dp", "x"), SWAP)
    pieces = spread(10, jnp.concatenate([own_piece[:, :64], swapped], axis=1))
    gate_all, up_all, query_all, key_all, value_all, down_all, out_all = unpack(ff_pieces, pieces)
    return (
        layer_out[None],
        input_grad[None],
        own_slice(0, 1024),
        query_all,
        key_all,
        value_all,
        out_all,
        own_slice(2048, 64),
        own_slice(2112, 64),
        own_slice(1024, 1024),
        gate_all,
        up_all,
        down_all,
    )


def solution(mesh):
    fine = Mesh(mesh.devices.reshape(4, 4, 4, 2), ("dp", "z", "x", "core"))
    ctx = ("z", "x", "core")
    rows = P("dp", ctx, None)
    vector, matrix = P("dp"), P("dp", None)
    return jax.shard_map(
        on_device,
        mesh=fine,
        in_specs=(rows, P("dp", ctx), P(), vector)
        + (matrix,) * 4
        + (vector,) * 3
        + (matrix,) * 3
        + (rows,),
        out_specs=(rows, rows, vector) + (matrix,) * 4 + (vector,) * 3 + (matrix,) * 3,
        check_vma=False,
    )
```

time: 479 us -> 366 us (0.76)
  blocking collectives: 104 us -> 0 us
  Pallas kernels: 274 us -> 258 us
  other arithmetic: 12.3 us -> 22.7 us
  matrix products: 35.2 us -> 26.4 us
  local copies, waits for them, and re-layouts: 28.7 us -> 34.6 us
    psum x1 -> x0, blocking collectives: 64.2 us -> none  [on_device(): lax.psum(jnp.concatenate([attn_gain_part, ffn_gain_part, q_gain_part, k_g...]
    unnamed x1 -> x0, blocking collectives: 25.6 us -> none
    pallas_call x1, Pallas kernels: 45.2 us -> 24.1 us  [spread(): pl.pallas_call(spread_kernel, out_shape=jax.ShapeDtypeStruct((2, 2, 4, 4,...]
    all_gather x1 -> x0, blocking collectives: 13.7 us -> none  [swapped_rows(): lax.all_gather(lax.ppermute(own, ('dp', 'x'), SWAP), 'dp', axis=0, tiled=...]
    dot_general x12 -> x15, matrix products: 35.2 us -> 26.4 us  [dot(): lax.dot_general(left, right, (((left_dim,), (right_dim,)), ((), ())), pre...]
    pallas_call x9 -> x8, Pallas kernels: 154 us -> 160 us  [the longest x3 54.4 us: line_scatter(): pl.pallas_call(functools.partial(line_scatter_kernel, rider), out_shape=(...]
    unnamed x144 -> x134, local copies, waits for them, and re-layouts: 15.4 us -> 12.6 us
  transfers between devices with their start and end apart: 6 -> 6, of which waited for: 0 -> 0; matrix products, arithmetic and copies ran while one was open for 6% -> 12% of each run, Pallas kernels for 18% -> 27%
where the time goes in v3:
time: 366 us; the launch traced here: 365 us
  Pallas kernels  258 us (70%)
  local copies, waits for them, and re-layouts  34.6 us (9%)
  matrix products  26.4 us (7%)
  other arithmetic  22.7 us (6%)
  between operations  15.9 us (4%)
  starting transfers between devices  6.73 us (2%)
    pallas_call x3, Pallas kernels, line_scatter(): pl.pallas_call(functools.partial(line_scatter_kernel, rider), out_shape=(...  54.4 us
    pallas_call x1, Pallas kernels, attend_back(): pl.pallas_call(attend_back_kernel, out_shape=(jax.ShapeDtypeStruct((4 * H...  34.2 us
    pallas_call x1, Pallas kernels, sum_grads(): pl.pallas_call(grads_kernel, out_shape=(jax.ShapeDtypeStruct((2, PIECE, 1...  31.9 us
    dot_general x15, matrix products, dot(): lax.dot_general(left, right, (((left_dim,), (right_dim,)), ((), ())), pre...  26.4 us
    pallas_call x1, Pallas kernels, sequence_gather(): pl.pallas_call(sequence_gather_kernel, out_shape=(jax.ShapeDtypeStruct((4...  25.9 us
    pallas_call x1, Pallas kernels, spread(): pl.pallas_call(spread_kernel, out_shape=jax.ShapeDtypeStruct((2, 2, 4, 4,...  24.1 us
    pallas_call x1, Pallas kernels, start_gather(): pl.pallas_call(start_kernel, out_shape=(jax.ShapeDtypeStruct((2, 4, BLK,...  17.4 us
    pallas_call x1, Pallas kernels, line_gather(): pl.pallas_call(line_gather_kernel, out_shape=(jax.ShapeDtypeStruct((2, 4,...  17 us
  transfers between devices with their start and end apart: 6, of which 0 were waited for; matrix products, arithmetic and copies ran while one was open for 12% of the time, Pallas kernels for 27%

profile of v3, /device:TPU:1, one launch (start us, length us, event | category | flops | bytes accessed | tf_op | source)
XLA Modules:
  0.0 364.6 jit_solution(1250990233998878961)
XLA Ops:
  7.2 1.1 constant_dynamic-slice_fusion.6
  8.3 0.9 constant_dynamic-slice_fusion.4
  9.2 0.7 pad_maximum_fusion.1
  9.9 1.4 fusion.39.gains
  11.3 17.4 %shard_map.246 = (bf16[2,4,64,1024]{3,2,1,0:T(8,128)(2,1)}, bf16[4,2,128,512]{3,2,1,0:T(8,128)(2,1)}, bf16[4,16,128]{2,1,0:T(8,128)(2,1)}) custom-call(bf16[2,64,1024]{2,1,0:T(8,128)(2,1)} %bitcast.168, bf16[2,128,512]{2,1,0:T(8,128)(2,1)} %bitcast.186, bf16[16,128]{1,0:T(8,128)(2,1)} %fusion.39.gains), custom_call_target="tpu_custom_call" | custom-call | tf_op jit(solution)/shard_map/pallas_call | solution.py:281
  28.7 1.7 constant_dynamic-slice_fusion.2
  30.4 2.2 collective-permute-start
  32.5 0.9 constant_dynamic-slice_fusion.1
  33.4 1.7 collective-permute-start.1
  35.2 0.7 convert_bitcast_fusion.1
  37.5 2.0 fusion.48
  40.1 3.4 add.248
  45.8 0.7 subtract_convert_fusion.1
  46.4 1.8 broadcast_add_fusion.ko_ref
  48.3 2.6 constant_dynamic-slice_fusion.3
  50.9 1.9 constant_dynamic-slice_fusion
  52.9 0.7 rsqrt.66
  53.6 1.6 pad_maximum_fusion.3.kv
  55.1 25.9 %shard_map.247 = (bf16[4,2,2,128,512]{4,3,2,1,0:T(8,128)(2,1)}, bf16[4,2,128,1152]{3,2,1,0:T(8,128)(2,1)}, bf16[4,2,32,1024]{3,2,1,0:T(8,128)(2,1)}) custom-call(bf16[2,128,512]{2,1,0:T(8,128)(2,1)} %pad_maximum_fusion.3.kv, bf16[2,128,1152]{2,1,0:T(8,128)(2,1)} %bitcast.179, bf16[2,32,1024]{2,1,0:T(8,128)(2,1)} %bitcast.16.out), custom_call_target="tpu_custom_call" | custom-call | tf_op jit(solution)/shard_map/pallas_call | solution.py:454
  81.1 1.6 copy-done.6
  82.7 14.8 %shard_map.248 = (f32[256,512]{1,0:T(8,128)S(1)}, bf16[256,512]{1,0:T(8,128)(2,1)S(1)}, f32[4,512]{1,0:T(4,128)S(1)}) custom-call(bf16[256,512]{1,0:T(8,128)(2,1)S(1)} %bitcast.159, bf16[8,2,128,512]{3,2,1,0:T(8,128)(2,1)S(1)} %bitcast.157, s32[1,512]{1,0:T(1,128)S(1)} %get-tuple-element.100.qo_ref, s32[8,512,1]{2,1,0:T(8,128)S(1)} %broadcast_add_fusion.ko_ref), custom_call_target="tpu_custom_call" | custom-call | flops 2000000000 | bytes 4000000 | tf_op jit(solution)/shard_map/pallas_call | solution.py:100
  98.0 0.8 copy-done.10
  98.8 1.1 copy-done.11
  99.9 18.5 %shard_map.249 = (f32[2,64,1024]{2,1,0:T(8,128)S(1)}, bf16[4,2,144,1024]{3,2,1,0:T(8,128)(2,1)S(1)}) custom-call(bf16[2,4,64,1024]{3,2,1,0:T(8,128)(2,1)S(1)} %bitcast.150, bf16[2,144,1024]{2,1,0:T(8,128)(2,1)S(1)} %bitcast.163), custom_call_target="tpu_custom_call" | custom-call | tf_op jit(solution)/shard_map/pallas_call | solution.py:552
  118.6 0.7 copy-done.45
  119.9 1.3 add.241
  121.2 1.5 multiply_convert_fusion.4.src
  122.7 17.0 %shard_map.250 = (bf16[2,4,64,1024]{3,2,1,0:T(8,128)(2,1)}, bf16[4,2,128,1152]{3,2,1,0:T(8,128)(2,1)}) custom-call(bf16[2,64,1024]{2,1,0:T(8,128)(2,1)} %multiply_convert_fusion.4.src, bf16[2,128,1152]{2,1,0:T(8,128)(2,1)} %bitcast.178), custom_call_target="tpu_custom_call" | custom-call | tf_op jit(solution)/shard_map/pallas_call | solution.py:324
  139.7 4.9 %fusion.50 = f32[512,1152]{1,0:T(8,128)} fusion(bf16[512,1024]{1,0:T(8,128)(2,1)} %bitcast.215, bf16[1024,1152]{1,0:T(8,128)(2,1)} %bitcast.209), kind=kOutput, calls=%fused_computation.144 | convolution fusion | flops 1207959552 | bytes 5767168 | tf_op jit(solution)/shard_map/dot_general | solution.py:31
  144.7 2.9 fusion.49
  147.6 2.3 multiply_convert_fusion
  149.9 1.5 fusion.51
  151.5 1.6 convolution_convert_fusion.1
  153.1 1.6 convolution_convert_fusion.2
  154.7 1.6 add_convert_fusion
  156.2 12.7 %shard_map.251 = f32[2,64,1024]{2,1,0:T(8,128)S(1)} custom-call(bf16[2,4,64,1024]{3,2,1,0:T(8,128)(2,1)S(1)} %bitcast.162), custom_call_target="tpu_custom_call" | custom-call | tf_op jit(solution)/shard_map/pallas_call | solution.py:552
  169.0 0.7 multiply_reduce_fusion.1
  169.8 1.4 convolution_convert_fusion
  171.4 13.0 %shard_map.252 = (bf16[2,4,64,1024]{3,2,1,0:T(8,128)(2,1)S(1)}, bf16[4,4,432,128]{3,2,1,0:T(8,128)(2,1)S(1)}, bf16[4,4,432,128]{3,2,1,0:T(8,128)(2,1)S(1)}) custom-call(bf16[2,64,1024]{2,1,0:T(8,128)(2,1)S(1)} %fusion.15.src, bf16[4,4,2,32,1152]{4,3,2,1,0:T(8,128)(2,1)S(1)} %bitcast.152, bf16[4,4,2,32,1152]{4,3,2,1,0:T(8,128)(2,1)S(1)} %bitcast.151, ...), custom_call_target="tpu_custom_call" | custom-call | tf_op jit(solution)/shard_map/pallas_call | solution.py:397
  184.4 2.5 convolution_convert_fusion.3
  187.5 34.2 %shard_map.253 = (f32[256,512]{1,0:T(8,128)S(1)}, bf16[8,2,128,512]{3,2,1,0:T(8,128)(2,1)}, bf16[2,432,128]{2,1,0:T(8,128)(2,1)S(1)}) custom-call(bf16[256,512]{1,0:T(8,128)(2,1)S(1)} %bitcast.160, bf16[8,2,128,512]{3,2,1,0:T(8,128)(2,1)} %bitcast.156, s32[1,512]{1,0:T(1,128)S(1)} %get-tuple-element.100.qo_ref, s32[8,512,1]{2,1,0:T(8,128)} %copy-done.4, ...), custom_call_target="tpu_custom_call" | custom-call | tf_op jit(solution)/shard_map/pallas_call | solution.py:769
  221.7 1.6 copy-done.5
  223.3 16.1 %shard_map.254 = f32[2,128,512]{2,1,0:T(8,128)S(1)} custom-call(bf16[4,2,2,128,512]{4,3,2,1,0:T(8,128)(2,1)S(1)} %bitcast.155), custom_call_target="tpu_custom_call" | custom-call | tf_op jit(solution)/shard_map/pallas_call | solution.py:833
  239.4 0.7 slice.151
  240.1 0.7 multiply_add_fusion.3
  240.9 0.9 multiply_add_fusion.1
  242.4 2.1 collective-permute-start.2
  244.6 2.3 copy.32
  247.0 2.1 multiply_reduce_fusion
  249.2 1.8 multiply_reduce_fusion.6
  251.9 0.8 convolution_convert_fusion.6
  252.7 1.9 convolution_convert_fusion.5
  254.7 0.8 fusion.30
  255.5 23.2 %shard_map.255 = (f32[2,64,1024]{2,1,0:T(8,128)S(1)}, bf16[4,432,128]{2,1,0:T(8,128)(2,1)S(1)}, bf16[4,432,128]{2,1,0:T(8,128)(2,1)S(1)}) custom-call(bf16[2,4,64,1024]{3,2,1,0:T(8,128)(2,1)S(1)} %bitcast.161, bf16[432,128]{1,0:T(8,128)(2,1)S(1)} %get-tuple-element.114.refs_1_, bf16[432,128]{1,0:T(8,128)(2,1)S(1)} %get-tuple-element.113.refs_2_), custom_call_target="tpu_custom_call" | custom-call | tf_op jit(solution)/shard_map/pallas_call | solution.py:552
  278.7 1.9 fusion.22
  280.9 1.2 copy-done.7
  282.1 31.9 %shard_map.256 = (bf16[2,96,128]{2,1,0:T(8,128)(2,1)S(1)}, f32[24,128]{1,0:T(8,128)S(1)}, bf16[2,2,4,4,432,128]{5,4,3,2,1,0:T(8,128)(2,1)}) custom-call(bf16[4,4,2,32,512]{4,3,2,1,0:T(8,128)(2,1)S(1)} %bitcast.158, bf16[4,2,32,1024]{3,2,1,0:T(8,128)(2,1)S(1)} %bitcast.154, f32[24,128]{1,0:T(8,128)S(1)} %pad_bitcast_fusion.gains, ...), custom_call_target="tpu_custom_call" | custom-call | tf_op jit(solution)/shard_map/pallas_call | solution.py:965
  314.1 0.7 collective-permute-start.3
  314.8 2.0 fusion.18
  319.9 24.1 %shard_map.257.pieces = bf16[2,2,4,4,96,128]{5,4,3,2,1,0:T(8,128)(2,1)} custom-call(bf16[2,96,128]{2,1,0:T(8,128)(2,1)} %pad_maximum_fusion.7.piece), custom_call_target="tpu_custom_call" | custom-call | tf_op jit(solution)/shard_map/pallas_call | solution.py:1069
  344.0 3.0 copy-done.2
  347.0 1.4 copy-done.3
  348.4 5.2 %shard_map.258 = (f32[256,4608]{1,0:T(8,128)}, f32[256,4608]{1,0:T(8,128)}, f32[256,1024]{1,0:T(8,128)}, f32[256,512]{1,0:T(8,128)}, f32[256,512]{1,0:T(8,128)}) custom-call(bf16[2,2,4,4,432,128]{5,4,3,2,1,0:T(8,128)(2,1)S(1)} %copy-done.2, bf16[2,2,4,4,96,128]{5,4,3,2,1,0:T(8,128)(2,1)S(1)} %copy-done.3), custom_call_target="tpu_custom_call" | custom-call | tf_op jit(solution)/shard_map/pallas_call | solution.py:1102
  353.6 4.1 %shard_map.259 = (f32[1152,1024]{1,0:T(8,128)}, f32[256,1024]{1,0:T(8,128)}) custom-call(bf16[2,2,4,4,432,128]{5,4,3,2,1,0:T(8,128)(2,1)S(1)} %copy-done.2, bf16[2,2,4,4,96,128]{5,4,3,2,1,0:T(8,128)(2,1)S(1)} %copy-done.3), custom_call_target="tpu_custom_call" | custom-call | tf_op jit(solution)/shard_map/pallas_call | solution.py:1118
  (195 shorter events, 10.9 us)
Async XLA Ops:
  7.2 25.4 %copy-start = (bf16[1152,1024]{1,0:T(8,128)(2,1)S(1)}, bf16[1152,1024]{1,0:T(8,128)(2,1)}, u32[]{:S(2)}) copy-start(bf16[1152,1024]{1,0:T(8,128)(2,1)} %param.28) | copy-start | bytes 7077892
  7.2 137.4 %all-gather.2.cloned.1.call-start = ((), (), s32[]{:S(2)}) async-start(), calls=%async_computation.1 | async-start | bytes 1310720 | tf_op jit(solution)/shard_map/all_gather | solution.py:1208
  28.7 7.9 %copy-start.21 = (bf16[2,4,64,1024]{3,2,1,0:T(8,128)(2,1)S(1)}, bf16[2,4,64,1024]{3,2,1,0:T(8,128)(2,1)}, u32[]{:S(2)}) copy-start(bf16[2,4,64,1024]{3,2,1,0:T(8,128)(2,1)} %get-tuple-element.53) | copy-start | bytes 3145732
  30.4 24.7 %collective-permute-start = (bf16[64,1024]{1,0:T(8,128)(2,1)}, bf16[64,1024]{1,0:T(8,128)(2,1)}, u32[]{:S(2)}, u32[]{:S(2)}) collective-permute-start(bf16[64,1024]{1,0:T(8,128)(2,1)} %constant_dynamic-slice_fusion.2), channel_id=1, source_target_pairs={{0,0},{2,32},{4,64},{6,96},{32,2},{34,34},{36,66},{38,98},{64,4},{... | collective-permute-start | bytes 393224 | tf_op jit(solution)/shard_map/ppermute | solution.py:1187
  33.4 64.6 %collective-permute-start.1 = (bf16[288,1024]{1,0:T(8,128)(2,1)}, bf16[288,1024]{1,0:T(8,128)(2,1)S(1)}, u32[]{:S(2)}, u32[]{:S(2)}) collective-permute-start(bf16[288,1024]{1,0:T(8,128)(2,1)} %constant_dynamic-slice_fusion.1), channel_id=1, source_target_pairs={{0,0},{2,32},{4,64},{6,96},{32,2},{34,34},{36,66},{38,98},{64,4},{... | collective-permute-start | bytes 1769480 | tf_op jit(solution)/shard_map/ppermute | solution.py:1187
  35.1 243.5 %reduce-scatter.2.cloned.1.call-start = ((), (), s32[]{:S(2)}) async-start(), calls=%async_computation.2 | async-start | bytes 1310720 | tf_op jit(solution)/shard_map/reduce_scatter | solution.py:1261
  37.2 2.4 copy-start.62
  39.5 6.9 %copy-start.18 = (f32[512,512]{1,0:T(8,128)}, f32[512,512]{1,0:T(8,128)S(1)}, u32[]{:S(2)}) copy-start(f32[512,512]{1,0:T(8,128)S(1)} %fusion.48) | copy-start | bytes 3145732
  39.5 5.7 %copy-start.63 = (s32[1,128]{1,0:T(1,128)S(1)}, s32[1,128]{1,0:T(1,128)}, u32[]{:S(2)}) copy-start(s32[1,128]{1,0:T(1,128)} %param.16) | copy-start | bytes 1540
  39.6 6.1 %copy-start.34 = (f32[4,512]{1,0:T(4,128)}, f32[4,512]{1,0:T(4,128)S(1)}, u32[]{:S(2)}) copy-start(f32[4,512]{1,0:T(4,128)S(1)} %multiply_reduce_fusion.5) | copy-start | bytes 24580
  39.6 6.1 %copy-start.40 = (f32[2,512]{1,0:T(2,128)}, f32[2,512]{1,0:T(2,128)S(1)}, u32[]{:S(2)}) copy-start(f32[2,512]{1,0:T(2,128)S(1)} %multiply_reduce_fusion.8) | copy-start | bytes 12292
  43.6 4.6 %copy-start.47 = (f32[64]{0:T(128)}, f32[64]{0:T(128)S(1)}, u32[]{:S(2)}) copy-start(f32[64]{0:T(128)S(1)} %mul.537) | copy-start | bytes 772
  43.6 4.6 %copy-start.31 = (f32[4,512]{1,0:T(4,128)}, f32[4,512]{1,0:T(4,128)S(1)}, u32[]{:S(2)}) copy-start(f32[4,512]{1,0:T(4,128)S(1)} %fusion.35) | copy-start | bytes 24580
  44.4 3.9 %copy-start.49 = (f32[64]{0:T(128)}, f32[64]{0:T(128)S(1)}, u32[]{:S(2)}) copy-start(f32[64]{0:T(128)S(1)} %mul.562) | copy-start | bytes 772
  44.4 3.9 %copy-start.38 = (f32[2,512]{1,0:T(2,128)}, f32[2,512]{1,0:T(2,128)S(1)}, u32[]{:S(2)}) copy-start(f32[2,512]{1,0:T(2,128)S(1)} %fusion.40) | copy-start | bytes 12292
  48.3 32.8 %copy-start.4 = (s32[8,512,1]{2,1,0:T(8,128)}, s32[8,512,1]{2,1,0:T(8,128)S(1)}, u32[]{:S(2)}) copy-start(s32[8,512,1]{2,1,0:T(8,128)S(1)} %broadcast_add_fusion.ko_ref) | copy-start | bytes 49156
  48.3 4.5 %copy-start.19 = (f32[512,512]{1,0:T(8,128)S(1)}, f32[512,512]{1,0:T(8,128)}, u32[]{:S(2)}) copy-start(f32[512,512]{1,0:T(8,128)} %copy-done.18) | copy-start | bytes 3145732
  48.3 5.2 %copy-start.44 = (f32[1,2,4,128]{3,2,1,0:T(4,128)S(1)}, f32[1,2,4,128]{3,2,1,0:T(4,128)}, u32[]{:S(2)}) copy-start(f32[1,2,4,128]{3,2,1,0:T(4,128)} %get-tuple-element.115) | copy-start | bytes 12292
  48.3 5.2 %copy-start.30 = (bf16[2,32,512]{2,1,0:T(8,128)(2,1)S(1)}, bf16[2,32,512]{2,1,0:T(8,128)(2,1)}, u32[]{:S(2)}) copy-start(bf16[2,32,512]{2,1,0:T(8,128)(2,1)} %get-tuple-element.110) | copy-start | bytes 196612
  52.9 44.6 %copy-start.8 = (bf16[4,64,512]{2,1,0:T(8,128)(2,1)}, bf16[4,64,512]{2,1,0:T(8,128)(2,1)S(1)}, u32[]{:S(2)}) copy-start(bf16[4,64,512]{2,1,0:T(8,128)(2,1)S(1)} %pad_maximum_fusion.2) | copy-start | bytes 786436
  81.1 1.6 copy-start.6
  82.7 14.8 %copy-start.26 = (bf16[4,2,32,1024]{3,2,1,0:T(8,128)(2,1)S(1)}, bf16[4,2,32,1024]{3,2,1,0:T(8,128)(2,1)}, u32[]{:S(2)}) copy-start(bf16[4,2,32,1024]{3,2,1,0:T(8,128)(2,1)} %get-tuple-element.58) | copy-start | bytes 1572868
  97.5 20.9 %copy-start.12 = (f32[256,512]{1,0:T(8,128)}, f32[256,512]{1,0:T(8,128)S(1)}, u32[]{:S(2)}) copy-start(f32[256,512]{1,0:T(8,128)S(1)} %get-tuple-element.70.mixed_ref) | copy-start | bytes 1572868
  97.5 21.0 %copy-start.16 = (bf16[1,128,1024]{2,1,0:T(8,128)(2,1)S(1)}, bf16[1,128,1024]{2,1,0:T(8,128)(2,1)}, u32[]{:S(2)}) copy-start(bf16[1,128,1024]{2,1,0:T(8,128)(2,1)} %param.15) | copy-start | bytes 786436
  118.4 26.2 %copy-start.14 = (bf16[4,2,144,1024]{3,2,1,0:T(8,128)(2,1)}, bf16[4,2,144,1024]{3,2,1,0:T(8,128)(2,1)S(1)}, u32[]{:S(2)}) copy-start(bf16[4,2,144,1024]{3,2,1,0:T(8,128)(2,1)S(1)} %get-tuple-element.62) | copy-start | bytes 7077892
  144.6 3.0 copy-start.57
  144.6 3.0 copy-start.61
  144.6 3.0 copy-start.64
  147.6 2.3 copy-start.58
  154.6 14.3 %copy-start.42 = (f32[2,64]{1,0:T(2,128)S(1)}, f32[2,64]{1,0:T(2,128)}, u32[]{:S(2)}) copy-start(f32[2,64]{1,0:T(2,128)} %get-tuple-element.126) | copy-start | bytes 1540
  156.2 13.5 %copy-start.46 = (f32[2,64]{1,0:T(2,128)S(1)}, f32[2,64]{1,0:T(2,128)}, u32[]{:S(2)}) copy-start(f32[2,64]{1,0:T(2,128)} %copy-done.45) | copy-start | bytes 1540
  156.2 13.5 %copy-start.60 = (bf16[2,4,64,1024]{3,2,1,0:T(8,128)(2,1)S(1)}, bf16[2,4,64,1024]{3,2,1,0:T(8,128)(2,1)}, u32[]{:S(2)}) copy-start(bf16[2,4,64,1024]{3,2,1,0:T(8,128)(2,1)} %all-gather.2.cloned.1.call-done) | copy-start | bytes 3145732
  169.7 1.5 copy-start.51
  169.7 1.5 copy-start.25
  171.4 13.0 %copy-start.15 = (bf16[4,2,144,1024]{3,2,1,0:T(8,128)(2,1)S(1)}, bf16[4,2,144,1024]{3,2,1,0:T(8,128)(2,1)}, u32[]{:S(2)}) copy-start(bf16[4,2,144,1024]{3,2,1,0:T(8,128)(2,1)} %copy-done.14) | copy-start | bytes 7077892
  184.4 2.6 copy-start.27
  184.4 3.0 copy-start.9
  184.4 3.0 copy-start.13
  221.7 19.2 %copy-start.52 = (f32[2,64]{1,0:T(2,128)S(1)}, f32[2,64]{1,0:T(2,128)}, u32[]{:S(2)}) copy-start(f32[2,64]{1,0:T(2,128)} %copy-done.51) | copy-start | bytes 1540
  221.7 1.6 copy-start.5
  240.8 6.1 %copy-start.32 = (f32[4,512]{1,0:T(4,128)S(1)}, f32[4,512]{1,0:T(4,128)}, u32[]{:S(2)}) copy-start(f32[4,512]{1,0:T(4,128)} %copy-done.31) | copy-start | bytes 24580
  240.8 6.2 %copy-start.48 = (f32[64]{0:T(128)S(1)}, f32[64]{0:T(128)}, u32[]{:S(2)}) copy-start(f32[64]{0:T(128)} %copy-done.47) | copy-start | bytes 772
  241.8 5.2 %slice-start.1 = ((f32[512,512]{1,0:T(8,128)}), f32[256,512]{1,0:T(8,128)S(1)}, s32[]{:S(2)}) async-start(f32[512,512]{1,0:T(8,128)} %copy-done.18), calls=%async_computation.4 | async-start | bytes 1048576 | tf_op jit(solution)/shard_map/slice | solution.py:1213
  242.4 12.2 %collective-permute-start.2 = (bf16[2,144,128]{2,1,0:T(8,128)(2,1)}, bf16[2,144,128]{2,1,0:T(8,128)(2,1)}, u32[]{:S(2)}, u32[]{:S(2)}) collective-permute-start(bf16[2,144,128]{2,1,0:T(8,128)(2,1)} %slice.94), channel_id=1, source_target_pairs={{0,0},{2,32},{4,64},{6,96},{32,2},{34,34},{36,66},{38,98},{64,4},{... | collective-permute-start | bytes 221192 | tf_op jit(solution)/shard_map/ppermute | solution.py:1273
  244.6 4.6 %slice-start = ((f32[512,512]{1,0:T(8,128)}), f32[128,512]{1,0:T(8,128)S(1)}, s32[]{:S(2)}) async-start(f32[512,512]{1,0:T(8,128)} %copy-done.18), calls=%async_computation.3 | async-start | bytes 524288 | tf_op jit(solution)/shard_map/slice | solution.py:1218
  244.6 4.6 %copy-start.28 = (f32[2,32,512]{2,1,0:T(8,128)S(1)}, f32[2,32,512]{2,1,0:T(8,128)}, u32[]{:S(2)}) copy-start(f32[2,32,512]{2,1,0:T(8,128)} %get-tuple-element.106) | copy-start | bytes 393220
  244.6 4.6 %copy-start.39 = (f32[2,512]{1,0:T(2,128)S(1)}, f32[2,512]{1,0:T(2,128)}, u32[]{:S(2)}) copy-start(f32[2,512]{1,0:T(2,128)} %copy-done.38) | copy-start | bytes 12292
  244.6 4.6 %copy-start.50 = (f32[64]{0:T(128)S(1)}, f32[64]{0:T(128)}, u32[]{:S(2)}) copy-start(f32[64]{0:T(128)} %copy-done.49) | copy-start | bytes 772
  244.6 6.4 %copy-start.41 = (f32[2,512]{1,0:T(2,128)S(1)}, f32[2,512]{1,0:T(2,128)}, u32[]{:S(2)}) copy-start(f32[2,512]{1,0:T(2,128)} %copy-done.40) | copy-start | bytes 12292
  244.6 6.4 %copy-start.35 = (f32[4,512]{1,0:T(4,128)S(1)}, f32[4,512]{1,0:T(4,128)}, u32[]{:S(2)}) copy-start(f32[4,512]{1,0:T(4,128)} %copy-done.34) | copy-start | bytes 24580
  246.9 4.1 %copy-start.20 = (f32[512,512]{1,0:T(8,128)S(1)}, f32[512,512]{1,0:T(8,128)}, u32[]{:S(2)}) copy-start(f32[512,512]{1,0:T(8,128)} %copy-done.18) | copy-start | bytes 3145732
  246.9 4.1 %copy-start.29 = (f32[2,32,512]{2,1,0:T(8,128)S(1)}, f32[2,32,512]{2,1,0:T(8,128)}, u32[]{:S(2)}) copy-start(f32[2,32,512]{2,1,0:T(8,128)} %get-tuple-element.107) | copy-start | bytes 393220
  246.9 4.2 %copy-start.23 = (f32[4,32,512]{2,1,0:T(8,128)S(1)}, f32[4,32,512]{2,1,0:T(8,128)}, u32[]{:S(2)}) copy-start(f32[4,32,512]{2,1,0:T(8,128)} %get-tuple-element.104) | copy-start | bytes 786436
  247.0 4.2 %copy-start.24 = (f32[4,32,512]{2,1,0:T(8,128)S(1)}, f32[4,32,512]{2,1,0:T(8,128)}, u32[]{:S(2)}) copy-start(f32[4,32,512]{2,1,0:T(8,128)} %get-tuple-element.105) | copy-start | bytes 786436
  249.1 2.7 copy-start.33
  249.1 2.7 copy-start.59
  252.7 1.9 copy-start.56
  252.7 26.0 %copy-start.17 = (bf16[1,128,1024]{2,1,0:T(8,128)(2,1)S(1)}, bf16[1,128,1024]{2,1,0:T(8,128)(2,1)}, u32[]{:S(2)}) copy-start(bf16[1,128,1024]{2,1,0:T(8,128)(2,1)} %param.15) | copy-start | bytes 786436
  254.6 26.2 %copy-start.43 = (f32[1024]{0:T(1024)S(1)}, f32[1024]{0:T(1024)}, u32[]{:S(2)}) copy-start(f32[1024]{0:T(1024)} %get-tuple-element.91) | copy-start | bytes 12292
  254.6 26.2 %copy-start.53 = (f32[64]{0:T(128)S(1)}, f32[64]{0:T(128)}, u32[]{:S(2)}) copy-start(f32[64]{0:T(128)} %get-tuple-element.93) | copy-start | bytes 772
  254.6 26.2 %copy-start.54 = (f32[64]{0:T(128)S(1)}, f32[64]{0:T(128)}, u32[]{:S(2)}) copy-start(f32[64]{0:T(128)} %get-tuple-element.95) | copy-start | bytes 772
  314.1 5.2 %collective-permute-start.3 = (bf16[2,32,128]{2,1,0:T(8,128)(2,1)S(1)}, bf16[2,32,128]{2,1,0:T(8,128)(2,1)S(1)}, u32[]{:S(2)}, u32[]{:S(2)}) collective-permute-start(bf16[2,32,128]{2,1,0:T(8,128)(2,1)S(1)} %slice.100), channel_id=1, source_target_pairs={{0,0},{2,32},{4,64},{6,96},{32,2},{34,34},{36,66},{38,98},{64,4},{... | collective-permute-start | bytes 49160 | tf_op jit(solution)/shard_map/ppermute | solution.py:1313
  344.0 3.0 copy-start.2
  348.4 9.3 %copy-start.1 = (bf16[1152,1024]{1,0:T(8,128)(2,1)S(1)}, bf16[1152,1024]{1,0:T(8,128)(2,1)}, u32[]{:S(2)}) copy-start(bf16[1152,1024]{1,0:T(8,128)(2,1)} %param.28) | copy-start | bytes 7077892
  (9 other events, 9.6 us)
Sparse Core Ops, SparseCore 0:
  35.3 40.7 all-gather.1
  247.0 23.3 reduce-scatter.1

commit v4 on v3

v4 whole, which is shorter than its diff:
```python
import functools

import jax
import jax.numpy as jnp
import numpy as np
from jax import lax
from jax.experimental import pallas as pl
from jax.experimental.pallas import tpu as pltpu
from jax.sharding import Mesh, PartitionSpec as P

HD = 64
BLK = 64
GROUPS = 8
HALF = 256
ROWS = 512
FF_PIECE = 432

NORM_EPS = 1e-05
ROPE_BASE = 1000000.0
EXP2_SCALE = float(HD**-0.5 * np.log2(np.e))
SCORE_SCALE = HD**-0.5

F32 = jnp.float32
BF16 = jnp.bfloat16
VMEM = pl.BlockSpec(memory_space=pltpu.VMEM)
ANY = pl.BlockSpec(memory_space=pl.ANY)


def dot(left, right, left_dim=1, right_dim=0):
    return lax.dot_general(
        left, right, (((left_dim,), (right_dim,)), ((), ())), preferred_element_type=F32
    )


def rms_scale(values, gain):
    return values * lax.rsqrt(jnp.mean(values * values, axis=-1, keepdims=True) + NORM_EPS) * gain


def head_norm_rope(raw, gain, cosine, sine):
    scaled = (
        raw
        * lax.rsqrt(jnp.mean(raw * raw, axis=1, keepdims=True) + NORM_EPS)
        * gain[None, :, None]
    )
    front = scaled[:, : HD // 2]
    back = scaled[:, HD // 2 :]
    return jnp.concatenate([front * cosine - back * sine, back * cosine + front * sine], axis=1)


def scores_of(keys_t, queries_t):
    return dot(keys_t, queries_t, 0, 0)


def head_pair(ref, kv_head, cols):
    first = 2 * kv_head * HD
    return jnp.concatenate(
        [ref[first : first + HD, cols], ref[first + HD : first + 2 * HD, cols]], axis=1
    )


def ring(axis):
    me = lax.axis_index(axis)
    return me, lax.rem(me + 1, 4), lax.rem(me + 2, 4), lax.rem(me + 3, 4)


def meet(partners):
    barrier = pltpu.get_barrier_semaphore()
    for partner in partners:
        pl.semaphore_signal(
            barrier, inc=1, device_id=partner, device_id_type=pl.DeviceIdType.MESH
        )
    pl.semaphore_wait(barrier, len(partners))


class Sends:
    def __init__(self, send_sems, recv_sems):
        self.send_sems, self.recv_sems, self.started = send_sems, recv_sems, []

    def __call__(self, source, target, partner):
        at = len(self.started)
        copy = pltpu.make_async_remote_copy(
            src_ref=source,
            dst_ref=target,
            send_sem=self.send_sems.at[at],
            recv_sem=self.recv_sems.at[at],
            device_id=partner,
            device_id_type=pl.DeviceIdType.MESH,
        )
        copy.start()
        self.started.append(copy)
        return copy

    def finish(self):
        for copy in self.started:
            copy.wait_send()


class RingGather:
    def __init__(self, send, axis, at, own, sibling=False, share_own=False):
        self.send, self.axis, self.own = send, axis, own
        self.me, self.right, self.far, self.left = ring(axis)
        self.to_right, self.to_left = {axis: self.right}, {axis: self.left}
        core = lax.axis_index("core")
        self.to_sib = {"core": 1 - core}
        self.at = lambda place, half: at(place, core, half)
        self.sibling, self.share_own = sibling, share_own
        self.from_sib = []

    def share(self, place, half, source=None):
        if self.sibling:
            target = self.at(place, half)
            source = target if source is None else source
            self.from_sib.append(self.send(source, target, self.to_sib))

    def begin(self):
        def own_to(half, partner):
            return self.send(self.own(half), self.at(self.me, half), partner)

        self.right0 = own_to(0, self.to_right)
        self.left1 = own_to(1, self.to_left)
        self.right1 = own_to(1, self.to_right)
        self.left0 = own_to(0, self.to_left)
        if self.share_own:
            for half in range(2):
                self.share(self.me, half, self.own(half))

    def middle(self):
        self.right0.wait_recv()
        passed = self.at(self.left, 0)
        self.far0 = self.send(passed, passed, self.to_right)
        self.left1.wait_recv()
        passed = self.at(self.right, 1)
        self.far1 = self.send(passed, passed, self.to_left)
        self.share(self.left, 0)
        self.share(self.right, 1)

    def near(self):
        self.right1.wait_recv()
        self.share(self.left, 1)
        self.left0.wait_recv()
        self.share(self.right, 0)

    def end(self):
        self.far0.wait_recv()
        self.share(self.far, 0)
        self.far1.wait_recv()
        self.share(self.far, 1)

    def finish(self):
        for copy in self.from_sib:
            copy.wait_recv()


def sems(count):
    return pltpu.SemaphoreType.DMA((count,))


def rows_half(rows):
    return lambda half: (pl.ds(half * rows, rows), slice(None))


def columns_half(columns):
    return lambda half: (slice(None), pl.ds(half * columns, columns))


def weight_gather(send, src, out, half_of):
    core = lax.axis_index("core")
    return RingGather(
        send,
        "dp",
        lambda place, core, half: out.at[(place, core) + half_of(half)],
        lambda half: src.at[(core,) + half_of(half)],
        sibling=True,
    )


def around(axes, sibling=True):
    partners = []
    for axis in axes:
        unused, right, unused, left = ring(axis)
        partners += [{axis: right}, {axis: left}]
    return partners + ([{"core": 1 - lax.axis_index("core")}] if sibling else [])


def load_columns(weight, own, width, at, loads, first):
    begin = pl.multiple_of(lax.axis_index("x") * width, 128)
    rows = own.shape[1]
    copies = [
        pltpu.make_async_copy(
            weight.at[pl.ds(c * rows, rows), pl.ds(begin, width)],
            own.at[c, :, pl.ds(at, width)],
            loads.at[first + c],
        )
        for c in range(2)
    ]
    for copy in copies:
        copy.start()
    return copies


def start_kernel(
    hidden, query, key, value, gains, hidden_out, qkv_out, gains_out, qkv, sends, recvs, loads
):
    me_x, me_y = lax.axis_index("x"), lax.axis_index("dp")
    far_y = lax.rem(me_y + 2, 4)
    slices = (
        load_columns(query, qkv, 256, 0, loads, 3)
        + load_columns(key, qkv, 128, 256, loads, 5)
        + load_columns(value, qkv, 128, 384, loads, 7)
    )
    own = [
        pltpu.make_async_copy(hidden, hidden_out.at[:, me_x], loads.at[0]),
        pltpu.make_async_copy(gains, gains_out.at[me_y], loads.at[2]),
    ]
    for copy in own:
        copy.start()
    partners = around(["x", "dp"])
    meet(partners + [{"dp": far_y}])
    send = Sends(sends, recvs)
    line = line_ring(send, hidden, hidden_out)
    line.begin()
    for copy in slices:
        copy.wait()
    own.append(pltpu.make_async_copy(qkv, qkv_out.at[me_y], loads.at[1]))
    own[-1].start()
    weights = weight_gather(send, qkv, qkv_out, rows_half(64))
    weights.begin()
    direct = [
        send(gains, gains_out.at[me_y], partner) for partner in partners[2:4] + [{"dp": far_y}]
    ]
    line.middle()
    weights.middle()
    for step in ("near", "end", "finish"):
        for gather in (weights, line):
            getattr(gather, step)()
    for copy in direct:
        copy.wait_recv()
    for copy in own:
        copy.wait()
    send.finish()


def start_gather(kernel_id, hidden_rows, query, key, value, gains):
    hidden, qkv, gains = pl.pallas_call(
        start_kernel,
        out_shape=(
            jax.ShapeDtypeStruct((2, 4, BLK, 1024), BF16),
            jax.ShapeDtypeStruct((4, 2, 128, 512), BF16),
            jax.ShapeDtypeStruct((4, 16, 128), BF16),
        ),
        in_specs=[VMEM] + [ANY] * 3 + [VMEM],
        out_specs=(ANY,) * 3,
        scratch_shapes=[pltpu.VMEM((2, 128, 512), BF16), sems(21), sems(21), sems(9)],
        compiler_params=pltpu.CompilerParams(collective_id=kernel_id, has_side_effects=True),
    )(hidden_rows.reshape(2, BLK, 1024), query, key, value, gains)
    return hidden.reshape(ROWS, 1024), qkv.reshape(1024, 512), gains


def line_gather_kernel(src, out, sends, recvs, loads):
    own = pltpu.make_async_copy(src, out.at[:, lax.axis_index("x")], loads.at[0])
    own.start()
    meet(around(["x"], sibling=False))
    send = Sends(sends, recvs)
    line = line_ring(send, src, out)
    for step in ("begin", "middle", "near", "end"):
        getattr(line, step)()
    own.wait()
    send.finish()


def line_ring(send, src, out):
    return RingGather(
        send, "x", lambda place, core, half: out.at[half, place], lambda half: src.at[half]
    )


def line_gather(kernel_id, rows):
    width = rows.shape[1]
    return pl.pallas_call(
        line_gather_kernel,
        out_shape=jax.ShapeDtypeStruct((2, 4, BLK, width), BF16),
        in_specs=[VMEM],
        out_specs=ANY,
        scratch_shapes=[sems(6), sems(6), sems(1)],
        compiler_params=pltpu.CompilerParams(collective_id=kernel_id, has_side_effects=True),
    )(rows.reshape(2, BLK, width)).reshape(ROWS, width)


def line_gather_pack_kernel(
    src, gate, up, down, out, packed_y, packed_z,
    gu_own, gu_sib, down_own, down_sib, sends, recvs, loads,
):
    core = lax.axis_index("core")
    to_sib = {"core": 1 - core}
    views = [
        (lambda c: gate.at[:, :, c], gu_own.at[0], gu_sib.at[0]),
        (lambda c: up.at[:, :, c], gu_own.at[1], gu_sib.at[1]),
        (lambda c: down.at[:, c], down_own, down_sib),
    ]
    local = [
        pltpu.make_async_copy(view(core), mine, loads.at[i])
        for i, (view, mine, unused) in enumerate(views)
    ]
    local.append(pltpu.make_async_copy(src, out.at[:, lax.axis_index("x")], loads.at[3]))
    for copy in local:
        copy.start()
    meet(around(["x"]))
    send = Sends(sends, recvs)
    line = line_ring(send, src, out)
    line.begin()
    shared = [send(view(1 - core), theirs, to_sib) for view, unused, theirs in views]
    line.middle()
    for copy in local:
        copy.wait()
    for copy in shared:
        copy.wait_recv()

    def pack(y, unused):
        for z in range(4):
            for s in range(2):

                def put(rows, value):
                    if s == 0:
                        packed_y[y, z, rows, :] = value
                    else:
                        packed_z[z, y, rows, :] = value

                for t in range(9):
                    cols = slice(t * 128, (t + 1) * 128)
                    put(
                        slice(t * 32, (t + 1) * 32),
                        add_low(gu_own[s, y, z, :, cols], gu_sib[s, y, z, :, cols]),
                    )
                cols = slice(s * 512 + z * 128, s * 512 + (z + 1) * 128)
                put(slice(288, 432), add_low(down_own[y, :, cols], down_sib[y, :, cols]))
        return unused

    lax.fori_loop(0, 4, pack, 0)
    line.near()
    line.end()
    send.finish()


def line_gather_pack(kernel_id, rows, gate, up, down):
    def vm(*shape):
        return pltpu.VMEM(shape, BF16)

    gathered, packed_y, packed_z = pl.pallas_call(
        line_gather_pack_kernel,
        out_shape=(jax.ShapeDtypeStruct((2, 4, BLK, 1024), BF16),)
        + (jax.ShapeDtypeStruct((4, 4, FF_PIECE, 128), BF16),) * 2,
        in_specs=[VMEM] + [ANY] * 3,
        out_specs=(ANY, VMEM, VMEM),
        scratch_shapes=[
            vm(2, 4, 4, 32, 1152), vm(2, 4, 4, 32, 1152),
            vm(4, 144, 1024), vm(4, 144, 1024),
            sems(9), sems(9), sems(4),
        ],
        compiler_params=pltpu.CompilerParams(
            collective_id=kernel_id, has_side_effects=True, vmem_limit_bytes=40 * 2**20
        ),
    )(
        rows.reshape(2, BLK, 1024),
        gate.reshape(4, 4, 2, 32, 1152),
        up.reshape(4, 4, 2, 32, 1152),
        down.reshape(4, 2, 144, 1024),
    )
    return gathered.reshape(ROWS, 1024), packed_y, packed_z


def sequence_gather_kernel(
    kv, gate, out, kv_all, gate_all, out_all, sends, recvs, loads
):
    me_z, me_y = lax.axis_index("z"), lax.axis_index("dp")
    core = lax.axis_index("core")
    own = [
        pltpu.make_async_copy(kv, kv_all.at[me_z, core], loads.at[0]),
        pltpu.make_async_copy(out, out_all.at[me_y], loads.at[2]),
        pltpu.make_async_copy(gate, gate_all.at[me_y], loads.at[1]),
    ]
    for copy in own:
        copy.start()
    meet(around(["z", "dp"]))
    send = Sends(sends, recvs)
    gathers = [
        RingGather(
            send,
            "z",
            lambda place, core, half: kv_all.at[place, core, half],
            lambda half: kv.at[half],
            sibling=True,
            share_own=True,
        ),
        weight_gather(send, out, out_all, columns_half(512)),
        weight_gather(send, gate, gate_all, rows_half(64)),
    ]
    gathers[0].begin()
    gathers[2].begin()
    gathers[1].begin()
    for step in ("middle", "near", "end", "finish"):
        for gather in gathers:
            getattr(gather, step)()
    for copy in own:
        copy.wait()
    send.finish()


def sequence_gather(kernel_id, kv, gate, out):
    kv_all, gate_all, out_all = pl.pallas_call(
        sequence_gather_kernel,
        out_shape=(
            jax.ShapeDtypeStruct((4, 2, 2, 2 * HD, ROWS), BF16),
            jax.ShapeDtypeStruct((4, 2, 128, 1152), BF16),
            jax.ShapeDtypeStruct((4, 2, 32, 1024), BF16),
        ),
        in_specs=[VMEM] * 3,
        out_specs=(ANY,) * 3,
        scratch_shapes=[sems(38), sems(38), sems(3)],
        compiler_params=pltpu.CompilerParams(collective_id=kernel_id, has_side_effects=True),
    )(kv, gate.reshape(2, 128, 1152), out.reshape(2, 32, 1024))
    return (
        kv_all.reshape(GROUPS, 2, 2 * HD, ROWS),
        gate_all.reshape(1024, 1152),
        out_all.reshape(256, 1024),
    )


def attend_kernel(
    q_ref, kv_ref, qo_ref, ko_ref, up, mixed_ref, low_ref, log_ref, up_all,
    sends, recvs, loads,
):
    meet(around(["dp"]))
    own = pltpu.make_async_copy(up, up_all.at[lax.axis_index("dp")], loads.at[0])
    own.start()
    send = Sends(sends, recvs)
    gather = weight_gather(send, up, up_all, rows_half(64))
    gather.begin()
    for half in range(2):
        cols = slice(half * HALF, (half + 1) * HALF)
        q_order = jnp.concatenate([qo_ref[:, cols]] * 2, axis=1)
        queries = [head_pair(q_ref, kv_head, cols) for kv_head in range(2)]

        def group(g, carried):
            carried = list(carried)
            for k_half in range(half + 1):
                keys = slice(k_half * HALF, (k_half + 1) * HALF)
                for kv_head in range(2):
                    acc, total = carried[kv_head]
                    probs = jnp.exp2(
                        scores_of(kv_ref[g, kv_head, 0:HD, keys], queries[kv_head]) * EXP2_SCALE
                    )
                    if k_half == half:
                        allowed = jnp.concatenate([ko_ref[g, keys, :]] * 4, axis=1) <= q_order
                        probs = jnp.where(allowed, probs, 0.0)
                    total = total + jnp.sum(probs, axis=0, keepdims=True)
                    acc = acc + dot(kv_ref[g, kv_head, HD : 2 * HD, keys], probs.astype(BF16))
                    carried[kv_head] = (acc, total)
            return tuple(carried)

        start = (jnp.zeros((HD, 2 * HALF), F32), jnp.zeros((1, 2 * HALF), F32))
        sums = lax.fori_loop(0, GROUPS, group, (start, start))
        for kv_head, (acc, total) in enumerate(sums):
            mixed = acc / total
            logs = jnp.log2(total)
            for head in range(2):
                at = 2 * kv_head + head
                rows = slice(at * HD, (at + 1) * HD)
                part = mixed[:, head * HALF : (head + 1) * HALF]
                mixed_ref[rows, cols] = part
                low_ref[rows, cols] = part.astype(BF16)
                log_ref[at : at + 1, cols] = logs[:, head * HALF : (head + 1) * HALF]
        if half == 0:
            gather.middle()
    gather.near()
    gather.end()
    gather.finish()
    own.wait()
    send.finish()


def attend(kernel_id, q_t, kv_all, q_order, k_order, up):
    *results, up_all = pl.pallas_call(
        attend_kernel,
        out_shape=(
            jax.ShapeDtypeStruct((4 * HD, ROWS), F32),
            jax.ShapeDtypeStruct((4 * HD, ROWS), BF16),
            jax.ShapeDtypeStruct((4, ROWS), F32),
            jax.ShapeDtypeStruct((4, 2, 128, 1152), BF16),
        ),
        in_specs=[VMEM] * 5,
        out_specs=(VMEM,) * 3 + (ANY,),
        scratch_shapes=[sems(12), sems(12), sems(1)],
        compiler_params=pltpu.CompilerParams(
            collective_id=kernel_id, has_side_effects=True, vmem_limit_bytes=40 * 2**20
        ),
    )(q_t, kv_all, q_order, k_order, up.reshape(2, 128, 1152))
    return *results, up_all.reshape(1024, 1152)


def add_low(left, right):
    return (left.astype(F32) + right.astype(F32)).astype(BF16)


def others(axis):
    return [{axis: place} for place in ring(axis)[1:]]


def send_to_others(send, axis, source, slots):
    slot = slots.at[lax.axis_index(axis)]
    return [send(source, slot, other) for other in others(axis)]


def send_each(send, axis, sources, slots):
    slot = slots.at[lax.axis_index(axis)]
    return [send(sources.at[place], slot, {axis: place}) for place in ring(axis)[1:]]


class LineSum:
    def __init__(self, part, buffers, loads, first):
        self.part = part
        self.pair, self.self_rows, self.far_in, self.left_in, self.right_in = buffers
        self.me, self.right, self.far, self.left = ring("x")
        self.to_right, self.to_left = {"x": self.right}, {"x": self.left}
        self.local = [
            pltpu.make_async_copy(part.at[0, self.right], self.pair.at[0], loads.at[first]),
            pltpu.make_async_copy(part.at[1, self.left], self.pair.at[1], loads.at[first + 1]),
            pltpu.make_async_copy(part.at[0, self.me], self.self_rows.at[0], loads.at[first + 2]),
            pltpu.make_async_copy(part.at[1, self.me], self.self_rows.at[1], loads.at[first + 3]),
        ]
        for copy in self.local:
            copy.start()

    def begin(self, send):
        part = self.part
        self.far0 = send(part.at[0, self.far], self.far_in.at[0], self.to_right)
        self.far1 = send(part.at[1, self.far], self.far_in.at[1], self.to_left)
        self.right1 = send(part.at[1, self.right], self.left_in.at[1], self.to_right)
        self.left0 = send(part.at[0, self.left], self.right_in.at[0], self.to_left)

    def middle(self, send):
        pair, far_in = self.pair, self.far_in
        self.local[0].wait()
        self.far0.wait_recv()
        pair[0] = add_low(pair[0], far_in[0])
        self.right0 = send(pair.at[0], self.left_in.at[0], self.to_right)
        self.local[1].wait()
        self.far1.wait_recv()
        pair[1] = add_low(pair[1], far_in[1])
        self.left1 = send(pair.at[1], self.right_in.at[1], self.to_left)

    def end(self, out):
        for copy in self.local[2:]:
            copy.wait()
        self.right1.wait_recv()
        self.left0.wait_recv()
        self.right0.wait_recv()
        self.left1.wait_recv()
        for h in range(2):
            out[h] = (
                self.self_rows[h].astype(F32)
                + self.left_in[h].astype(F32)
                + self.right_in[h].astype(F32)
            )


def line_buffers(width):
    return [pltpu.VMEM((2, BLK, width), BF16)] * 5


def line_scatter_kernel(rider, *refs):
    inputs, outputs = {None: (1, 1), "down": (2, 2), "pieces": (3, 3)}[rider]
    part, *riding = refs[:inputs]
    out, *riding_out = refs[inputs : inputs + outputs]
    *buffers, sends, recvs, loads = refs[inputs + outputs :]
    line = LineSum(part, buffers, loads, 0)
    own = []
    for i, (source, target) in enumerate(zip(riding, riding_out)):
        place = lax.axis_index("dp" if rider == "down" else ("z", "x")[i])
        own.append(pltpu.make_async_copy(source, target.at[place], loads.at[4 + i]))
        own[-1].start()
    if rider == "down":
        meet(around(["x", "dp"]))
    elif rider == "pieces":
        meet(others("z") + others("x"))
    else:
        meet(around(["x"], sibling=False))
    send = Sends(sends, recvs)
    line.begin(send)
    rings = []
    if rider == "down":
        rings = [weight_gather(send, riding[0], riding_out[0], columns_half(512))]
    direct = send_to_others(send, "z", *riding[:1], riding_out[0]) if rider == "pieces" else []
    for gather in rings:
        gather.begin()
    line.middle(send)
    if rider == "pieces":
        direct += send_to_others(send, "x", riding[1], riding_out[1])
    for gather in rings:
        gather.middle()
    for gather in rings:
        gather.near()
    line.end(out)
    for copy in own:
        copy.wait()
    for gather in rings:
        gather.end()
    for gather in rings:
        gather.finish()
    for copy in direct:
        copy.wait_recv()
    send.finish()


def line_scatter(kernel_id, partial, rider=None, riding=()):
    width = partial.shape[1]
    count = {None: 6, "down": 18, "pieces": 12}[rider]
    gathered = {None: (), "down": ((4, 2, 144, 1024),), "pieces": ((4, FF_PIECE, 128),) * 2}
    result = pl.pallas_call(
        functools.partial(line_scatter_kernel, rider),
        out_shape=(jax.ShapeDtypeStruct((2, BLK, width), F32),)
        + tuple(jax.ShapeDtypeStruct(shape, BF16) for shape in gathered[rider]),
        in_specs=[ANY] + [VMEM] * len(riding),
        out_specs=(VMEM,) + (ANY,) * len(riding),
        scratch_shapes=line_buffers(width) + [sems(count), sems(count), sems(6)],
        compiler_params=pltpu.CompilerParams(
            collective_id=kernel_id, has_side_effects=True, vmem_limit_bytes=32 * 2**20
        ),
    )(partial.reshape(2, 4, BLK, width), *riding)
    summed = result[0].reshape(2 * BLK, width)
    return (summed, *result[1:]) if rider else summed


class RingSum:
    def __init__(self, send, axis, chunk, far_in, left_in, right_in):
        self.send, self.chunk = send, chunk
        self.far_in, self.left_in, self.right_in = far_in, left_in, right_in
        self.me, self.right, self.far, self.left = ring(axis)
        self.to_right, self.to_left = {axis: self.right}, {axis: self.left}

    def begin(self):
        send, chunk = self.send, self.chunk
        self.far0 = send(chunk(self.far, 0), self.far_in(0), self.to_right)
        self.far1 = send(chunk(self.far, 1), self.far_in(1), self.to_left)
        self.right1 = send(chunk(self.right, 1), self.left_in(1), self.to_right)
        self.left0 = send(chunk(self.left, 0), self.right_in(0), self.to_left)

    def middle(self):
        send, chunk = self.send, self.chunk
        self.far0.wait_recv()
        mine = chunk(self.right, 0)
        mine[...] = add_low(mine[...], self.far_in(0)[...])
        self.right0 = send(mine, self.left_in(0), self.to_right)
        self.far1.wait_recv()
        mine = chunk(self.left, 1)
        mine[...] = add_low(mine[...], self.far_in(1)[...])
        self.left1 = send(mine, self.right_in(1), self.to_left)

    def end(self, store):
        self.right1.wait_recv()
        self.left0.wait_recv()
        self.right0.wait_recv()
        self.left1.wait_recv()
        for h in range(2):
            store(
                h,
                self.chunk(self.me, h)[...].astype(F32)
                + self.left_in(h)[...].astype(F32)
                + self.right_in(h)[...].astype(F32),
            )


def attend_back_kernel(
    q_ref, kv_ref, qo_ref, ko_ref, mixed_ref, log_ref, grad_ref, packed_y, packed_z,
    dq_ref, dkv_ref, mid_ref,
    dkv_acc, packed, far_in, left_in, right_in, sends, recvs, loads,
):
    local = [
        pltpu.make_async_copy(source, packed.at[i], loads.at[i])
        for i, source in enumerate((packed_y, packed_z))
    ]
    for copy in local:
        copy.start()
    meet(around(["dp", "z"], sibling=False))
    for copy in local:
        copy.wait()
    send = Sends(sends, recvs)
    two = (pl.ds(0, 2), pl.ds(2, 2))
    sums = [
        RingSum(
            send,
            axis,
            lambda place, h, s=s: packed.at[s, place, two[h]],
            lambda h, s=s: far_in.at[s, h],
            lambda h, s=s: left_in.at[s, h],
            lambda h, s=s: right_in.at[s, h],
        )
        for s, axis in enumerate(("dp", "z"))
    ]
    for step in sums:
        step.begin()

    dkv_acc[...] = jnp.zeros_like(dkv_acc)
    for half in range(2):
        cols = slice(half * HALF, (half + 1) * HALF)
        q_order = jnp.concatenate([qo_ref[:, cols]] * 2, axis=1)
        queries = [head_pair(q_ref, kv_head, cols) for kv_head in range(2)]
        grads = [head_pair(grad_ref, kv_head, cols) for kv_head in range(2)]
        logs = [
            jnp.concatenate([log_ref[at : at + 1, cols], log_ref[at + 1 : at + 2, cols]], axis=1)
            for at in (0, 2)
        ]
        dots = [
            jnp.sum(
                head_pair(mixed_ref, kv_head, cols) * grads[kv_head].astype(F32),
                axis=0,
                keepdims=True,
            )
            for kv_head in range(2)
        ]

        def group(g, carried):
            carried = list(carried)
            for k_half in range(half + 1):
                keys = slice(k_half * HALF, (k_half + 1) * HALF)
                for kv_head in range(2):
                    q_t, grad_t = queries[kv_head], grads[kv_head]
                    k_t = kv_ref[g, kv_head, 0:HD, keys]
                    v_t = kv_ref[g, kv_head, HD : 2 * HD, keys]
                    probs = jnp.exp2(scores_of(k_t, q_t) * EXP2_SCALE - logs[kv_head])
                    if k_half == half:
                        allowed = jnp.concatenate([ko_ref[g, keys, :]] * 4, axis=1) <= q_order
                        probs = jnp.where(allowed, probs, 0.0)
                    score_grad = (probs * (scores_of(v_t, grad_t) - dots[kv_head])).astype(BF16)
                    dkv_acc[g, kv_head, HD : 2 * HD, keys] += dot(
                        grad_t, probs.astype(BF16), 1, 1
                    )
                    dkv_acc[g, kv_head, 0:HD, keys] += dot(q_t, score_grad, 1, 1)
                    carried[kv_head] = carried[kv_head] + dot(k_t, score_grad)
            return tuple(carried)

        start = jnp.zeros((HD, 2 * HALF), F32)
        if half == 0:
            query_grads = lax.fori_loop(0, GROUPS, group, (start, start))
            for step in sums:
                step.middle()
        else:
            query_grads = lax.fori_loop(0, GROUPS, group, (start, start))
        for kv_head, dq in enumerate(query_grads):
            for head in range(2):
                at = 2 * kv_head + head
                rows = slice(at * HD, (at + 1) * HD)
                dq_ref[rows, cols] = dq[:, head * HALF : (head + 1) * HALF] * SCORE_SCALE

    def finish(g, unused):
        for kv_head in range(2):
            dkv_ref[g, kv_head, 0:HD, :] = (dkv_acc[g, kv_head, 0:HD, :] * SCORE_SCALE).astype(
                BF16
            )
            dkv_ref[g, kv_head, HD : 2 * HD, :] = dkv_acc[g, kv_head, HD : 2 * HD, :].astype(BF16)
        return unused

    lax.fori_loop(0, GROUPS, finish, 0)
    for s in range(2):

        def keep(half, value, s=s):
            mid_ref[s, 2 * half : 2 * half + 2] = value.astype(BF16)

        sums[s].end(keep)
    send.finish()


def attend_back(kernel_id, q_t, kv_all, q_order, k_order, mixed, log_total, mixed_grad, packed):
    return pl.pallas_call(
        attend_back_kernel,
        out_shape=(
            jax.ShapeDtypeStruct((4 * HD, ROWS), F32),
            jax.ShapeDtypeStruct((GROUPS, 2, 2 * HD, ROWS), BF16),
            jax.ShapeDtypeStruct((2, 4, FF_PIECE, 128), BF16),
        ),
        in_specs=[VMEM] * 7 + [ANY] * 2,
        out_specs=(VMEM,) * 3,
        scratch_shapes=[pltpu.VMEM((GROUPS, 2, 2 * HD, ROWS), F32)]
        + [pltpu.VMEM((2, 4, 4, FF_PIECE, 128), BF16)]
        + [pltpu.VMEM((2, 2, 2, FF_PIECE, 128), BF16)] * 3
        + [sems(12), sems(12), sems(2)],
        compiler_params=pltpu.CompilerParams(
            collective_id=kernel_id, has_side_effects=True, vmem_limit_bytes=48 * 2**20
        ),
    )(q_t, kv_all, q_order, k_order, mixed, log_total, mixed_grad, *packed)


def sequence_scatter_kernel(
    part, mid, line_part, out, piece, line_out,
    own, other, far_in, left_in, right_in, slots, pair, self_rows, line_far, line_left, line_right,
    sends, recvs, loads,
):
    core = lax.axis_index("core")
    me, right, far, left = ring("z")
    order = (far, right, left, me)
    local = [
        pltpu.make_async_copy(part.at[place, core], own.at[place], loads.at[i])
        for i, place in enumerate(order)
    ]
    for copy in local:
        copy.start()
    line = LineSum(line_part, (pair, self_rows, line_far, line_left, line_right), loads, 4)
    to_sib = {"core": 1 - core}
    meet(others("z") + others("dp") + around(["x"], sibling=False) + [to_sib])
    send = Sends(sends, recvs)
    shared = [send(part.at[place, 1 - core], other.at[place], to_sib) for place in order]

    def merge(i):
        local[i].wait()
        shared[i].wait_recv()
        own[order[i]] = add_low(own[order[i]], other[order[i]])

    ring_sum = RingSum(
        send,
        "z",
        lambda place, h: own.at[place, h],
        lambda h: far_in.at[h],
        lambda h: left_in.at[h],
        lambda h: right_in.at[h],
    )
    for i in range(3):
        merge(i)
    ring_sum.begin()
    line.begin(send)
    direct = send_each(send, "dp", mid.at[1], slots.at[1])
    merge(3)
    ring_sum.middle()
    direct += send_each(send, "z", mid.at[0], slots.at[0])
    line.middle(send)

    def store(h, value):
        out[h] = value

    ring_sum.end(store)
    line.end(line_out)
    for copy in direct:
        copy.wait_recv()
    for s, axis in enumerate(("z", "dp")):
        me, *places = ring(axis)
        total = mid[s, me].astype(F32)
        for place in places:
            total = total + slots[s, place].astype(F32)
        piece[s] = total.astype(BF16)
    send.finish()


def sequence_scatter(kernel_id, partial, mid, line_part):
    buffer = pltpu.VMEM((2, 2 * HD, ROWS), BF16)
    wide = pltpu.VMEM((4, 2, 2 * HD, ROWS), BF16)
    return pl.pallas_call(
        sequence_scatter_kernel,
        out_shape=(
            jax.ShapeDtypeStruct((2, 2 * HD, ROWS), F32),
            jax.ShapeDtypeStruct((2, FF_PIECE, 128), BF16),
            jax.ShapeDtypeStruct((2, BLK, 1024), F32),
        ),
        in_specs=[ANY, VMEM, ANY],
        out_specs=(VMEM,) * 3,
        scratch_shapes=[wide, wide, buffer, buffer, buffer]
        + [pltpu.VMEM((2, 4, FF_PIECE, 128), BF16)]
        + line_buffers(1024)
        + [sems(22), sems(22), sems(8)],
        compiler_params=pltpu.CompilerParams(
            collective_id=kernel_id, has_side_effects=True, vmem_limit_bytes=32 * 2**20
        ),
    )(partial.reshape(4, 2, 2, 2 * HD, ROWS), mid, line_part)


def tail_kernel(
    qkv, out, gains, ff_a, ff_b, gain_sums, ff_out, qkv_out, out_out,
    qkv_own, qkv_sib, out_own, out_sib, gain_slots,
    packed, slots_y, mid, slots_z, qkv_line, out_x, out_y,
    sends, recvs, loads,
):
    core = lax.axis_index("core")
    me_x, me_y, me_z = lax.axis_index("x"), lax.axis_index("dp"), lax.axis_index("z")
    to_sib = {"core": 1 - core}
    views = [
        (lambda c: qkv.at[:, :, c], qkv_own, qkv_sib),
        (lambda c: out.at[:, c], out_own, out_sib),
    ]
    local = [
        pltpu.make_async_copy(view(core), mine, loads.at[i])
        for i, (view, mine, unused) in enumerate(views)
    ]
    own = [
        pltpu.make_async_copy(ff_a, ff_out.at[0, core, :, me_x], loads.at[2]),
        pltpu.make_async_copy(ff_b, ff_out.at[1, core, me_z], loads.at[3]),
    ]
    for copy in local + own:
        copy.start()
    meet(others("z") + others("dp") + others("x") + [to_sib])
    send = Sends(sends, recvs)

    def arrived(copies):
        for copy in copies:
            copy.wait_recv()

    def gain_begin(step, axis, value):
        place = lax.axis_index(axis)
        gain_slots[step, place] = value
        slot = gain_slots.at[step, place]
        return [send(slot, slot, to) for to in ([to_sib] if axis == "core" else others(axis))]

    def gain_end(step, copies):
        arrived(copies)
        total = gain_slots[step, 0] + gain_slots[step, 1]
        for place in range(2, 4 if step else 2):
            total = total + gain_slots[step, place]
        return total

    gain_copies = gain_begin(0, "core", gains[...])
    shared = [send(view(1 - core), theirs, to_sib) for view, unused, theirs in views]
    two = (pl.ds(0, 2), pl.ds(2, 2))
    bulk = [
        RingGather(
            send,
            "x",
            lambda place, core, half: ff_out.at[0, core, two[half], place],
            lambda half: ff_a.at[two[half]],
            sibling=True,
            share_own=True,
        ),
        RingGather(
            send,
            "z",
            lambda place, core, half: ff_out.at[1, core, place, two[half]],
            lambda half: ff_b.at[two[half]],
            sibling=True,
            share_own=True,
        ),
    ]
    for gather in bulk:
        gather.begin()
    for copy in local:
        copy.wait()
    arrived(shared)

    def pack(y, unused):
        for z in range(4):
            for t in range(4):
                cols = slice(t * 128, (t + 1) * 128)
                packed[y, z, t * 32 : (t + 1) * 32, :] = add_low(
                    qkv_own[y, z, :, cols], qkv_sib[y, z, :, cols]
                )
            for s in range(2):
                cols = slice(s * 512 + z * 128, s * 512 + (z + 1) * 128)
                packed[y, z, 128 + s * 32 : 160 + s * 32, :] = add_low(
                    out_own[y, :, cols], out_sib[y, :, cols]
                )
        return unused

    lax.fori_loop(0, 4, pack, 0)
    to_y = send_each(send, "dp", packed, slots_y)
    gain_copies = gain_begin(1, "z", gain_end(0, gain_copies))
    for gather in bulk:
        gather.middle()
    gain_copies = gain_begin(2, "dp", gain_end(1, gain_copies))
    arrived(to_y)
    total = packed[me_y].astype(F32)
    for place in ring("dp")[1:]:
        total = total + slots_y[place].astype(F32)
    mid[...] = total.astype(BF16)
    to_z = send_each(send, "z", mid, slots_z)
    gain_copies = gain_begin(3, "x", gain_end(2, gain_copies))
    arrived(to_z)
    total = mid[me_z].astype(F32)
    for place in ring("z")[1:]:
        total = total + slots_z[place].astype(F32)
    total = total.astype(BF16)
    qkv_line[me_z] = total[0:128]
    out_x[me_x] = total[128:192]
    qkv_z = send_to_others(send, "z", qkv_line.at[me_z], qkv_line)
    out_line = send_to_others(send, "x", out_x.at[me_x], out_x)
    for gather in bulk:
        gather.near()
    arrived(out_line)
    out_y[me_y] = out_x[me_y]
    out_places = send_each(send, "dp", out_x, out_y)
    arrived(qkv_z)
    own.append(pltpu.make_async_copy(qkv_line, qkv_out.at[core, me_x], loads.at[4]))
    own[-1].start()
    qkv_x = send_to_others(send, "x", qkv_line, qkv_out.at[core])
    for gather in bulk:
        gather.end()
    arrived(out_places)
    own.append(pltpu.make_async_copy(out_y, out_out.at[core, me_z], loads.at[5]))
    own[-1].start()
    out_z = send_to_others(send, "z", out_y, out_out.at[core])
    gain_sums[...] = gain_end(3, gain_copies)
    for copy in own:
        copy.wait()
    arrived(qkv_x)
    last = [send(qkv_out.at[core], qkv_out.at[core], to_sib)]
    arrived(out_z)
    last.append(send(out_out.at[core], out_out.at[core], to_sib))
    for gather in bulk:
        gather.finish()
    arrived(last)
    send.finish()


def tail(kernel_id, qkv, out, gains, ff_a, ff_b):
    def vm(*shape):
        return pltpu.VMEM(shape, BF16)

    return pl.pallas_call(
        tail_kernel,
        out_shape=(
            jax.ShapeDtypeStruct((24, 128), F32),
            jax.ShapeDtypeStruct((2, 2, 4, 4, FF_PIECE, 128), BF16),
            jax.ShapeDtypeStruct((2, 4, 4, 128, 128), BF16),
            jax.ShapeDtypeStruct((2, 4, 4, 64, 128), BF16),
        ),
        in_specs=[ANY] * 2 + [VMEM] * 3,
        out_specs=(VMEM, ANY, ANY, ANY),
        scratch_shapes=[
            vm(4, 4, 32, 512), vm(4, 4, 32, 512),
            vm(4, 32, 1024), vm(4, 32, 1024),
            pltpu.VMEM((4, 4, 24, 128), F32),
            vm(4, 4, 192, 128), vm(4, 4, 192, 128),
            vm(4, 192, 128), vm(4, 192, 128),
            vm(4, 128, 128), vm(4, 64, 128), vm(4, 64, 128),
            sems(64), sems(64), sems(6),
        ],
        compiler_params=pltpu.CompilerParams(
            collective_id=kernel_id, has_side_effects=True, vmem_limit_bytes=48 * 2**20
        ),
    )(qkv.reshape(4, 4, 2, 32, 512), out.reshape(4, 2, 32, 1024), gains, ff_a, ff_b)


def unpack_rows_kernel(ff_pieces, qkv, gate, up, query, key, value):
    for x in range(4):
        for s, target in enumerate((gate, up)):
            row = jnp.concatenate(
                [
                    ff_pieces[s, 0, 0, x, t * 32 : (t + 1) * 32, :].astype(F32)
                    for t in range(9)
                ],
                axis=1,
            )
            for part in range(4):
                begin = part * 1152 + x * 288
                target[:, begin : begin + 288] = row[:, part * 288 : (part + 1) * 288]
        for t in range(2):
            cols = slice(x * 256 + t * 128, x * 256 + (t + 1) * 128)
            query[:, cols] = qkv[0, x, 0, t * 32 : (t + 1) * 32, :].astype(F32)
        cols = slice(x * 128, (x + 1) * 128)
        key[:, cols] = qkv[0, x, 0, 64:96, :].astype(F32)
        value[:, cols] = qkv[0, x, 0, 96:128, :].astype(F32)


def unpack_columns_kernel(ff_pieces, pieces, down, out):
    for s in range(2):
        for z in range(4):
            cols = slice(s * 512 + z * 128, s * 512 + (z + 1) * 128)
            down[:, cols] = ff_pieces[s, 0, z, 0].astype(F32)
            out[:, cols] = pieces[0, z, 0, s * 32 : (s + 1) * 32, :].astype(F32)


def unpack(ff_pieces, qkv, out):
    rows = pl.pallas_call(
        unpack_rows_kernel,
        grid=(4, 2),
        out_shape=tuple(
            jax.ShapeDtypeStruct((256, width), F32) for width in (4608, 4608, 1024, 512, 512)
        ),
        in_specs=[
            pl.BlockSpec((2, 1, 1, 4, 288, 128), lambda z, c: (0, c, z, 0, 0, 0)),
            pl.BlockSpec((1, 4, 1, 128, 128), lambda z, c: (c, 0, z, 0, 0)),
        ],
        out_specs=tuple(
            pl.BlockSpec((32, width), lambda z, c: (2 * z + c, 0))
            for width in (4608, 4608, 1024, 512, 512)
        ),
        compiler_params=pltpu.CompilerParams(vmem_limit_bytes=32 * 2**20),
    )(ff_pieces, qkv)
    columns = pl.pallas_call(
        unpack_columns_kernel,
        grid=(4, 2),
        out_shape=(
            jax.ShapeDtypeStruct((1152, 1024), F32),
            jax.ShapeDtypeStruct((256, 1024), F32),
        ),
        in_specs=[
            pl.BlockSpec((2, 1, 4, 1, 144, 128), lambda x, c: (0, c, 0, x, 2, 0)),
            pl.BlockSpec((1, 4, 1, 64, 128), lambda x, c: (c, 0, x, 0, 0)),
        ],
        out_specs=(
            pl.BlockSpec((144, 1024), lambda x, c: (2 * x + c, 0)),
            pl.BlockSpec((32, 1024), lambda x, c: (2 * x + c, 0)),
        ),
        compiler_params=pltpu.CompilerParams(vmem_limit_bytes=32 * 2**20),
    )(ff_pieces, out)
    return rows + columns


def after(value, anchor):
    return lax.optimization_barrier((value, anchor))[0]


def ff_columns_kernel(gate, up, gate_own, up_own):
    x_at = lax.axis_index("x")
    for x in range(4):

        @pl.when(x_at == x)
        def take(x=x):
            for source, target in ((gate, gate_own), (up, up_own)):
                for part in range(4):
                    begin = part * 1152 + x * 288
                    target[:, part * 288 : (part + 1) * 288] = (
                        source[:, begin : begin + 288].astype(F32).astype(BF16)
                    )


def ff_columns(gate, up):
    return pl.pallas_call(
        ff_columns_kernel,
        grid=(4,),
        out_shape=(jax.ShapeDtypeStruct((256, 1152), BF16),) * 2,
        in_specs=[pl.BlockSpec((64, 4608), lambda i: (i, 0))] * 2,
        out_specs=(pl.BlockSpec((64, 1152), lambda i: (i, 0)),) * 2,
        compiler_params=pltpu.CompilerParams(vmem_limit_bytes=32 * 2**20),
    )(gate, up)


SWAP = [(a * 4 + b, b * 4 + a) for a in range(4) for b in range(4)]


def on_device(
    hidden_in,
    positions,
    block_of,
    attn_gain,
    query_weight,
    key_weight,
    value_weight,
    out_weight,
    query_gain,
    key_gain,
    ffn_gain,
    gate_weight,
    up_weight,
    down_weight,
    cotangent,
):
    z_at = lax.axis_index("z")
    x_at = lax.axis_index("x")
    core_at = lax.axis_index("core")
    dp_at = lax.axis_index("dp")

    hidden_rows = hidden_in[0]
    grad_rows = cotangent[0]

    in_block = jnp.arange(BLK, dtype=jnp.int32)
    blocks = block_of.reshape(4, 4, 2, 2).transpose(0, 2, 3, 1)
    order_all = (blocks[..., None] * BLK + in_block).reshape(GROUPS, ROWS)
    own_order = lax.dynamic_index_in_dim(order_all, z_at * 2 + core_at, 0, keepdims=True)
    k_order = blocks.reshape(GROUPS, 8, 1, 1) * BLK + lax.broadcasted_iota(
        jnp.int32, (GROUPS, 8, BLK, 128), 2
    )
    k_order = k_order.reshape(GROUPS, ROWS, 128)
    own_slot = 2 * (z_at * 8 + x_at * 2 + core_at)
    first_block = lax.dynamic_index_in_dim(block_of, own_slot, 0, keepdims=False)
    offset = positions[0, 0] - first_block * BLK
    frequency = ROPE_BASE ** (-2.0 * jnp.arange(HD // 2, dtype=F32) / HD)
    angles = (own_order + offset).astype(F32) * frequency[:, None]
    cosine, sine = jnp.cos(angles), jnp.sin(angles)

    def swapped_rows(weight, rows):
        own = lax.dynamic_slice_in_dim(weight, x_at * rows, rows, axis=0)
        return lax.ppermute(own, ("dp", "x"), SWAP)

    gate_own, up_own = ff_columns(gate_weight, up_weight)
    down_own = lax.dynamic_slice_in_dim(down_weight, x_at * 288, 288, axis=0)
    gains_own = jnp.pad(
        jnp.concatenate([attn_gain, ffn_gain, query_gain, key_gain]), (0, 2048 - 544)
    )
    hidden = hidden_rows.astype(F32)
    line_hidden, qkv_weight, gains = start_gather(
        0, hidden_rows, query_weight, key_weight, value_weight, gains_own.reshape(16, 128)
    )
    gains = gains.reshape(4, 2048).astype(F32)
    attn_gain_all = gains[:, 0:256].reshape(1024)
    ffn_gain_all = gains[:, 256:512].reshape(1024)
    query_gain_all = gains[:, 512:528].reshape(HD)
    key_gain_all = gains[:, 528:544].reshape(HD)
    out_own = swapped_rows(after(out_weight, line_hidden), 64)
    branch_low = lax.all_gather(after(grad_rows, line_hidden).reshape(2, BLK, 1024), "x", axis=1).reshape(ROWS, 1024)
    attn_in = rms_scale(line_hidden.astype(F32), attn_gain_all).astype(BF16)
    qkv_t = dot(qkv_weight, attn_in, 0, 1)
    q_rot, q_back = jax.vjp(
        lambda r, g: head_norm_rope(r, g, cosine, sine),
        qkv_t[0:256].reshape(4, HD, ROWS),
        query_gain_all,
    )
    k_rot, k_back = jax.vjp(
        lambda r, g: head_norm_rope(r, g, cosine, sine),
        qkv_t[256:384].reshape(2, HD, ROWS),
        key_gain_all,
    )
    q_low = q_rot.reshape(4 * HD, ROWS).astype(BF16)
    kv_low = jnp.concatenate([k_rot, qkv_t[384:512].reshape(2, HD, ROWS)], axis=1).astype(BF16)
    kv_all, gate_slice, out_slice = sequence_gather(
        1, kv_low, gate_own, out_own
    )
    mixed, attn_low, log_total, up_slice = attend(
        10, q_low, kv_all, own_order, k_order, up_own
    )
    attn_rows, down_slice = line_scatter(
        2, dot(attn_low, out_slice, 0, 0).astype(BF16), "down", (down_own.reshape(2, 144, 1024),)
    )
    down_slice = down_slice.reshape(1152, 1024)
    after_attn = hidden + attn_rows
    normed_ffn, norm_ffn_back = jax.vjp(rms_scale, after_attn, ffn_gain_all)
    ffn_in = line_gather(3, normed_ffn.astype(BF16))
    gate_proj = dot(ffn_in, gate_slice)
    up_proj = dot(ffn_in, up_slice)
    activated, swiglu_back = jax.vjp(lambda g, u: jax.nn.silu(g) * u, gate_proj, up_proj)
    activated_low = activated.astype(BF16)
    residual_grad = grad_rows.astype(F32)
    activated_grad = dot(branch_low, down_slice, 1, 1)
    gate_grad, up_grad = swiglu_back(activated_grad)
    gate_grad_low = gate_grad.astype(BF16)
    up_grad_low = up_grad.astype(BF16)
    ffn_in_grad = line_scatter(
        5,
        (dot(gate_grad_low, gate_slice, 1, 1) + dot(up_grad_low, up_slice, 1, 1)).astype(BF16),
    )
    mid_part, ffn_gain_part = norm_ffn_back(ffn_in_grad)
    mid_grad = residual_grad + mid_part
    branch_attn, packed_y, packed_z = line_gather_pack(
        6,
        mid_grad.astype(BF16),
        dot(ffn_in, gate_grad_low, 0, 0).astype(BF16),
        dot(ffn_in, up_grad_low, 0, 0).astype(BF16),
        dot(activated_low, branch_low, 0, 0).astype(BF16),
    )
    out_part = dot(activated_low, down_slice).astype(BF16).reshape(2, 4, BLK, 1024)

    mixed_grad = dot(out_slice, branch_attn, 1, 1).astype(BF16)
    q_grad, kv_grad_all, ff_mid = attend_back(
        11, q_low, kv_all, own_order, k_order, mixed, log_total, mixed_grad, (packed_y, packed_z)
    )
    kv_grad, ff_piece, out_rows = sequence_scatter(7, kv_grad_all, ff_mid, out_part)
    layer_out = (after_attn + out_rows.reshape(2 * BLK, 1024)).astype(BF16)
    q_pre, q_gain_part = q_back(q_grad.reshape(4, HD, ROWS))
    k_pre, k_gain_part = k_back(kv_grad[:, 0:HD])
    qkv_pre = jnp.concatenate(
        [
            q_pre.reshape(4 * HD, ROWS),
            k_pre.reshape(2 * HD, ROWS),
            kv_grad[:, HD:].reshape(2 * HD, ROWS),
        ],
        axis=0,
    ).astype(BF16)
    attn_in_grad, ff_a, ff_b = line_scatter(
        8,
        dot(qkv_pre, qkv_weight, 0, 1).astype(BF16),
        "pieces",
        (ff_piece[0], ff_piece[1]),
    )
    unused, norm_attn_back = jax.vjp(rms_scale, hidden, attn_gain_all)
    hidden_part, attn_gain_part = norm_attn_back(attn_in_grad)
    input_grad = (mid_grad + hidden_part).astype(BF16)

    gain_parts = jnp.concatenate([attn_gain_part, ffn_gain_part, q_gain_part, k_gain_part])
    gain_parts = jnp.pad(gain_parts, (0, 3072 - 2176)).reshape(24, 128)

    def own_slice(begin, size):
        return lax.dynamic_slice_in_dim(
            gain_sums[begin : begin + size], dp_at * (size // 4), size // 4
        )

    gain_sums, ff_pieces, qkv_pieces, out_pieces = tail(
        9,
        dot(attn_in, qkv_pre, 0, 1).astype(BF16),
        dot(attn_low, branch_attn).astype(BF16),
        gain_parts,
        ff_a,
        ff_b,
    )
    gain_sums = gain_sums.reshape(3072)
    gate_all, up_all, query_all, key_all, value_all, down_all, out_all = unpack(
        ff_pieces, qkv_pieces, out_pieces
    )
    return (
        layer_out[None],
        input_grad[None],
        own_slice(0, 1024),
        query_all,
        key_all,
        value_all,
        out_all,
        own_slice(2048, 64),
        own_slice(2112, 64),
        own_slice(1024, 1024),
        gate_all,
        up_all,
        down_all,
    )


def solution(mesh):
    fine = Mesh(mesh.devices.reshape(4, 4, 4, 2), ("dp", "z", "x", "core"))
    ctx = ("z", "x", "core")
    rows = P("dp", ctx, None)
    vector, matrix = P("dp"), P("dp", None)
    return jax.shard_map(
        on_device,
        mesh=fine,
        in_specs=(rows, P("dp", ctx), P(), vector)
        + (matrix,) * 4
        + (vector,) * 3
        + (matrix,) * 3
        + (rows,),
        out_specs=(rows, rows, vector) + (matrix,) * 4 + (vector,) * 3 + (matrix,) * 3,
        check_vma=False,
    )
```

time: 366 us -> 335 us (0.915)
  Pallas kernels: 258 us -> 231 us
  starting transfers between devices: 6.73 us -> 2.19 us
    pallas_call x4, Pallas kernels: 89.1 us -> 71.8 us  [the longest x1 36.6 us: tail(): pl.pallas_call(tail_kernel, out_shape=(jax.ShapeDtypeStruct((24, 128), F3...]
    pallas_call x3, Pallas kernels: 54.4 us -> 46.6 us  [line_scatter(): pl.pallas_call(functools.partial(line_scatter_kernel, rider), out_shape=(...]
    unnamed x134 -> x148, local copies, waits for them, and re-layouts: 12.6 us -> 20.2 us
    pallas_call x1, Pallas kernels: 34.2 us -> 27.7 us  [attend_back(): pl.pallas_call(attend_back_kernel, out_shape=(jax.ShapeDtypeStruct((4 * H...]
    dynamic_slice x4 -> x1, local copies, waits for them, and re-layouts: 6.45 us -> 0.04 us  [on_device(): down_own = lax.dynamic_slice_in_dim(down_weight, x_at * 288, 288, axis=0)]
    pallas_call x1, Pallas kernels: 14.8 us -> 19.3 us  [attend(): pl.pallas_call(attend_kernel, out_shape=(jax.ShapeDtypeStruct((4 * HD, RO...]
  transfers between devices with their start and end apart: 6 -> 2, of which waited for: 0 -> 0; matrix products, arithmetic and copies ran while one was open for 12% -> 10% of each run, Pallas kernels for 27% -> 22%
where the time goes in v4:
time: 335 us; the launch traced here: 334 us
  Pallas kernels  231 us (69%)
  local copies, waits for them, and re-layouts  37.8 us (11%)
  matrix products  26.4 us (8%)
  other arithmetic  20.3 us (6%)
  between operations  15.7 us (5%)
    pallas_call x3, Pallas kernels, line_scatter(): pl.pallas_call(functools.partial(line_scatter_kernel, rider), out_shape=(...  46.6 us
    pallas_call x1, Pallas kernels, tail(): pl.pallas_call(tail_kernel, out_shape=(jax.ShapeDtypeStruct((24, 128), F3...  36.6 us
    pallas_call x1, Pallas kernels, attend_back(): pl.pallas_call(attend_back_kernel, out_shape=(jax.ShapeDtypeStruct((4 * H...  27.7 us
    dot_general x15, matrix products, dot(): lax.dot_general(left, right, (((left_dim,), (right_dim,)), ((), ())), pre...  26.4 us
    pallas_call x1, Pallas kernels, sequence_gather(): pl.pallas_call(sequence_gather_kernel, out_shape=(jax.ShapeDtypeStruct((4...  24.5 us
    pallas_call x1, Pallas kernels, sequence_scatter(): pl.pallas_call(sequence_scatter_kernel, out_shape=(jax.ShapeDtypeStruct((...  21.6 us
    unnamed x148, local copies, waits for them, and re-layouts  20.2 us
    pallas_call x1, Pallas kernels, attend(): pl.pallas_call(attend_kernel, out_shape=(jax.ShapeDtypeStruct((4 * HD, RO...  19.3 us
  transfers between devices with their start and end apart: 2, of which 0 were waited for; matrix products, arithmetic and copies ran while one was open for 10% of the time, Pallas kernels for 22%

profile of v4, /device:TPU:1, one launch (start us, length us, event | category | flops | bytes accessed | tf_op | source)
XLA Modules:
  0.0 333.9 jit_solution(16018315791425419052)
XLA Ops:
  7.2 1.5 fusion.33.gains
  8.8 18.2 %shard_map.246 = (bf16[2,4,64,1024]{3,2,1,0:T(8,128)(2,1)}, bf16[4,2,128,512]{3,2,1,0:T(8,128)(2,1)}, bf16[4,16,128]{2,1,0:T(8,128)(2,1)}) custom-call(bf16[2,64,1024]{2,1,0:T(8,128)(2,1)} %bitcast.170, bf16[256,1024]{1,0:T(8,128)(2,1)} %query.1, bf16[256,512]{1,0:T(8,128)(2,1)} %key.1, bf16[256,512]{1,0:T(8,128)(2,1)} %value.1, bf16[16,128]{1,0:T(8,128)(2,1)} %fusion.33.gains), custom_call_target="tpu_custom_call" | custom-call | tf_op jit(solution)/shard_map/pallas_call | solution.py:244
  27.0 1.7 constant_dynamic-slice_fusion.1
  28.6 2.2 collective-permute-start
  30.8 0.7 convert_bitcast_fusion.1
  32.2 1.5 fusion.4
  34.6 2.0 fusion.42
  37.8 0.7 mul.571
  39.3 0.9 multiply_multiply_fusion
  40.9 1.0 multiply_cosine_fusion
  41.9 0.8 multiply_multiply_fusion.1
  42.7 1.8 subtract_convert_fusion
  44.5 0.7 subtract_convert_fusion.1
  45.8 1.3 iota.22
  47.1 1.4 add.210
  48.5 1.4 add.211
  50.0 2.5 broadcast_add_fusion.ko_ref
  52.5 1.0 pad_maximum_fusion.1
  53.5 1.1 slice.128
  54.6 0.7 pad_maximum_fusion.2.kv
  55.3 1.7 slice.94
  57.7 1.7 copy-done.9
  59.4 1.7 copy-done.10
  61.0 0.8 shard_map.247
  61.8 0.8 copy-done.13
  62.6 0.8 copy-done.15
  63.5 24.5 %shard_map.248 = (bf16[4,2,2,128,512]{4,3,2,1,0:T(8,128)(2,1)}, bf16[4,2,128,1152]{3,2,1,0:T(8,128)(2,1)}, bf16[4,2,32,1024]{3,2,1,0:T(8,128)(2,1)}) custom-call(bf16[2,128,512]{2,1,0:T(8,128)(2,1)} %pad_maximum_fusion.2.kv, bf16[2,128,1152]{2,1,0:T(8,128)(2,1)} %bitcast.162, bf16[2,32,1024]{2,1,0:T(8,128)(2,1)} %bitcast.14.out), custom_call_target="tpu_custom_call" | custom-call | tf_op jit(solution)/shard_map/pallas_call | solution.py:409
  88.0 1.6 copy-done.3
  89.6 1.6 copy-done.4
  91.2 1.1 copy-done.14
  92.3 19.3 %shard_map.249 = (f32[256,512]{1,0:T(8,128)S(1)}, bf16[256,512]{1,0:T(8,128)(2,1)S(1)}, f32[4,512]{1,0:T(4,128)S(1)}, bf16[4,2,128,1152]{3,2,1,0:T(8,128)(2,1)S(1)}) custom-call(bf16[256,512]{1,0:T(8,128)(2,1)S(1)} %bitcast.153, bf16[8,2,128,512]{3,2,1,0:T(8,128)(2,1)S(1)} %bitcast.144, s32[1,512]{1,0:T(1,128)S(1)} %get-tuple-element.100.qo_ref, ...), custom_call_target="tpu_custom_call" | custom-call | tf_op jit(solution)/shard_map/pallas_call | solution.py:482
  112.0 16.4 %shard_map.250 = (f32[2,64,1024]{2,1,0:T(8,128)S(1)}, bf16[4,2,144,1024]{3,2,1,0:T(8,128)(2,1)S(1)}) custom-call(bf16[2,4,64,1024]{3,2,1,0:T(8,128)(2,1)S(1)} %bitcast.148, bf16[2,144,1024]{2,1,0:T(8,128)(2,1)S(1)} %bitcast.152), custom_call_target="tpu_custom_call" | custom-call | tf_op jit(solution)/shard_map/pallas_call | solution.py:618
  128.4 1.4 copy-done.26
  130.0 0.8 multiply_convert_fusion.4.src
  130.8 12.9 %shard_map.251 = bf16[2,4,64,1024]{3,2,1,0:T(8,128)(2,1)} custom-call(bf16[2,64,1024]{2,1,0:T(8,128)(2,1)} %multiply_convert_fusion.4.src), custom_call_target="tpu_custom_call" | custom-call | tf_op jit(solution)/shard_map/pallas_call | solution.py:279
  144.3 4.9 %fusion.44 = f32[512,1152]{1,0:T(8,128)} fusion(bf16[512,1024]{1,0:T(8,128)(2,1)} %bitcast.182, bf16[1024,1152]{1,0:T(8,128)(2,1)} %bitcast.166), kind=kOutput, calls=%fused_computation.131 | convolution fusion | flops 1207959552 | bytes 5767168 | tf_op jit(solution)/shard_map/dot_general | solution.py:30
  149.2 3.7 %fusion.43 = f32[512,1152]{1,0:T(8,128)S(1)} fusion(bf16[512,1024]{1,0:T(8,128)(2,1)} %bitcast.211, bf16[1152,1024]{1,0:T(8,128)(2,1)} %bitcast.168), kind=kOutput, calls=%fused_computation.130 | convolution fusion | flops 1207959552 | bytes 5767168 | tf_op jit(solution)/shard_map/dot_general | solution.py:30
  152.9 2.4 multiply_convert_fusion
  155.4 1.5 fusion.45
  156.9 1.6 convolution_convert_fusion.1
  158.5 1.4 convolution_convert_fusion
  160.2 1.5 convolution_convert_fusion.3
  161.7 1.6 convolution_convert_fusion.2
  163.3 1.8 add_convert_fusion
  165.1 11.8 %shard_map.252 = f32[2,64,1024]{2,1,0:T(8,128)S(1)} custom-call(bf16[2,4,64,1024]{3,2,1,0:T(8,128)(2,1)S(1)} %bitcast.159), custom_call_target="tpu_custom_call" | custom-call | tf_op jit(solution)/shard_map/pallas_call | solution.py:618
  176.8 0.7 multiply_reduce_fusion.1
  177.8 13.5 %shard_map.253 = (bf16[2,4,64,1024]{3,2,1,0:T(8,128)(2,1)S(1)}, bf16[4,4,432,128]{3,2,1,0:T(8,128)(2,1)S(1)}, bf16[4,4,432,128]{3,2,1,0:T(8,128)(2,1)S(1)}) custom-call(bf16[2,64,1024]{2,1,0:T(8,128)(2,1)S(1)} %fusion.16.src, bf16[4,4,2,32,1152]{4,3,2,1,0:T(8,128)(2,1)S(1)} %bitcast.151, bf16[4,4,2,32,1152]{4,3,2,1,0:T(8,128)(2,1)S(1)} %bitcast.149, ...), custom_call_target="tpu_custom_call" | custom-call | tf_op jit(solution)/shard_map/pallas_call | solution.py:348
  191.9 27.7 %shard_map.254 = (f32[256,512]{1,0:T(8,128)S(1)}, bf16[8,2,128,512]{3,2,1,0:T(8,128)(2,1)}, bf16[2,4,432,128]{3,2,1,0:T(8,128)(2,1)S(1)}) custom-call(bf16[256,512]{1,0:T(8,128)(2,1)S(1)} %bitcast.154, bf16[8,2,128,512]{3,2,1,0:T(8,128)(2,1)} %bitcast.143, s32[1,512]{1,0:T(1,128)S(1)} %get-tuple-element.100.qo_ref, s32[8,512,128]{2,1,0:T(8,128)} %broadcast_add_fusion.ko_ref, ...), custom_call_target="tpu_custom_call" | custom-call | tf_op jit(solution)/shard_map/pallas_call | solution.py:773
  219.6 1.8 copy-done.11
  221.4 21.6 %shard_map.255 = (f32[2,128,512]{2,1,0:T(8,128)S(1)}, bf16[2,432,128]{2,1,0:T(8,128)(2,1)S(1)}, f32[2,64,1024]{2,1,0:T(8,128)S(1)}) custom-call(bf16[4,2,2,128,512]{4,3,2,1,0:T(8,128)(2,1)S(1)} %bitcast.156, bf16[2,4,432,128]{3,2,1,0:T(8,128)(2,1)S(1)} %get-tuple-element.72.mid, bf16[2,4,64,1024]{3,2,1,0:T(8,128)(2,1)S(1)} %bitcast.160), custom_call_target="tpu_custom_call" | custom-call | tf_op jit(solution)/shard_map/pallas_call | solution.py:854
  243.0 0.7 copy-done.22
  244.4 0.8 multiply_add_fusion.3
  245.1 1.3 reduce_sum.126
  246.9 1.4 multiply_reduce_fusion.6
  249.9 0.8 convolution_convert_fusion.6
  250.7 18.5 %shard_map.256 = (f32[2,64,1024]{2,1,0:T(8,128)S(1)}, bf16[4,432,128]{2,1,0:T(8,128)(2,1)S(1)}, bf16[4,432,128]{2,1,0:T(8,128)(2,1)S(1)}) custom-call(bf16[2,4,64,1024]{3,2,1,0:T(8,128)(2,1)S(1)} %bitcast.158, bf16[432,128]{1,0:T(8,128)(2,1)S(1)} %get-tuple-element.115.refs_1_, bf16[432,128]{1,0:T(8,128)(2,1)S(1)} %get-tuple-element.114.refs_2_), custom_call_target="tpu_custom_call" | custom-call | tf_op jit(solution)/shard_map/pallas_call | solution.py:618
  269.4 1.9 convolution_convert_fusion.5
  271.7 1.2 copy-done.12
  272.9 1.0 copy-done.21
  273.9 36.6 %shard_map.257 = (f32[24,128]{1,0:T(8,128)S(1)}, bf16[2,2,4,4,432,128]{5,4,3,2,1,0:T(8,128)(2,1)}, bf16[2,4,4,128,128]{4,3,2,1,0:T(8,128)(2,1)S(1)}, bf16[2,4,4,64,128]{4,3,2,1,0:T(8,128)(2,1)S(1)}) custom-call(bf16[4,4,2,32,512]{4,3,2,1,0:T(8,128)(2,1)S(1)} %bitcast.157, bf16[4,2,32,1024]{3,2,1,0:T(8,128)(2,1)S(1)} %bitcast.155, ...), custom_call_target="tpu_custom_call" | custom-call | tf_op jit(solution)/shard_map/pallas_call | solution.py:1011
  310.5 3.0 copy-done.2
  313.5 5.7 %shard_map.258 = (f32[256,4608]{1,0:T(8,128)}, f32[256,4608]{1,0:T(8,128)}, f32[256,1024]{1,0:T(8,128)}, f32[256,512]{1,0:T(8,128)}, f32[256,512]{1,0:T(8,128)}) custom-call(bf16[2,2,4,4,432,128]{5,4,3,2,1,0:T(8,128)(2,1)S(1)} %copy-done.2, bf16[2,4,4,128,128]{4,3,2,1,0:T(8,128)(2,1)S(1)} %get-tuple-element.82.qkv), custom_call_target="tpu_custom_call" | custom-call | tf_op jit(solution)/shard_map/pallas_call | solution.py:1066
  319.3 4.1 %shard_map.259 = (f32[1152,1024]{1,0:T(8,128)}, f32[256,1024]{1,0:T(8,128)}) custom-call(bf16[2,2,4,4,432,128]{5,4,3,2,1,0:T(8,128)(2,1)S(1)} %copy-done.2, bf16[2,4,4,64,128]{4,3,2,1,0:T(8,128)(2,1)S(1)} %get-tuple-element.86.pieces), custom_call_target="tpu_custom_call" | custom-call | tf_op jit(solution)/shard_map/pallas_call | solution.py:1082
  325.9 1.2 fusion.19
  (191 shorter events, 12.7 us)
Async XLA Ops:
  7.2 56.3 %copy-start = (bf16[1152,1024]{1,0:T(8,128)(2,1)S(1)}, bf16[1152,1024]{1,0:T(8,128)(2,1)}, u32[]{:S(2)}) copy-start(bf16[1152,1024]{1,0:T(8,128)(2,1)} %param.28) | copy-start | bytes 7077892
  7.2 142.0 %all-gather.2.cloned.1.call-start = ((), (), s32[]{:S(2)}) async-start(), calls=%async_computation | async-start | bytes 1310720 | tf_op jit(solution)/shard_map/all_gather | solution.py:1193
  26.9 7.3 %copy-start.33 = (bf16[2,4,64,1024]{3,2,1,0:T(8,128)(2,1)S(1)}, bf16[2,4,64,1024]{3,2,1,0:T(8,128)(2,1)}, u32[]{:S(2)}) copy-start(bf16[2,4,64,1024]{3,2,1,0:T(8,128)(2,1)} %get-tuple-element.53) | copy-start | bytes 3145732
  28.6 34.9 %collective-permute-start = (bf16[64,1024]{1,0:T(8,128)(2,1)}, bf16[64,1024]{1,0:T(8,128)(2,1)}, u32[]{:S(2)}, u32[]{:S(2)}) collective-permute-start(bf16[64,1024]{1,0:T(8,128)(2,1)} %constant_dynamic-slice_fusion.1), channel_id=1, source_target_pairs={{0,0},{2,32},{4,64},{6,96},{32,2},{34,34},{36,66},{38,98},{64,4},{... | collective-permute-start | bytes 393224 | tf_op jit(solution)/shard_map/ppermute | solution.py:1176
  34.2 2.4 copy-start.49
  34.3 2.4 copy-start.55
  34.6 2.3 copy-start.69
  34.6 6.3 %copy-start.70 = (s32[1,128]{1,0:T(1,128)S(1)}, s32[1,128]{1,0:T(1,128)}, u32[]{:S(2)}) copy-start(s32[1,128]{1,0:T(1,128)} %param.16) | copy-start | bytes 1540
  36.6 15.9 %copy-start.31 = (f32[512,512]{1,0:T(8,128)}, f32[512,512]{1,0:T(8,128)S(1)}, u32[]{:S(2)}) copy-start(f32[512,512]{1,0:T(8,128)S(1)} %fusion.42) | copy-start | bytes 3145732
  36.8 4.2 %copy-start.53 = (f32[2,512]{1,0:T(2,128)}, f32[2,512]{1,0:T(2,128)S(1)}, u32[]{:S(2)}) copy-start(f32[2,512]{1,0:T(2,128)S(1)} %multiply_reduce_fusion.8) | copy-start | bytes 12292
  36.9 4.1 %copy-start.59 = (f32[64]{0:T(128)}, f32[64]{0:T(128)S(1)}, u32[]{:S(2)}) copy-start(f32[64]{0:T(128)S(1)} %mul.536) | copy-start | bytes 772
  39.3 13.2 %copy-start.51 = (f32[2,512]{1,0:T(2,128)}, f32[2,512]{1,0:T(2,128)S(1)}, u32[]{:S(2)}) copy-start(f32[2,512]{1,0:T(2,128)S(1)} %fusion.34) | copy-start | bytes 12292
  41.9 12.7 %copy-start.39 = (f32[32,512]{1,0:T(8,128)}, f32[32,512]{1,0:T(8,128)S(1)}, u32[]{:S(2)}) copy-start(f32[32,512]{1,0:T(8,128)S(1)} %get-tuple-element.125) | copy-start | bytes 196612
  50.0 4.7 %copy-start.44 = (bf16[2,32,512]{2,1,0:T(8,128)(2,1)S(1)}, bf16[2,32,512]{2,1,0:T(8,128)(2,1)}, u32[]{:S(2)}) copy-start(bf16[2,32,512]{2,1,0:T(8,128)(2,1)} %get-tuple-element.112) | copy-start | bytes 196612
  50.0 4.7 %copy-start.45 = (bf16[2,32,512]{2,1,0:T(8,128)(2,1)S(1)}, bf16[2,32,512]{2,1,0:T(8,128)(2,1)}, u32[]{:S(2)}) copy-start(bf16[2,32,512]{2,1,0:T(8,128)(2,1)} %get-tuple-element.113) | copy-start | bytes 196612
  52.5 4.5 %copy-start.56 = (f32[2,4,64]{2,1,0:T(4,128)S(1)}, f32[2,4,64]{2,1,0:T(4,128)}, u32[]{:S(2)}) copy-start(f32[2,4,64]{2,1,0:T(4,128)} %copy-done.55) | copy-start | bytes 6148
  52.5 5.2 %copy-start.58 = (f32[1,2,4,128]{3,2,1,0:T(4,128)S(1)}, f32[1,2,4,128]{3,2,1,0:T(4,128)}, u32[]{:S(2)}) copy-start(f32[1,2,4,128]{3,2,1,0:T(4,128)} %get-tuple-element.116) | copy-start | bytes 12292
  53.5 34.5 %copy-start.7 = (bf16[4,64,512]{2,1,0:T(8,128)(2,1)}, bf16[4,64,512]{2,1,0:T(8,128)(2,1)S(1)}, u32[]{:S(2)}) copy-start(bf16[4,64,512]{2,1,0:T(8,128)(2,1)S(1)} %pad_maximum_fusion.1) | copy-start | bytes 786436
  57.7 1.7 copy-start.9
  59.4 1.7 copy-start.10
  88.0 1.6 copy-start.3
  89.6 1.6 copy-start.4
  92.3 19.3 %copy-start.37 = (bf16[4,2,32,1024]{3,2,1,0:T(8,128)(2,1)S(1)}, bf16[4,2,32,1024]{3,2,1,0:T(8,128)(2,1)}, u32[]{:S(2)}) copy-start(bf16[4,2,32,1024]{3,2,1,0:T(8,128)(2,1)} %get-tuple-element.60) | copy-start | bytes 1572868
  111.5 16.9 %copy-start.24 = (bf16[4,2,128,1152]{3,2,1,0:T(8,128)(2,1)}, bf16[4,2,128,1152]{3,2,1,0:T(8,128)(2,1)S(1)}, u32[]{:S(2)}) copy-start(bf16[4,2,128,1152]{3,2,1,0:T(8,128)(2,1)S(1)} %get-tuple-element.66) | copy-start | bytes 7077892
  111.5 18.3 %copy-start.28 = (bf16[1,128,1024]{2,1,0:T(8,128)(2,1)S(1)}, bf16[1,128,1024]{2,1,0:T(8,128)(2,1)}, u32[]{:S(2)}) copy-start(bf16[1,128,1024]{2,1,0:T(8,128)(2,1)} %param.15) | copy-start | bytes 786436
  149.2 3.7 %copy-start.43 = (bf16[2,4,64,1024]{3,2,1,0:T(8,128)(2,1)S(1)}, bf16[2,4,64,1024]{3,2,1,0:T(8,128)(2,1)}, u32[]{:S(2)}) copy-start(bf16[2,4,64,1024]{3,2,1,0:T(8,128)(2,1)} %shard_map.251) | copy-start | bytes 3145732
  149.2 3.7 %copy-start.66 = (bf16[4,2,128,1152]{3,2,1,0:T(8,128)(2,1)S(1)}, bf16[4,2,128,1152]{3,2,1,0:T(8,128)(2,1)}, u32[]{:S(2)}) copy-start(bf16[4,2,128,1152]{3,2,1,0:T(8,128)(2,1)} %get-tuple-element.67) | copy-start | bytes 7077892
  149.2 3.7 %copy-start.71 = (f32[512,1152]{1,0:T(8,128)S(1)}, f32[512,1152]{1,0:T(8,128)}, u32[]{:S(2)}) copy-start(f32[512,1152]{1,0:T(8,128)} %fusion.44) | copy-start | bytes 7077892
  152.9 2.4 copy-start.25
  156.9 1.6 copy-start.68
  158.5 1.7 copy-start.27
  165.1 12.5 %copy-start.35 = (bf16[1,128,1024]{2,1,0:T(8,128)(2,1)S(1)}, bf16[1,128,1024]{2,1,0:T(8,128)(2,1)}, u32[]{:S(2)}) copy-start(bf16[1,128,1024]{2,1,0:T(8,128)(2,1)} %param.29) | copy-start | bytes 786436
  177.6 13.8 %copy-start.62 = (f32[2,64]{1,0:T(2,128)}, f32[2,64]{1,0:T(2,128)S(1)}, u32[]{:S(2)}) copy-start(f32[2,64]{1,0:T(2,128)S(1)} %get-tuple-element.92) | copy-start | bytes 1540
  177.8 13.6 %copy-start.38 = (bf16[4,2,32,1024]{3,2,1,0:T(8,128)(2,1)S(1)}, bf16[4,2,32,1024]{3,2,1,0:T(8,128)(2,1)}, u32[]{:S(2)}) copy-start(bf16[4,2,32,1024]{3,2,1,0:T(8,128)(2,1)} %get-tuple-element.60) | copy-start | bytes 1572868
  177.8 14.1 %copy-start.8 = (bf16[4,64,512]{2,1,0:T(8,128)(2,1)S(1)}, bf16[4,64,512]{2,1,0:T(8,128)(2,1)}, u32[]{:S(2)}) copy-start(bf16[4,64,512]{2,1,0:T(8,128)(2,1)} %copy-done.7) | copy-start | bytes 786436
  191.9 52.5 %copy-start.40 = (f32[32,512]{1,0:T(8,128)S(1)}, f32[32,512]{1,0:T(8,128)}, u32[]{:S(2)}) copy-start(f32[32,512]{1,0:T(8,128)} %copy-done.39) | copy-start | bytes 196612
  219.6 23.4 %copy-start.16 = (f32[256,512]{1,0:T(8,128)}, f32[256,512]{1,0:T(8,128)S(1)}, u32[]{:S(2)}) copy-start(f32[256,512]{1,0:T(8,128)S(1)} %get-tuple-element.74) | copy-start | bytes 1572868
  219.6 1.8 copy-start.11
  243.7 1.4 copy-start.18
  243.7 3.2 copy-start.52
  243.7 4.9 %copy-start.17 = (f32[256,512]{1,0:T(8,128)S(1)}, f32[256,512]{1,0:T(8,128)}, u32[]{:S(2)}) copy-start(f32[256,512]{1,0:T(8,128)} %copy-done.16) | copy-start | bytes 1572868
  246.4 2.0 copy-start.54
  246.4 2.0 copy-start.32
  246.4 2.0 copy-start.41
  246.4 2.0 copy-start.42
  246.4 2.0 copy-start.61
  246.4 2.3 slice-start
  246.4 2.3 copy-start.60
  246.9 2.0 copy-start.48
  249.9 19.3 %copy-start.29 = (bf16[1,128,1024]{2,1,0:T(8,128)(2,1)S(1)}, bf16[1,128,1024]{2,1,0:T(8,128)(2,1)}, u32[]{:S(2)}) copy-start(bf16[1,128,1024]{2,1,0:T(8,128)(2,1)} %param.15) | copy-start | bytes 786436
  249.9 19.3 %copy-start.50 = (f32[1,2,4,128]{3,1,2,0:T(2,128)S(1)}, f32[1,2,4,128]{3,1,2,0:T(2,128)}, u32[]{:S(2)}) copy-start(f32[1,2,4,128]{3,1,2,0:T(2,128)} %copy-done.49) | copy-start | bytes 12292
  249.9 19.5 %copy-start.34 = (bf16[2,4,64,1024]{3,2,1,0:T(8,128)(2,1)S(1)}, bf16[2,4,64,1024]{3,2,1,0:T(8,128)(2,1)}, u32[]{:S(2)}) copy-start(bf16[2,4,64,1024]{3,2,1,0:T(8,128)(2,1)} %get-tuple-element.53) | copy-start | bytes 3145732
  249.9 19.5 %copy-start.63 = (f32[512]{0:T(512)S(1)}, f32[512]{0:T(512)}, u32[]{:S(2)}) copy-start(f32[512]{0:T(512)} %rsqrt.66) | copy-start | bytes 6148
  269.2 2.2 copy-start.20
  269.2 2.3 copy-start.5
  269.4 1.9 copy-start.64
  269.4 1.9 copy-start.65
  269.4 2.2 copy-start.57
  310.5 3.0 copy-start.2
  319.2 6.7 %copy-start.6 = (f32[2,64,1024]{2,1,0:T(8,128)S(1)}, f32[2,64,1024]{2,1,0:T(8,128)}, u32[]{:S(2)}) copy-start(f32[2,64,1024]{2,1,0:T(8,128)} %copy-done.5) | copy-start | bytes 1572868
  319.2 6.7 %copy-start.19 = (f32[2,64,1024]{2,1,0:T(8,128)S(1)}, f32[2,64,1024]{2,1,0:T(8,128)}, u32[]{:S(2)}) copy-start(f32[2,64,1024]{2,1,0:T(8,128)} %copy-done.18) | copy-start | bytes 1572868
  319.2 6.7 %copy-start.30 = (bf16[1,128,1024]{2,1,0:T(8,128)(2,1)S(1)}, bf16[1,128,1024]{2,1,0:T(8,128)(2,1)}, u32[]{:S(2)}) copy-start(bf16[1,128,1024]{2,1,0:T(8,128)(2,1)} %param.15) | copy-start | bytes 786436
  319.2 6.6 %copy-start.36 = (bf16[1,128,1024]{2,1,0:T(8,128)(2,1)S(1)}, bf16[1,128,1024]{2,1,0:T(8,128)(2,1)}, u32[]{:S(2)}) copy-start(bf16[1,128,1024]{2,1,0:T(8,128)(2,1)} %param.29) | copy-start | bytes 786436
  319.3 7.8 %copy-start.1 = (bf16[1152,1024]{1,0:T(8,128)(2,1)S(1)}, bf16[1152,1024]{1,0:T(8,128)(2,1)}, u32[]{:S(2)}) copy-start(bf16[1152,1024]{1,0:T(8,128)(2,1)} %param.28) | copy-start | bytes 7077892
  (11 other events, 11.4 us)
Sparse Core Ops, SparseCore 0:
  30.9 23.7 all-gather.1
